TPU v7x, 128 devices: a whole 4x4x4 slice. The times are simulated.
128 devices in a mesh: frames: 4 (over x), tiles: 32 (over y, z, core).
Axes of the slice: x: 4, y: 4, z: 4, core: 2. Of those that a mesh axis runs over, the one named last changes fastest.
Arguments:
- features: bfloat16 [16, 256, 480, 128], P('frames', 'tiles'), may hold values from -6 to 6
- w_conv: bfloat16 [3, 3, 128, 128], replicated, may hold values from -0.1875 to 0.1875
- query_feats: bfloat16 [16384, 128], P(('frames', 'tiles')), may hold values from -6 to 6
- offset_rows: int32 [16, 128], P('frames'), may hold values from 0 to 7
- offset_cols: int32 [16, 128], P('frames'), may hold values from 0 to 471
- owners: int32 [128, 1], replicated, may hold values from 0 to 31; in each aligned block of 128 rows (0 to 127, 128 to 255, ...) at most 12 rows name the same one
- start_frames: int32 [16384], P(('frames', 'tiles')), may hold values from 0 to 15
- w_corr: bfloat16 [81, 384], replicated, may hold values from -0.625 to 0.625
- w_feat: bfloat16 [128, 384], replicated, may hold values from -0.5 to 0.5
- time_embed: float32 [16, 384], replicated, may hold values from -3 to 3
- gain_attn: float32 [384], replicated, may hold values from 0.5 to 1.5
- w_qkv: bfloat16 [384, 1152], replicated, may hold values from -1.0716518 to 1.0716518
- w_attn_out: bfloat16 [384, 384], replicated, may hold values from -0.3125 to 0.3125
- gain_mlp: float32 [384], replicated, may hold values from 0.5 to 1.5
- w_up: bfloat16 [384, 1536], replicated, may hold values from -0.3125 to 0.3125
- w_down: bfloat16 [1536, 384], replicated, may hold values from -0.15625 to 0.15625
Outputs:
- refined: bfloat16 [16384, 16, 384], P(('frames', 'tiles'))
Inputs may be any that keep to these rules, and one draw needn't show every extreme that they name: `owners`: no tile owns more than 12 query blocks; some tile owns exactly 12; every tile owns at least one.
All inputs are finite; a program needn't handle non-finite values.
Results may differ from a plain program's by a relative error of at most 0.0066.
Values may be sent and summed in bfloat16 or wider, within the bound.
No kernel may reach another device: no remote copies, remote signals or barrier semaphores. Data moves between devices by JAX's collectives and lax.ppermute only.
A program may use at most 192 MiB of HBM per device.

v0:
```python
import functools

import jax
import jax.numpy as jnp
from jax import lax
from jax.experimental import pallas as pl
from jax.experimental.pallas import tpu as pltpu
from jax.sharding import PartitionSpec as P

HEADS = 8
HEAD = 48
WIN = 9
RAW = WIN + 2
CELLS = RAW * RAW
QBLK = 128
CAP = 12
TILE = 8
EDGE = 5
MSG = 56
PIECES = 32
PROWS = 16
SLOT = PIECES * PROWS
CHUNK = 512
F32 = jnp.float32
BF16 = jnp.bfloat16


def window_rows(feat_ref, tmp_ref, dst_ref, base, frame, row0, rows, col):
    wide = feat_ref.shape[2]
    start = pl.multiple_of(jnp.clip((col >> 4) << 4, 0, wide - 32), 16)
    tmp_ref[0:rows, 8:40, :] = feat_ref[frame, row0 : row0 + rows, pl.ds(start, 32), :].astype(F32)
    for i in range(rows):
        dst_ref[base + RAW * i : base + RAW * i + 16, :] = tmp_ref[i, pl.ds(8 + col - start, 16), :]


def edge_kernel(ids_ref, count_ref, cols_ref, feat_ref, up_ref, down_ref, tmp_ref, win_ref):
    frames = feat_ref.shape[0]
    rows = feat_ref.shape[1]
    tmp_ref[...] = jnp.zeros_like(tmp_ref)

    def part(which, row0, out_ref):
        def slot(s, carry):
            block = ids_ref[which, s]
            for k in range(frames):
                window_rows(
                    feat_ref, tmp_ref, win_ref, k * MSG, k, row0, EDGE, cols_ref[k, block] - 1
                )
            out_ref[pl.ds(pl.multiple_of(s * frames * MSG, 16), frames * MSG), :] = win_ref[
                0 : frames * MSG, :
            ].astype(BF16)
            return carry

        lax.fori_loop(0, count_ref[which], slot, 0)

    win_ref[...] = jnp.zeros_like(win_ref)
    part(2, rows - EDGE, up_ref)
    part(0, 0, down_ref)


def merge_kernel(
    ids_ref, count_ref, info_ref, cols_ref, offs_ref, feat_ref, low_ref, high_ref, out_ref,
    tmp_ref, side_ref, win_ref, all_ref,
):
    frames, rows = feat_ref.shape[0], feat_ref.shape[1]
    tmp_ref[...] = jnp.zeros_like(tmp_ref)
    win_ref[...] = jnp.zeros_like(win_ref)

    def slot(s, carry):
        block = ids_ref[1, s]
        here = pl.ds(pl.multiple_of(s * frames * MSG, 16), frames * MSG)
        side_ref[0] = low_ref[here, :].astype(F32)
        side_ref[1] = high_ref[here, :].astype(F32)
        own = EDGE * RAW
        for k in range(frames):
            row = offs_ref[k, block]
            win_ref[0:MSG, :] = side_ref[0, k * MSG : (k + 1) * MSG, :]
            window_rows(feat_ref, tmp_ref, win_ref, own, k, 0, rows, cols_ref[k, block] - 1)
            top = own + rows * RAW
            win_ref[top : top + MSG, :] = side_ref[1, k * MSG : (k + 1) * MSG, :]
            all_ref[k * CELLS : k * CELLS + 128, :] = win_ref[pl.ds(row * RAW, 128), :]
        end = frames * CELLS
        all_ref[end:SLOT, :] = jnp.zeros((SLOT - end, 128), F32)
        for k in range(frames):
            first = (info_ref[0] * rows + offs_ref[k, block] - WIN // 2).astype(F32)
            all_ref[end + k : end + k + 1, :] = jnp.full((1, 128), first, F32)
        for i in range(PIECES):
            out_ref[i, pl.ds(pl.multiple_of(s * PROWS, 16), PROWS), :] = all_ref[
                i * PROWS : (i + 1) * PROWS, :
            ].astype(BF16)
        return carry

    lax.fori_loop(0, count_ref[1], slot, 0)


def route_kernel(owner_ref, rank_ref, in_ref, out_ref):
    def step(b, carry):
        out_ref[b] = in_ref[owner_ref[b], pl.ds(pl.multiple_of(rank_ref[b] * PROWS, 16), PROWS), :]
        return carry

    lax.fori_loop(0, out_ref.shape[0], step, 0, unroll=8)


def nt(a, b):
    return lax.dot_general(a, b, (((1,), (1,)), ((), ())), preferred_element_type=F32)


def rms_scale(values, gain):
    return values * lax.rsqrt(jnp.mean(values * values, axis=-1, keepdims=True) + 1e-06) * gain


def refine_kernel(
    height, raw_ref, wconv_ref, query_ref, wcorr_ref, wfeat_ref, time_ref, start_ref, gain1_ref,
    wk_ref, wq_ref, wv_ref, wout_ref, gain2_ref, wup_ref, wdown_ref, out_ref,
    cells_ref, cols_ref, tok_ref,
):
    groups, per = raw_ref.shape[0] // SLOT, 4
    frames = groups * per
    step = pl.program_id(0)

    @pl.when(step == 0)
    def _():
        cells_ref[0 : groups * SLOT, :] = raw_ref[...].astype(F32)
        cells_ref[groups * SLOT :, :] = jnp.zeros_like(cells_ref[groups * SLOT :, :])
        line = lax.broadcasted_iota(jnp.int32, (128, 128), 0) // RAW
        line = line.astype(F32)
        for f in range(frames):
            base = (f // per) * SLOT + (f % per) * CELLS
            for a in range(3):
                for b in range(3):
                    at = base + a * RAW + b
                    cols_ref[f * 128 : (f + 1) * 128, (a * 3 + b) * 128 : (a * 3 + b + 1) * 128] = (
                        cells_ref[at : at + 128, :].astype(BF16)
                    )
        feat = jnp.dot(query_ref[...], wfeat_ref[...], preferred_element_type=F32)
        for f in range(frames):
            conv = jnp.dot(
                cols_ref[f * 128 : (f + 1) * 128, :], wconv_ref[...], preferred_element_type=F32
            )
            info = (f // per) * SLOT + per * CELLS + f % per
            row = line + cells_ref[info : info + 1, :]
            conv = jnp.where((row >= 0) & (row < height), conv, 0.0).astype(BF16)
            corr = (nt(query_ref[...], conv) * (128 ** -0.5)).astype(BF16)
            tokens = jnp.dot(corr, wcorr_ref[...], preferred_element_type=F32)
            tokens = tokens + feat + time_ref[f : f + 1, :]
            for part in range(3):
                tok_ref[part, pl.ds(f, 128, stride=frames), :] = tokens[
                    :, part * 128 : (part + 1) * 128
                ]

    here = pl.ds(pl.multiple_of(step * CHUNK, CHUNK), CHUNK)
    tokens = jnp.concatenate([tok_ref[part, here, :] for part in range(3)], axis=1)
    normed = rms_scale(tokens, gain1_ref[...]).astype(BF16)
    keys = jnp.dot(normed, wk_ref[...], preferred_element_type=F32).astype(BF16)
    query = nt(wq_ref[...], normed).astype(BF16)
    values = nt(wv_ref[...], normed).astype(BF16)
    track = lax.broadcasted_iota(jnp.int32, (16, 128), 1) // frames
    frame = lax.broadcasted_iota(jnp.int32, (16, 128), 0)
    key_track = lax.broadcasted_iota(jnp.int32, (128, 128), 0) // frames
    query_track = lax.broadcasted_iota(jnp.int32, (128, 128), 1) // frames
    same = (key_track == query_track).astype(BF16)
    factor = HEAD ** -0.5 * 1.4426950408889634
    zeros16 = jnp.zeros((16, 128), BF16)
    zeros64 = jnp.zeros((64, 128), BF16)
    attended = []
    for g in range(CHUNK // 128):
        lanes = slice(g * 128, (g + 1) * 128)
        valid = frame >= start_ref[0, :, lanes]
        heads = []
        for pair in range(HEADS // 2):
            one = query[2 * pair * HEAD : (2 * pair + 1) * HEAD, lanes]
            two = query[(2 * pair + 1) * HEAD : (2 * pair + 2) * HEAD, lanes]
            both = jnp.concatenate(
                [
                    jnp.concatenate([one, zeros16, zeros64], axis=0),
                    jnp.concatenate([zeros64, two, zeros16], axis=0),
                ],
                axis=1,
            )
            scores = jnp.dot(
                keys[lanes, pair * 128 : (pair + 1) * 128], both, preferred_element_type=F32
            )
            for h in range(2):
                full = scores[:, h * 128 : (h + 1) * 128]
                own = full[0:16, :]
                for t in range(1, 8):
                    own = jnp.where(track == t, full[16 * t : 16 * (t + 1), :], own)
                own = jnp.where(valid, own, -1e30)
                top = jnp.max(own, axis=0, keepdims=True)
                weights = jnp.exp2((own - top) * factor)
                probs = (weights / jnp.sum(weights, axis=0, keepdims=True)).astype(BF16)
                spread = jnp.concatenate([probs] * 8, axis=0) * same
                at = (2 * pair + h) * HEAD
                heads.append(
                    jnp.dot(values[at : at + HEAD, lanes], spread, preferred_element_type=F32)
                )
        attended.append(jnp.concatenate(heads, axis=0).T.astype(BF16))
    attended = jnp.concatenate(attended, axis=0)
    mixed = tokens + jnp.dot(attended, wout_ref[...], preferred_element_type=F32)
    normed2 = rms_scale(mixed, gain2_ref[...]).astype(BF16)
    hidden = jax.nn.gelu(
        jnp.dot(normed2, wup_ref[...], preferred_element_type=F32), approximate=True
    ).astype(BF16)
    result = mixed + jnp.dot(hidden, wdown_ref[...], preferred_element_type=F32)
    out_ref[...] = result.astype(BF16)


def params(mib):
    return pltpu.CompilerParams(vmem_limit_bytes=mib << 20)


SMEM = pl.BlockSpec(memory_space=pltpu.SMEM)
VMEM = pl.BlockSpec(memory_space=pltpu.VMEM)


def body(
    features, w_conv, query_feats, offset_rows, offset_cols, owners, start_frames, w_corr, w_feat,
    time_embed, gain_attn, w_qkv, w_attn_out, gain_mlp, w_up, w_down,
):
    n_tiles = lax.axis_size("tiles")
    tile = lax.axis_index("tiles")
    frames, rows, width, chans = features.shape
    blocks = owners.shape[0]
    tracks = query_feats.shape[0]
    total = time_embed.shape[0]
    dim = w_feat.shape[1]

    owner = owners[:, 0]
    number = jnp.arange(blocks, dtype=jnp.int32)
    rank = jnp.sum(
        (owner[:, None] == owner[None, :]) & (number[None, :] < number[:, None]), axis=1, dtype=jnp.int32
    )
    near = tile + jnp.arange(-1, 2, dtype=jnp.int32)
    mine = owner[None, :] == near[:, None]
    count = jnp.sum(mine, axis=1, dtype=jnp.int32)
    slots = jnp.arange(CAP, dtype=jnp.int32)
    ids = jnp.sum(
        jnp.where(mine[:, None, :] & (rank[None, None, :] == slots[None, :, None]), number, 0),
        axis=2,
        dtype=jnp.int32,
    )

    message = jax.ShapeDtypeStruct((CAP * frames * MSG, chans), BF16)
    up, down = pl.pallas_call(
        edge_kernel,
        out_shape=(message, message),
        in_specs=[SMEM, SMEM, SMEM, VMEM],
        out_specs=(VMEM, VMEM),
        scratch_shapes=[pltpu.VMEM((TILE, 48, 128), F32), pltpu.VMEM((frames * MSG + 16, 128), F32)],
        compiler_params=params(24),
        name="edges",
    )(ids, count, offset_cols, features)
    low = lax.ppermute(up, "tiles", [(i, i + 1) for i in range(n_tiles - 1)])
    high = lax.ppermute(down, "tiles", [(i + 1, i) for i in range(n_tiles - 1)])
    pieces = pl.pallas_call(
        merge_kernel,
        out_shape=jax.ShapeDtypeStruct((PIECES, CAP * PROWS, chans), BF16),
        in_specs=[SMEM, SMEM, SMEM, SMEM, SMEM, VMEM, VMEM, VMEM],
        out_specs=VMEM,
        scratch_shapes=[
            pltpu.VMEM((TILE, 48, 128), F32),
            pltpu.VMEM((2, frames * MSG, 128), F32),
            pltpu.VMEM((208, 128), F32),
            pltpu.VMEM((SLOT, 128), F32),
        ],
        compiler_params=params(24),
        name="windows",
    )(ids, count, tile.reshape(1), offset_cols, offset_rows, features, low, high)
    spread = lax.all_to_all(pieces, "tiles", 0, 0, tiled=True)
    routed = pl.pallas_call(
        route_kernel,
        out_shape=jax.ShapeDtypeStruct((blocks, PROWS, chans), BF16),
        in_specs=[SMEM, SMEM, VMEM],
        out_specs=VMEM,
        compiler_params=params(24),
        name="route",
    )(owner, rank, spread)
    raw = lax.all_to_all(routed, ("frames", "tiles"), 0, 0, tiled=True)
    raw = raw.reshape(blocks * PROWS, chans)

    wk = jnp.pad(w_qkv[:, dim : 2 * dim].reshape(dim, HEADS, HEAD), ((0, 0), (0, 0), (0, 16)))
    wk = wk.reshape(dim, HEADS * 64)
    wq, wv = w_qkv[:, :dim].T, w_qkv[:, 2 * dim :].T
    wcorr = jnp.pad(w_corr.reshape(WIN, WIN, dim), ((0, 0), (0, RAW - WIN), (0, 0)))
    wcorr = jnp.pad(wcorr.reshape(WIN * RAW, dim), ((0, 128 - WIN * RAW), (0, 0)))
    tokens = tracks * total
    start = jnp.repeat(start_frames, total).reshape(tokens // CHUNK, 1, CHUNK)
    whole = lambda *shape: pl.BlockSpec(shape, lambda i: (0,) * len(shape))
    refined = pl.pallas_call(
        functools.partial(refine_kernel, n_tiles * rows),
        grid=(tokens // CHUNK,),
        out_shape=jax.ShapeDtypeStruct((tokens, dim), BF16),
        in_specs=[
            whole(blocks * PROWS, chans),
            whole(9 * chans, chans),
            whole(tracks, chans),
            whole(128, dim),
            whole(chans, dim),
            whole(total, dim),
            pl.BlockSpec((1, 1, CHUNK), lambda i: (i, 0, 0)),
            whole(1, dim),
            whole(dim, HEADS * 64),
            whole(dim, dim),
            whole(dim, dim),
            whole(dim, dim),
            whole(1, dim),
            whole(*w_up.shape),
            whole(*w_down.shape),
        ],
        out_specs=pl.BlockSpec((CHUNK, dim), lambda i: (i, 0)),
        scratch_shapes=[
            pltpu.VMEM((blocks * PROWS + 16, 128), F32),
            pltpu.VMEM((total * 128, 9 * chans), BF16),
            pltpu.VMEM((3, tokens, 128), F32),
        ],
        compiler_params=params(56),
        name="refine",
    )(
        raw, w_conv.reshape(9 * chans, chans), query_feats, wcorr, w_feat, time_embed, start,
        gain_attn.reshape(1, dim), wk, wq, wv, w_attn_out, gain_mlp.reshape(1, dim), w_up, w_down,
    )
    return refined.reshape(tracks, total, dim)


def solution(mesh):
    placed = (
        P("frames", "tiles", None, None),
        P(),
        P(("frames", "tiles"), None),
        P("frames", None),
        P("frames", None),
        P(),
        P(("frames", "tiles")),
        P(), P(), P(), P(), P(), P(), P(), P(), P(),
    )
    return jax.shard_map(
        body,
        mesh=mesh,
        in_specs=placed,
        out_specs=P(("frames", "tiles"), None, None),
        check_vma=False,
    )
```

profile of v0, /device:TPU:1, one launch (start us, length us, event | category | flops | bytes accessed | tf_op | source)
XLA Modules:
  0.0 114.0 jit_solution(3844534500917333585)
XLA Ops:
  0.0 0.9 convert_reduce_fusion.rank_ref
  0.9 0.8 convert_reduce_fusion.1
  1.8 0.2 select_reduce_fusion.ids_ref
  1.9 0.0 copy-start
  1.9 2.1 %copy-done = bf16[4,8,480,128]{3,2,1,0:T(8,128)(2,1)S(1)} copy-done((bf16[4,8,480,128]{3,2,1,0:T(8,128)(2,1)S(1)}, bf16[4,8,480,128]{3,2,1,0:T(8,128)(2,1)}, u32[]{:S(2)}) %copy-start) | copy-done | bytes 3932184
  4.0 0.0 copy-start.1
  4.0 0.7 copy-done.1
  4.7 0.0 copy-start.2
  4.7 0.9 edges.1
  5.7 5.1 %collective-permute-start = (bf16[2688,128]{1,0:T(8,128)(2,1)S(1)}, bf16[2688,128]{1,0:T(8,128)(2,1)S(1)}, u32[]{:S(2)}, u32[]{:S(2)}) collective-permute-start(bf16[2688,128]{1,0:T(8,128)(2,1)S(1)} %get-tuple-element.7), channel_id=1, source_target_pairs={{0,1},{1,2},{2,3},{3,4},{4,5},{5,6},{6,7},{7,8},{8,9},{9,10},{10,1... | collective-permute-start | bytes 2064392 | tf_op jit(solution)/shard_map/ppermute | solution.py:252
  10.7 1.9 %collective-permute-start.1 = (bf16[2688,128]{1,0:T(8,128)(2,1)S(1)}, bf16[2688,128]{1,0:T(8,128)(2,1)S(1)}, u32[]{:S(2)}, u32[]{:S(2)}) collective-permute-start(bf16[2688,128]{1,0:T(8,128)(2,1)S(1)} %get-tuple-element.8), channel_id=1, source_target_pairs={{1,0},{2,1},{3,2},{4,3},{5,4},{6,5},{7,6},{8,7},{9,8},{10,9},{11,1... | collective-permute-start | bytes 2064392 | tf_op jit(solution)/shard_map/ppermute | solution.py:253
  12.7 5.9 %collective-permute-done.low_ref = bf16[2688,128]{1,0:T(8,128)(2,1)S(1)} collective-permute-done((bf16[2688,128]{1,0:T(8,128)(2,1)S(1)}, bf16[2688,128]{1,0:T(8,128)(2,1)S(1)}, u32[]{:S(2)}, u32[]{:S(2)}) %collective-permute-start) | collective-permute-done | bytes 688160 | tf_op jit(solution)/shard_map/ppermute | solution.py:252
  18.6 4.4 %collective-permute-done.1.high_ref = bf16[2688,128]{1,0:T(8,128)(2,1)S(1)} collective-permute-done((bf16[2688,128]{1,0:T(8,128)(2,1)S(1)}, bf16[2688,128]{1,0:T(8,128)(2,1)S(1)}, u32[]{:S(2)}, u32[]{:S(2)}) %collective-permute-start.1) | collective-permute-done | bytes 688160 | tf_op jit(solution)/shard_map/ppermute | solution.py:253
  23.0 0.0 copy-done.2
  23.0 0.9 windows.1
  23.9 0.0 copy-start.3
  23.9 31.2 %all_to_all.10.in_ref = bf16[32,192,128]{2,1,0:T(8,128)(2,1)S(1)} all-to-all(bf16[32,192,128]{2,1,0:T(8,128)(2,1)S(1)} %windows.1), channel_id=1, replica_groups=mesh['frames'=4,'tiles'=32] {'tiles'}, dimensions={0} | all-to-all | bytes 3145728 | tf_op jit(solution)/shard_map/all_to_all | solution.py:268
  55.1 0.0 copy-done.3
  55.1 0.0 copy-start.5
  55.1 1.7 %route.1 = bf16[128,16,128]{2,1,0:T(8,128)(2,1)} custom-call(s32[128]{0:T(128)S(1)} %bitcast.11, s32[128]{0:T(128)S(1)} %convert_reduce_fusion.rank_ref, bf16[32,192,128]{2,1,0:T(8,128)(2,1)S(1)} %all_to_all.10.in_ref), custom_call_target="tpu_custom_call" | custom-call | tf_op jit(solution)/shard_map/route/pallas_call | solution.py:269
  56.8 5.5 %all-to-all-start.1 = ((bf16[128,16,128]{2,1,0:T(8,128)(2,1)}), bf16[128,16,128]{2,1,0:T(8,128)(2,1)S(1)}, u32[]{:S(2)}, u32[]{:S(2)}) async-start(bf16[128,16,128]{2,1,0:T(8,128)(2,1)} %route.1), calls=%async_computation.1 | async-start | bytes 1048576 | tf_op jit(solution)/shard_map/all_to_all | solution.py:277
  62.3 0.0 copy-done.5
  62.4 0.1 fusion.1
  62.5 0.0 copy-start.6
  62.5 0.2 copy.29
  62.7 0.0 copy-start.9
  62.7 0.0 copy-start.7
  62.8 0.0 copy-start.8
  62.8 0.9 copy.28.wk_ref
  63.7 0.9 copy.30
  64.6 0.9 copy.31
  65.5 0.0 copy-done.6
  65.6 0.6 pad.13.wcorr_ref
  66.3 0.0 copy-done.9
  66.3 0.1 broadcast_in_dim.23
  66.4 0.1 broadcast_in_dim.24
  66.4 0.7 broadcast_in_dim.26.start_ref
  67.1 0.0 copy-done.7
  67.1 0.5 reshape.101.gain2_ref
  67.7 0.0 copy-done.8
  67.7 0.6 reshape.98.gain1_ref
  68.3 7.8 %all-to-all-done.1 = bf16[128,16,128]{2,1,0:T(8,128)(2,1)S(1)} async-done(((bf16[128,16,128]{2,1,0:T(8,128)(2,1)}), bf16[128,16,128]{2,1,0:T(8,128)(2,1)S(1)}, u32[]{:S(2)}, u32[]{:S(2)}) %all-to-all-start.1) | async-done | bytes 524320 | tf_op jit(solution)/shard_map/all_to_all | solution.py:277
  76.0 0.0 copy-start.4
  76.0 0.8 copy-done.4
  76.8 37.2 %refine.1 = bf16[2048,384]{1,0:T(8,128)(2,1)} custom-call(bf16[2048,128]{1,0:T(8,128)(2,1)} %bitcast.12, bf16[1152,128]{1,0:T(8,128)(2,1)} %bitcast.17, bf16[128,128]{1,0:T(8,128)(2,1)} %query_ref.1, bf16[128,384]{1,0:T(8,128)(2,1)} %pad.13.wcorr_ref, bf16[128,384]{1,0:T(8,128)(2,1)} %wfeat_ref.1, f32[16,384]{1,0:T(8,128)} %time_ref.1, ...), custom_call_target="tpu_custom_call" | custom-call | tf_op jit(solution)/shard_map/refine/pallas_call | solution.py:288
  (6 shorter events, 0.1 us)
Async XLA Ops:
  1.9 2.1 %copy-start = (bf16[4,8,480,128]{3,2,1,0:T(8,128)(2,1)S(1)}, bf16[4,8,480,128]{3,2,1,0:T(8,128)(2,1)}, u32[]{:S(2)}) copy-start(bf16[4,8,480,128]{3,2,1,0:T(8,128)(2,1)} %feat_ref.3) | copy-start | bytes 11796484
  4.0 0.7 copy-start.1
  4.7 18.3 %copy-start.2 = (s32[4,128]{1,0:T(4,128)S(1)}, s32[4,128]{1,0:T(4,128)}, u32[]{:S(2)}) copy-start(s32[4,128]{1,0:T(4,128)} %offs_ref.1) | copy-start | bytes 6148
  5.7 12.9 %collective-permute-start = (bf16[2688,128]{1,0:T(8,128)(2,1)S(1)}, bf16[2688,128]{1,0:T(8,128)(2,1)S(1)}, u32[]{:S(2)}, u32[]{:S(2)}) collective-permute-start(bf16[2688,128]{1,0:T(8,128)(2,1)S(1)} %get-tuple-element.7), channel_id=1, source_target_pairs={{0,1},{1,2},{2,3},{3,4},{4,5},{5,6},{6,7},{7,8},{8,9},{9,10},{10,1... | collective-permute-start | bytes 2064392 | tf_op jit(solution)/shard_map/ppermute | solution.py:252
  10.7 12.3 %collective-permute-start.1 = (bf16[2688,128]{1,0:T(8,128)(2,1)S(1)}, bf16[2688,128]{1,0:T(8,128)(2,1)S(1)}, u32[]{:S(2)}, u32[]{:S(2)}) collective-permute-start(bf16[2688,128]{1,0:T(8,128)(2,1)S(1)} %get-tuple-element.8), channel_id=1, source_target_pairs={{1,0},{2,1},{3,2},{4,3},{5,4},{6,5},{7,6},{8,7},{9,8},{10,9},{11,1... | collective-permute-start | bytes 2064392 | tf_op jit(solution)/shard_map/ppermute | solution.py:253
  23.9 31.2 %copy-start.3 = (s32[128,1]{0,1:T(1,128)S(1)}, s32[128,1]{0,1:T(1,128)}, u32[]{:S(2)}) copy-start(s32[128,1]{0,1:T(1,128)} %param.21) | copy-start | bytes 1540
  55.1 7.3 %copy-start.5 = (bf16[384,1152]{1,0:T(8,128)(2,1)S(1)}, bf16[384,1152]{1,0:T(8,128)(2,1)}, u32[]{:S(2)}) copy-start(bf16[384,1152]{1,0:T(8,128)(2,1)} %param.27) | copy-start | bytes 2654212
  56.8 19.2 %all-to-all-start.1 = ((bf16[128,16,128]{2,1,0:T(8,128)(2,1)}), bf16[128,16,128]{2,1,0:T(8,128)(2,1)S(1)}, u32[]{:S(2)}, u32[]{:S(2)}) async-start(bf16[128,16,128]{2,1,0:T(8,128)(2,1)} %route.1), calls=%async_computation.1 | async-start | bytes 1048576 | tf_op jit(solution)/shard_map/all_to_all | solution.py:277
  62.5 3.1 %copy-start.6 = (bf16[81,384]{1,0:T(8,128)(2,1)S(1)}, bf16[81,384]{1,0:T(8,128)(2,1)}, u32[]{:S(2)}) copy-start(bf16[81,384]{1,0:T(8,128)(2,1)} %param.23) | copy-start | bytes 186628
  62.7 3.6 %copy-start.9 = (s32[128]{0:T(128)S(1)}, s32[128]{0:T(128)}, u32[]{:S(2)}) copy-start(s32[128]{0:T(128)} %param.22) | copy-start | bytes 1540
  62.7 4.4 %copy-start.7 = (f32[384]{0:T(512)S(1)}, f32[384]{0:T(512)}, u32[]{:S(2)}) copy-start(f32[384]{0:T(512)} %param.29) | copy-start | bytes 4612
  62.8 4.9 %copy-start.8 = (f32[384]{0:T(512)S(1)}, f32[384]{0:T(512)}, u32[]{:S(2)}) copy-start(f32[384]{0:T(512)} %param.26) | copy-start | bytes 4612
  76.0 0.8 copy-start.4
where the time goes:
time: 114 us
  Pallas kernels  40.7 us (36%)
  blocking collectives  31.2 us (27%)
  waiting for transfers between devices  18.1 us (16%)
  starting transfers between devices  12.5 us (11%)
  local copies, waits for them, and re-layouts  9.45 us (8%)
  other arithmetic  1.91 us (2%)
    pallas_call x1, Pallas kernels, body(): pl.pallas_call(functools.partial(refine_kernel, n_tiles * rows), grid=(to...  37.2 us
    all_to_all x1, blocking collectives, body(): spread = lax.all_to_all(pieces, 'tiles', 0, 0, tiled=True)  31.2 us
    all_to_all x1, waiting for transfers between devices, body(): raw = lax.all_to_all(routed, ('frames', 'tiles'), 0, 0, tiled=True)  7.76 us
    ppermute x1, waiting for transfers between devices, body(): low = lax.ppermute(up, 'tiles', [(i, i + 1) for i in range(n_tiles - 1)])  5.93 us
    unnamed x23, local copies, waits for them, and re-layouts  5.66 us
    all_to_all x1, starting transfers between devices, body(): raw = lax.all_to_all(routed, ('frames', 'tiles'), 0, 0, tiled=True)  5.52 us
    ppermute x1, starting transfers between devices, body(): low = lax.ppermute(up, 'tiles', [(i, i + 1) for i in range(n_tiles - 1)])  5.06 us
    ppermute x1, waiting for transfers between devices, body(): high = lax.ppermute(down, 'tiles', [(i + 1, i) for i in range(n_tiles - 1)])  4.4 us
  transfers between devices with their start and end apart: 3, of which 3 were waited for; matrix products, arithmetic and copies ran while one was open for 5% of the time, Pallas kernels for 0%

commit v1 on v0

--- a/solution.py
+++ b/solution.py
@@ -20,7 +20,8 @@
 PIECES = 32
 PROWS = 16
 SLOT = PIECES * PROWS
-CHUNK = 512
+CHUNK = 1024
+BATCH = 4
 F32 = jnp.float32
 BF16 = jnp.bfloat16
 
@@ -123,6 +124,7 @@
         cells_ref[groups * SLOT :, :] = jnp.zeros_like(cells_ref[groups * SLOT :, :])
         line = lax.broadcasted_iota(jnp.int32, (128, 128), 0) // RAW
         line = line.astype(F32)
+        feat = jnp.dot(query_ref[...], wfeat_ref[...], preferred_element_type=F32)
         for f in range(frames):
             base = (f // per) * SLOT + (f % per) * CELLS
             for a in range(3):
@@ -131,19 +133,21 @@
                     cols_ref[f * 128 : (f + 1) * 128, (a * 3 + b) * 128 : (a * 3 + b + 1) * 128] = (
                         cells_ref[at : at + 128, :].astype(BF16)
                     )
-        feat = jnp.dot(query_ref[...], wfeat_ref[...], preferred_element_type=F32)
+        conv = jnp.dot(cols_ref[...], wconv_ref[...], preferred_element_type=F32)
+        corr = []
         for f in range(frames):
-            conv = jnp.dot(
-                cols_ref[f * 128 : (f + 1) * 128, :], wconv_ref[...], preferred_element_type=F32
-            )
             info = (f // per) * SLOT + per * CELLS + f % per
             row = line + cells_ref[info : info + 1, :]
-            conv = jnp.where((row >= 0) & (row < height), conv, 0.0).astype(BF16)
-            corr = (nt(query_ref[...], conv) * (128 ** -0.5)).astype(BF16)
-            tokens = jnp.dot(corr, wcorr_ref[...], preferred_element_type=F32)
-            tokens = tokens + feat + time_ref[f : f + 1, :]
+            inside = (row >= 0) & (row < height)
+            here = jnp.where(inside, conv[f * 128 : (f + 1) * 128], 0.0).astype(BF16)
+            corr.append((nt(query_ref[...], here) * (128 ** -0.5)).astype(BF16))
+        tokens = jnp.dot(
+            jnp.concatenate(corr, axis=0), wcorr_ref[...], preferred_element_type=F32
+        )
+        for f in range(frames):
+            here = tokens[f * 128 : (f + 1) * 128] + feat + time_ref[f : f + 1, :]
             for part in range(3):
-                tok_ref[part, pl.ds(f, 128, stride=frames), :] = tokens[
+                tok_ref[part, pl.ds(f, 128, stride=frames), :] = here[
                     :, part * 128 : (part + 1) * 128
                 ]
 
@@ -162,38 +166,52 @@
     zeros16 = jnp.zeros((16, 128), BF16)
     zeros64 = jnp.zeros((64, 128), BF16)
     attended = []
-    for g in range(CHUNK // 128):
-        lanes = slice(g * 128, (g + 1) * 128)
-        valid = frame >= start_ref[0, :, lanes]
-        heads = []
-        for pair in range(HEADS // 2):
-            one = query[2 * pair * HEAD : (2 * pair + 1) * HEAD, lanes]
-            two = query[(2 * pair + 1) * HEAD : (2 * pair + 2) * HEAD, lanes]
-            both = jnp.concatenate(
-                [
-                    jnp.concatenate([one, zeros16, zeros64], axis=0),
-                    jnp.concatenate([zeros64, two, zeros16], axis=0),
-                ],
-                axis=1,
-            )
-            scores = jnp.dot(
-                keys[lanes, pair * 128 : (pair + 1) * 128], both, preferred_element_type=F32
-            )
-            for h in range(2):
-                full = scores[:, h * 128 : (h + 1) * 128]
-                own = full[0:16, :]
-                for t in range(1, 8):
-                    own = jnp.where(track == t, full[16 * t : 16 * (t + 1), :], own)
-                own = jnp.where(valid, own, -1e30)
-                top = jnp.max(own, axis=0, keepdims=True)
-                weights = jnp.exp2((own - top) * factor)
-                probs = (weights / jnp.sum(weights, axis=0, keepdims=True)).astype(BF16)
-                spread = jnp.concatenate([probs] * 8, axis=0) * same
-                at = (2 * pair + h) * HEAD
-                heads.append(
-                    jnp.dot(values[at : at + HEAD, lanes], spread, preferred_element_type=F32)
+    for first in range(0, CHUNK // 128, BATCH):
+        some = range(first, first + BATCH)
+        own, valid = [], []
+        for g in some:
+            lanes = slice(g * 128, (g + 1) * 128)
+            valid += [frame >= start_ref[0, :, lanes]] * HEADS
+            for pair in range(HEADS // 2):
+                one = query[2 * pair * HEAD : (2 * pair + 1) * HEAD, lanes]
+                two = query[(2 * pair + 1) * HEAD : (2 * pair + 2) * HEAD, lanes]
+                both = jnp.concatenate(
+                    [
+                        jnp.concatenate([one, zeros16, zeros64], axis=0),
+                        jnp.concatenate([zeros64, two, zeros16], axis=0),
+                    ],
+                    axis=1,
                 )
-        attended.append(jnp.concatenate(heads, axis=0).T.astype(BF16))
+                scores = jnp.dot(
+                    keys[lanes, pair * 128 : (pair + 1) * 128], both, preferred_element_type=F32
+                )
+                for h in range(2):
+                    full = scores[:, h * 128 : (h + 1) * 128]
+                    part = full[0:16, :]
+                    for t in range(1, 8):
+                        part = jnp.where(track == t, full[16 * t : 16 * (t + 1), :], part)
+                    own.append(part)
+        own = [jnp.where(v, p, -1e30) for v, p in zip(valid, own)]
+        top = [jnp.max(p, axis=0, keepdims=True) for p in own]
+        weights = [jnp.exp2((p - t) * factor) for p, t in zip(own, top)]
+        total = [jnp.sum(w, axis=0, keepdims=True) for w in weights]
+        probs = [(w * (1.0 / t)).astype(BF16) for w, t in zip(weights, total)]
+        for g in some:
+            lanes = slice(g * 128, (g + 1) * 128)
+            heads = []
+            for pair in range(HEADS // 2):
+                two = [
+                    jnp.concatenate([probs[(g - first) * HEADS + 2 * pair + h]] * 8, axis=0) * same
+                    for h in range(2)
+                ]
+                at = 2 * pair * HEAD
+                both = jnp.dot(
+                    values[at : at + 2 * HEAD, lanes],
+                    jnp.concatenate(two, axis=1),
+                    preferred_element_type=F32,
+                )
+                heads += [both[:HEAD, :128], both[HEAD:, 128:]]
+            attended.append(jnp.concatenate(heads, axis=0).T.astype(BF16))
     attended = jnp.concatenate(attended, axis=0)
     mixed = tokens + jnp.dot(attended, wout_ref[...], preferred_element_type=F32)
     normed2 = rms_scale(mixed, gain2_ref[...]).astype(BF16)
@@ -210,6 +228,26 @@
 
 SMEM = pl.BlockSpec(memory_space=pltpu.SMEM)
 VMEM = pl.BlockSpec(memory_space=pltpu.VMEM)
+
+
+def refine_call(height, raw, *rest):
+    tokens, dim = rest[5].size, rest[4].shape[1]
+    chans = raw.shape[1]
+    step = pl.BlockSpec((1, 1, CHUNK), lambda i: (i, 0, 0))
+    return pl.pallas_call(
+        functools.partial(refine_kernel, height),
+        grid=(tokens // CHUNK,),
+        out_shape=jax.ShapeDtypeStruct((tokens, dim), BF16),
+        in_specs=[VMEM] * 6 + [step] + [VMEM] * (len(rest) - 6),
+        out_specs=pl.BlockSpec((CHUNK, dim), lambda i: (i, 0)),
+        scratch_shapes=[
+            pltpu.VMEM((raw.shape[0] + 16, 128), F32),
+            pltpu.VMEM((tokens, 9 * chans), BF16),
+            pltpu.VMEM((3, tokens, 128), F32),
+        ],
+        compiler_params=params(48),
+        name="refine",
+    )(raw, *rest)
 
 
 def body(
@@ -284,39 +322,9 @@
     wcorr = jnp.pad(wcorr.reshape(WIN * RAW, dim), ((0, 128 - WIN * RAW), (0, 0)))
     tokens = tracks * total
     start = jnp.repeat(start_frames, total).reshape(tokens // CHUNK, 1, CHUNK)
-    whole = lambda *shape: pl.BlockSpec(shape, lambda i: (0,) * len(shape))
-    refined = pl.pallas_call(
-        functools.partial(refine_kernel, n_tiles * rows),
-        grid=(tokens // CHUNK,),
-        out_shape=jax.ShapeDtypeStruct((tokens, dim), BF16),
-        in_specs=[
-            whole(blocks * PROWS, chans),
-            whole(9 * chans, chans),
-            whole(tracks, chans),
-            whole(128, dim),
-            whole(chans, dim),
-            whole(total, dim),
-            pl.BlockSpec((1, 1, CHUNK), lambda i: (i, 0, 0)),
-            whole(1, dim),
-            whole(dim, HEADS * 64),
-            whole(dim, dim),
-            whole(dim, dim),
-            whole(dim, dim),
-            whole(1, dim),
-            whole(*w_up.shape),
-            whole(*w_down.shape),
-        ],
-        out_specs=pl.BlockSpec((CHUNK, dim), lambda i: (i, 0)),
-        scratch_shapes=[
-            pltpu.VMEM((blocks * PROWS + 16, 128), F32),
-            pltpu.VMEM((total * 128, 9 * chans), BF16),
-            pltpu.VMEM((3, tokens, 128), F32),
-        ],
-        compiler_params=params(56),
-        name="refine",
-    )(
-        raw, w_conv.reshape(9 * chans, chans), query_feats, wcorr, w_feat, time_embed, start,
-        gain_attn.reshape(1, dim), wk, wq, wv, w_attn_out, gain_mlp.reshape(1, dim), w_up, w_down,
+    refined = refine_call(
+        n_tiles * rows, raw, w_conv.reshape(9 * chans, chans), query_feats, wcorr, w_feat, time_embed,
+        start, gain_attn.reshape(1, dim), wk, wq, wv, w_attn_out, gain_mlp.reshape(1, dim), w_up, w_down,
     )
     return refined.reshape(tracks, total, dim)
 

time: 114 us -> 96.1 us (0.84)
  Pallas kernels: 40.7 us -> 22.2 us
  local copies, waits for them, and re-layouts: 9.45 us -> 12.6 us
  waiting for transfers between devices: 18.1 us -> 15.3 us
    pallas_call x1, Pallas kernels: 37.2 us -> 18.4 us  [refine_call(): pl.pallas_call(functools.partial(refine_kernel, height), grid=(tokens //...]
    all_to_all x1, waiting for transfers between devices: 7.76 us -> 4.99 us  [body(): raw = lax.all_to_all(routed, ('frames', 'tiles'), 0, 0, tiled=True)]
    reshape x1, local copies, waits for them, and re-layouts: 0.04 us -> 1.55 us  [body(): w_corr.reshape(WIN, WIN, dim)]
    unnamed x23 -> x33, local copies, waits for them, and re-layouts: 5.66 us -> 5.84 us
  transfers between devices with their start and end apart: 3 -> 3, of which waited for: 3 -> 3; matrix products, arithmetic and copies ran while one was open for 5% -> 9% of each run, Pallas kernels for 0% -> 0%
where the time goes in v1:
time: 96.1 us; the launch traced here: 95.4 us
  blocking collectives  30.5 us (32%)
  Pallas kernels  22.2 us (23%)
  waiting for transfers between devices  15.3 us (16%)
  starting transfers between devices  12.7 us (13%)
  local copies, waits for them, and re-layouts  12.6 us (13%)
  other arithmetic  1.91 us (2%)
    all_to_all x1, blocking collectives, body(): spread = lax.all_to_all(pieces, 'tiles', 0, 0, tiled=True)  30.5 us
    pallas_call x1, Pallas kernels, refine_call(): pl.pallas_call(functools.partial(refine_kernel, height), grid=(tokens //...  18.4 us
    ppermute x1, waiting for transfers between devices, body(): low = lax.ppermute(up, 'tiles', [(i, i + 1) for i in range(n_tiles - 1)])  5.93 us
    unnamed x33, local copies, waits for them, and re-layouts  5.84 us
    all_to_all x1, starting transfers between devices, body(): raw = lax.all_to_all(routed, ('frames', 'tiles'), 0, 0, tiled=True)  5.52 us
    ppermute x1, starting transfers between devices, body(): low = lax.ppermute(up, 'tiles', [(i, i + 1) for i in range(n_tiles - 1)])  5.25 us
    all_to_all x1, waiting for transfers between devices, body(): raw = lax.all_to_all(routed, ('frames', 'tiles'), 0, 0, tiled=True)  4.99 us
    ppermute x1, waiting for transfers between devices, body(): high = lax.ppermute(down, 'tiles', [(i + 1, i) for i in range(n_tiles - 1)])  4.4 us
  transfers between devices with their start and end apart: 3, of which 3 were waited for; matrix products, arithmetic and copies ran while one was open for 9% of the time, Pallas kernels for 0%

profile of v1, /device:TPU:1, one launch (start us, length us, event | category | flops | bytes accessed | tf_op | source)
XLA Modules:
  0.0 95.4 jit_solution(4906804615402104784)
XLA Ops:
  0.0 0.9 convert_reduce_fusion.rank_ref
  0.9 0.8 convert_reduce_fusion.1
  1.8 0.2 select_reduce_fusion.ids_ref
  1.9 2.1 %copy-done = bf16[4,8,480,128]{3,2,1,0:T(8,128)(2,1)S(1)} copy-done((bf16[4,8,480,128]{3,2,1,0:T(8,128)(2,1)S(1)}, bf16[4,8,480,128]{3,2,1,0:T(8,128)(2,1)}, u32[]{:S(2)}) %copy-start) | copy-done | bytes 3932184
  4.0 0.7 copy-done.8
  4.7 0.9 edges.1
  5.6 5.3 %collective-permute-start = (bf16[2688,128]{1,0:T(8,128)(2,1)S(1)}, bf16[2688,128]{1,0:T(8,128)(2,1)S(1)}, u32[]{:S(2)}, u32[]{:S(2)}) collective-permute-start(bf16[2688,128]{1,0:T(8,128)(2,1)S(1)} %get-tuple-element.7), channel_id=1, source_target_pairs={{0,1},{1,2},{2,3},{3,4},{4,5},{5,6},{6,7},{7,8},{8,9},{9,10},{10,1... | collective-permute-start | bytes 2064392 | tf_op jit(solution)/shard_map/ppermute | solution.py:290
  10.9 1.9 %collective-permute-start.1 = (bf16[2688,128]{1,0:T(8,128)(2,1)S(1)}, bf16[2688,128]{1,0:T(8,128)(2,1)S(1)}, u32[]{:S(2)}, u32[]{:S(2)}) collective-permute-start(bf16[2688,128]{1,0:T(8,128)(2,1)S(1)} %get-tuple-element.8), channel_id=1, source_target_pairs={{1,0},{2,1},{3,2},{4,3},{5,4},{6,5},{7,6},{8,7},{9,8},{10,9},{11,1... | collective-permute-start | bytes 2064392 | tf_op jit(solution)/shard_map/ppermute | solution.py:291
  12.8 5.9 %collective-permute-done.low_ref = bf16[2688,128]{1,0:T(8,128)(2,1)S(1)} collective-permute-done((bf16[2688,128]{1,0:T(8,128)(2,1)S(1)}, bf16[2688,128]{1,0:T(8,128)(2,1)S(1)}, u32[]{:S(2)}, u32[]{:S(2)}) %collective-permute-start) | collective-permute-done | bytes 688160 | tf_op jit(solution)/shard_map/ppermute | solution.py:290
  18.7 4.4 %collective-permute-done.1.high_ref = bf16[2688,128]{1,0:T(8,128)(2,1)S(1)} collective-permute-done((bf16[2688,128]{1,0:T(8,128)(2,1)S(1)}, bf16[2688,128]{1,0:T(8,128)(2,1)S(1)}, u32[]{:S(2)}, u32[]{:S(2)}) %collective-permute-start.1) | collective-permute-done | bytes 688160 | tf_op jit(solution)/shard_map/ppermute | solution.py:291
  23.1 0.0 copy-done.9
  23.1 1.2 %windows.1 = bf16[32,192,128]{2,1,0:T(8,128)(2,1)S(1)} custom-call(s32[3,12]{1,0:T(4,128)S(1)} %select_reduce_fusion.ids_ref, s32[3]{0:T(128)S(1)} %get-tuple-element.9.count_ref, s32[1]{0:T(128)} %bitcast.1.info_ref, s32[4,128]{1,0:T(4,128)S(1)} %copy-done.8, s32[4,128]{1,0:T(4,128)S(1)} %copy-done.9, bf16[4,8,480,128]{3,2,1,0:T(8,128)(2,1)S(1)} %copy-done, ...), custom_call_target="tpu_custom_call" | custom-call | tf_op jit(solution)/shard_map/windows/pallas_call | solution.py:292
  24.3 0.0 copy-start.10
  24.3 30.5 %all_to_all.10.in_ref = bf16[32,192,128]{2,1,0:T(8,128)(2,1)S(1)} all-to-all(bf16[32,192,128]{2,1,0:T(8,128)(2,1)S(1)} %windows.1), channel_id=1, replica_groups=mesh['frames'=4,'tiles'=32] {'tiles'}, dimensions={0} | all-to-all | bytes 3145728 | tf_op jit(solution)/shard_map/all_to_all | solution.py:306
  54.8 0.0 copy-done.10
  54.8 1.7 %route.1 = bf16[128,16,128]{2,1,0:T(8,128)(2,1)} custom-call(s32[128]{0:T(128)S(1)} %bitcast.15, s32[128]{0:T(128)S(1)} %convert_reduce_fusion.rank_ref, bf16[32,192,128]{2,1,0:T(8,128)(2,1)S(1)} %all_to_all.10.in_ref), custom_call_target="tpu_custom_call" | custom-call | tf_op jit(solution)/shard_map/route/pallas_call | solution.py:307
  56.5 5.5 %all-to-all-start.1 = ((bf16[128,16,128]{2,1,0:T(8,128)(2,1)}), bf16[128,16,128]{2,1,0:T(8,128)(2,1)S(1)}, u32[]{:S(2)}, u32[]{:S(2)}) async-start(bf16[128,16,128]{2,1,0:T(8,128)(2,1)} %route.1), calls=%async_computation.1 | async-start | bytes 1048576 | tf_op jit(solution)/shard_map/all_to_all | solution.py:315
  62.0 0.0 copy-done.11
  62.1 0.8 fusion.1
  62.9 0.2 copy.29
  63.1 0.0 copy-start.14
  63.1 0.0 copy-start.12
  63.1 0.0 copy-start.13
  63.2 0.0 copy-start.1
  63.2 0.0 copy-start.3
  63.2 0.0 copy-start.4
  63.2 0.0 copy-start.5
  63.2 0.0 copy-start.6
  63.2 0.0 copy-start.7
  63.2 0.2 copy.28.wk_ref
  63.4 0.2 copy.30
  63.7 1.3 %copy.31 = bf16[384,384]{0,1:T(8,128)(2,1)S(1)} copy(bf16[384,384]{1,0:T(8,128)(2,1)} %get-tuple-element.11) | data formatting | bytes 589824
  64.9 1.6 %reshape.96 = bf16[9,9,384]{2,1,0:T(8,128)(2,1)} reshape(bf16[81,384]{1,0:T(8,128)(2,1)} %param.23) | data formatting | bytes 124416 | tf_op jit(solution)/shard_map/reshape | solution.py:321
  66.5 0.9 pad.12
  67.4 0.7 reshape.97
  68.1 0.9 pad.13.wcorr_ref
  69.0 0.0 copy-done.14
  69.0 0.1 broadcast_in_dim.23
  69.1 0.7 broadcast_in_dim.24
  69.8 0.9 broadcast_in_dim.26.start_ref
  70.7 0.0 copy-done.12
  70.7 0.0 copy-done.13
  70.7 5.0 %all-to-all-done.1 = bf16[128,16,128]{2,1,0:T(8,128)(2,1)S(1)} async-done(((bf16[128,16,128]{2,1,0:T(8,128)(2,1)}), bf16[128,16,128]{2,1,0:T(8,128)(2,1)S(1)}, u32[]{:S(2)}, u32[]{:S(2)}) %all-to-all-start.1) | async-done | bytes 524320 | tf_op jit(solution)/shard_map/all_to_all | solution.py:315
  75.7 0.0 copy-done.1
  75.7 0.0 copy-done.3
  75.8 0.0 copy-start.2
  75.8 1.3 %copy-done.2 = bf16[1536,384]{1,0:T(8,128)(2,1)S(1)} copy-done((bf16[1536,384]{1,0:T(8,128)(2,1)S(1)}, bf16[1536,384]{1,0:T(8,128)(2,1)}, u32[]{:S(2)}) %copy-start.2) | copy-done | bytes 1179672
  77.0 18.4 %refine.1 = bf16[2048,384]{1,0:T(8,128)(2,1)} custom-call(bf16[2048,128]{1,0:T(8,128)(2,1)S(1)} %bitcast.9, bf16[1152,128]{1,0:T(8,128)(2,1)S(1)} %bitcast.12, bf16[128,128]{1,0:T(8,128)(2,1)S(1)} %copy-done.6, bf16[128,384]{1,0:T(8,128)(2,1)S(1)} %pad.13.wcorr_ref, bf16[128,384]{1,0:T(8,128)(2,1)S(1)} %copy-done.5, f32[16,384]{1,0:T(8,128)S(1)} %copy-done.7, ...), custom_call_target="tpu_custom_call" | custom-call | tf_op jit(solution)/shard_map/refine/pallas_call | solution.py:237
  (13 shorter events, 0.1 us)
Async XLA Ops:
  1.9 2.1 %copy-start = (bf16[4,8,480,128]{3,2,1,0:T(8,128)(2,1)S(1)}, bf16[4,8,480,128]{3,2,1,0:T(8,128)(2,1)}, u32[]{:S(2)}) copy-start(bf16[4,8,480,128]{3,2,1,0:T(8,128)(2,1)} %feat_ref.3) | copy-start | bytes 11796484
  4.0 0.7 copy-start.8
  4.7 18.4 %copy-start.9 = (s32[4,128]{1,0:T(4,128)S(1)}, s32[4,128]{1,0:T(4,128)}, u32[]{:S(2)}) copy-start(s32[4,128]{1,0:T(4,128)} %offs_ref.1) | copy-start | bytes 6148
  5.6 13.1 %collective-permute-start = (bf16[2688,128]{1,0:T(8,128)(2,1)S(1)}, bf16[2688,128]{1,0:T(8,128)(2,1)S(1)}, u32[]{:S(2)}, u32[]{:S(2)}) collective-permute-start(bf16[2688,128]{1,0:T(8,128)(2,1)S(1)} %get-tuple-element.7), channel_id=1, source_target_pairs={{0,1},{1,2},{2,3},{3,4},{4,5},{5,6},{6,7},{7,8},{8,9},{9,10},{10,1... | collective-permute-start | bytes 2064392 | tf_op jit(solution)/shard_map/ppermute | solution.py:290
  10.9 12.3 %collective-permute-start.1 = (bf16[2688,128]{1,0:T(8,128)(2,1)S(1)}, bf16[2688,128]{1,0:T(8,128)(2,1)S(1)}, u32[]{:S(2)}, u32[]{:S(2)}) collective-permute-start(bf16[2688,128]{1,0:T(8,128)(2,1)S(1)} %get-tuple-element.8), channel_id=1, source_target_pairs={{1,0},{2,1},{3,2},{4,3},{5,4},{6,5},{7,6},{8,7},{9,8},{10,9},{11,1... | collective-permute-start | bytes 2064392 | tf_op jit(solution)/shard_map/ppermute | solution.py:291
  24.3 30.5 %copy-start.10 = (s32[128,1]{0,1:T(1,128)S(1)}, s32[128,1]{0,1:T(1,128)}, u32[]{:S(2)}) copy-start(s32[128,1]{0,1:T(1,128)} %param.21) | copy-start | bytes 1540
  54.8 7.3 %copy-start.11 = (bf16[384,1152]{1,0:T(8,128)(2,1)S(1)}, bf16[384,1152]{1,0:T(8,128)(2,1)}, u32[]{:S(2)}) copy-start(bf16[384,1152]{1,0:T(8,128)(2,1)} %param.27) | copy-start | bytes 2654212
  56.5 19.2 %all-to-all-start.1 = ((bf16[128,16,128]{2,1,0:T(8,128)(2,1)}), bf16[128,16,128]{2,1,0:T(8,128)(2,1)S(1)}, u32[]{:S(2)}, u32[]{:S(2)}) async-start(bf16[128,16,128]{2,1,0:T(8,128)(2,1)} %route.1), calls=%async_computation.1 | async-start | bytes 1048576 | tf_op jit(solution)/shard_map/all_to_all | solution.py:315
  63.1 5.9 %copy-start.14 = (s32[128]{0:T(128)S(1)}, s32[128]{0:T(128)}, u32[]{:S(2)}) copy-start(s32[128]{0:T(128)} %param.22) | copy-start | bytes 1540
  63.1 7.6 %copy-start.12 = (f32[384]{0:T(512)S(1)}, f32[384]{0:T(512)}, u32[]{:S(2)}) copy-start(f32[384]{0:T(512)} %param.29) | copy-start | bytes 4612
  63.1 7.6 %copy-start.13 = (f32[384]{0:T(512)S(1)}, f32[384]{0:T(512)}, u32[]{:S(2)}) copy-start(f32[384]{0:T(512)} %param.26) | copy-start | bytes 4612
  63.2 12.6 %copy-start.1 = (bf16[384,1536]{1,0:T(8,128)(2,1)S(1)}, bf16[384,1536]{1,0:T(8,128)(2,1)}, u32[]{:S(2)}) copy-start(bf16[384,1536]{1,0:T(8,128)(2,1)} %wup_ref.1) | copy-start | bytes 3538948
  63.2 12.6 %copy-start.3 = (bf16[3,3,128,128]{3,2,1,0:T(8,128)(2,1)S(1)}, bf16[3,3,128,128]{3,2,1,0:T(8,128)(2,1)}, u32[]{:S(2)}) copy-start(bf16[3,3,128,128]{3,2,1,0:T(8,128)(2,1)} %param.17) | copy-start | bytes 884740
  63.2 12.5 %copy-start.4 = (bf16[384,384]{1,0:T(8,128)(2,1)S(1)}, bf16[384,384]{1,0:T(8,128)(2,1)}, u32[]{:S(2)}) copy-start(bf16[384,384]{1,0:T(8,128)(2,1)} %wout_ref.1) | copy-start | bytes 884740
  63.2 12.5 %copy-start.5 = (bf16[128,384]{1,0:T(8,128)(2,1)S(1)}, bf16[128,384]{1,0:T(8,128)(2,1)}, u32[]{:S(2)}) copy-start(bf16[128,384]{1,0:T(8,128)(2,1)} %wfeat_ref.1) | copy-start | bytes 294916
  63.2 12.5 %copy-start.6 = (bf16[128,128]{1,0:T(8,128)(2,1)S(1)}, bf16[128,128]{1,0:T(8,128)(2,1)}, u32[]{:S(2)}) copy-start(bf16[128,128]{1,0:T(8,128)(2,1)} %query_ref.1) | copy-start | bytes 98308
  63.2 12.5 %copy-start.7 = (f32[16,384]{1,0:T(8,128)S(1)}, f32[16,384]{1,0:T(8,128)}, u32[]{:S(2)}) copy-start(f32[16,384]{1,0:T(8,128)} %time_ref.1) | copy-start | bytes 73732
  75.8 1.3 %copy-start.2 = (bf16[1536,384]{1,0:T(8,128)(2,1)S(1)}, bf16[1536,384]{1,0:T(8,128)(2,1)}, u32[]{:S(2)}) copy-start(bf16[1536,384]{1,0:T(8,128)(2,1)} %wdown_ref.1) | copy-start | bytes 3538948

commit v2 on v1

--- a/solution.py
+++ b/solution.py
@@ -26,63 +26,98 @@
 BF16 = jnp.bfloat16
 
 
-def window_rows(feat_ref, tmp_ref, dst_ref, base, frame, row0, rows, col):
-    wide = feat_ref.shape[2]
-    start = pl.multiple_of(jnp.clip((col >> 4) << 4, 0, wide - 32), 16)
-    tmp_ref[0:rows, 8:40, :] = feat_ref[frame, row0 : row0 + rows, pl.ds(start, 32), :].astype(F32)
+def aligned(col, wide):
+    return pl.multiple_of(jnp.clip((col >> 4) << 4, 0, wide - 32), 16)
+
+
+def window_rows(source, rows, shift, tmp_ref, dst_ref, base):
+    tmp_ref[0:rows, 8:40, :] = source.astype(F32)
     for i in range(rows):
-        dst_ref[base + RAW * i : base + RAW * i + 16, :] = tmp_ref[i, pl.ds(8 + col - start, 16), :]
-
-
-def edge_kernel(ids_ref, count_ref, cols_ref, feat_ref, up_ref, down_ref, tmp_ref, win_ref):
-    frames = feat_ref.shape[0]
-    rows = feat_ref.shape[1]
+        dst_ref[base + RAW * i : base + RAW * i + 16, :] = tmp_ref[i, pl.ds(8 + shift, 16), :]
+
+
+def edge_kernel(
+    owners_ref, cols_ref, feat_ref, pair_ref, cross_ref, ids_ref, buf_ref, tmp_ref, win_ref, sems
+):
+    frames, rows, wide, _ = feat_ref.shape
+    tile = lax.axis_index("tiles")
+
+    def scan(b, counts):
+        near = owners_ref[b] - tile + 1
+        for d in range(3):
+            ids_ref[16 * d + counts[d]] = b
+        return tuple(counts[d] + (near == d).astype(jnp.int32) for d in range(3))
+
+    zero = jnp.int32(0)
+    counts = lax.fori_loop(0, owners_ref.shape[0], scan, (zero, zero, zero), unroll=8)
+    for d in range(3):
+        ids_ref[48 + d] = counts[d]
+    odd = tile & 1
+    parts = []
+    for w, after in ((0, odd), (1, 1 - odd)):
+        first = jnp.where(after == 1, rows - EDGE, 0)
+        parts.append((w, 32 * after, ids_ref[48 + 2 * after], first))
+
+    def copy(w, s, k, first, block):
+        start = aligned(cols_ref[k, block] - 1, wide)
+        return pltpu.make_async_copy(
+            feat_ref.at[k, pl.ds(first, EDGE), pl.ds(start, 32), :], buf_ref.at[w, s, k], sems.at[w, s, k]
+        )
+
+    for w, at, count, first in parts:
+
+        def begin(s, carry):
+            for k in range(frames):
+                copy(w, s, k, first, ids_ref[at + s]).start()
+            return carry
+
+        lax.fori_loop(0, count, begin, 0)
     tmp_ref[...] = jnp.zeros_like(tmp_ref)
-
-    def part(which, row0, out_ref):
+    win_ref[...] = jnp.zeros_like(win_ref)
+    for w, at, count, first in parts:
+        out_ref = (cross_ref, pair_ref)[w]
+
         def slot(s, carry):
-            block = ids_ref[which, s]
+            block = ids_ref[at + s]
             for k in range(frames):
-                window_rows(
-                    feat_ref, tmp_ref, win_ref, k * MSG, k, row0, EDGE, cols_ref[k, block] - 1
-                )
+                copy(w, s, k, first, block).wait()
+                col = cols_ref[k, block] - 1
+                window_rows(buf_ref[w, s, k], EDGE, col - aligned(col, wide), tmp_ref, win_ref, k * MSG)
             out_ref[pl.ds(pl.multiple_of(s * frames * MSG, 16), frames * MSG), :] = win_ref[
                 0 : frames * MSG, :
             ].astype(BF16)
             return carry
 
-        lax.fori_loop(0, count_ref[which], slot, 0)
-
-    win_ref[...] = jnp.zeros_like(win_ref)
-    part(2, rows - EDGE, up_ref)
-    part(0, 0, down_ref)
+        lax.fori_loop(0, count, slot, 0)
 
 
 def merge_kernel(
-    ids_ref, count_ref, info_ref, cols_ref, offs_ref, feat_ref, low_ref, high_ref, out_ref,
-    tmp_ref, side_ref, win_ref, all_ref,
+    ids_ref, cols_ref, offs_ref, feat_ref, pair_ref, cross_ref, out_ref, tmp_ref, side_ref, win_ref, all_ref
 ):
-    frames, rows = feat_ref.shape[0], feat_ref.shape[1]
+    frames, rows, wide, _ = feat_ref.shape
+    tile = lax.axis_index("tiles")
+    odd = tile & 1
     tmp_ref[...] = jnp.zeros_like(tmp_ref)
     win_ref[...] = jnp.zeros_like(win_ref)
 
     def slot(s, carry):
-        block = ids_ref[1, s]
+        block = ids_ref[16 + s]
         here = pl.ds(pl.multiple_of(s * frames * MSG, 16), frames * MSG)
-        side_ref[0] = low_ref[here, :].astype(F32)
-        side_ref[1] = high_ref[here, :].astype(F32)
+        side_ref[odd] = cross_ref[here, :].astype(F32)
+        side_ref[1 - odd] = pair_ref[here, :].astype(F32)
         own = EDGE * RAW
         for k in range(frames):
-            row = offs_ref[k, block]
+            row, col = offs_ref[k, block], cols_ref[k, block] - 1
             win_ref[0:MSG, :] = side_ref[0, k * MSG : (k + 1) * MSG, :]
-            window_rows(feat_ref, tmp_ref, win_ref, own, k, 0, rows, cols_ref[k, block] - 1)
+            start = aligned(col, wide)
+            window_rows(feat_ref[k, :, pl.ds(start, 32), :], rows, col - start, tmp_ref, win_ref, own)
             top = own + rows * RAW
             win_ref[top : top + MSG, :] = side_ref[1, k * MSG : (k + 1) * MSG, :]
             all_ref[k * CELLS : k * CELLS + 128, :] = win_ref[pl.ds(row * RAW, 128), :]
         end = frames * CELLS
         all_ref[end:SLOT, :] = jnp.zeros((SLOT - end, 128), F32)
         for k in range(frames):
-            first = (info_ref[0] * rows + offs_ref[k, block] - WIN // 2).astype(F32)
+            first = (tile * rows + offs_ref[k, block] - WIN // 2).astype(F32)
             all_ref[end + k : end + k + 1, :] = jnp.full((1, 128), first, F32)
         for i in range(PIECES):
             out_ref[i, pl.ds(pl.multiple_of(s * PROWS, 16), PROWS), :] = all_ref[
@@ -90,15 +125,15 @@
             ].astype(BF16)
         return carry
 
-    lax.fori_loop(0, count_ref[1], slot, 0)
-
-
-def route_kernel(owner_ref, rank_ref, in_ref, out_ref):
+    lax.fori_loop(0, ids_ref[49], slot, 0)
+
+
+def route_kernel(index_ref, in_ref, out_ref):
     def step(b, carry):
-        out_ref[b] = in_ref[owner_ref[b], pl.ds(pl.multiple_of(rank_ref[b] * PROWS, 16), PROWS), :]
+        out_ref[b] = in_ref[index_ref[b]]
         return carry
 
-    lax.fori_loop(0, out_ref.shape[0], step, 0, unroll=8)
+    lax.fori_loop(0, out_ref.shape[0], step, 0, unroll=16)
 
 
 def nt(a, b):
@@ -112,7 +147,7 @@
 def refine_kernel(
     height, raw_ref, wconv_ref, query_ref, wcorr_ref, wfeat_ref, time_ref, start_ref, gain1_ref,
     wk_ref, wq_ref, wv_ref, wout_ref, gain2_ref, wup_ref, wdown_ref, out_ref,
-    cells_ref, cols_ref, tok_ref,
+    cells_ref, cols_ref, tok_ref, down_ref, sem,
 ):
     groups, per = raw_ref.shape[0] // SLOT, 4
     frames = groups * per
@@ -120,6 +155,8 @@
 
     @pl.when(step == 0)
     def _():
+        fetch = pltpu.make_async_copy(wdown_ref, down_ref, sem)
+        fetch.start()
         cells_ref[0 : groups * SLOT, :] = raw_ref[...].astype(F32)
         cells_ref[groups * SLOT :, :] = jnp.zeros_like(cells_ref[groups * SLOT :, :])
         line = lax.broadcasted_iota(jnp.int32, (128, 128), 0) // RAW
@@ -150,6 +187,7 @@
                 tok_ref[part, pl.ds(f, 128, stride=frames), :] = here[
                     :, part * 128 : (part + 1) * 128
                 ]
+        fetch.wait()
 
     here = pl.ds(pl.multiple_of(step * CHUNK, CHUNK), CHUNK)
     tokens = jnp.concatenate([tok_ref[part, here, :] for part in range(3)], axis=1)
@@ -211,14 +249,14 @@
                     preferred_element_type=F32,
                 )
                 heads += [both[:HEAD, :128], both[HEAD:, 128:]]
-            attended.append(jnp.concatenate(heads, axis=0).T.astype(BF16))
+            attended.append(jnp.concatenate(heads, axis=0).astype(BF16).T)
     attended = jnp.concatenate(attended, axis=0)
     mixed = tokens + jnp.dot(attended, wout_ref[...], preferred_element_type=F32)
     normed2 = rms_scale(mixed, gain2_ref[...]).astype(BF16)
     hidden = jax.nn.gelu(
         jnp.dot(normed2, wup_ref[...], preferred_element_type=F32), approximate=True
     ).astype(BF16)
-    result = mixed + jnp.dot(hidden, wdown_ref[...], preferred_element_type=F32)
+    result = mixed + jnp.dot(hidden, down_ref[...], preferred_element_type=F32)
     out_ref[...] = result.astype(BF16)
 
 
@@ -228,6 +266,7 @@
 
 SMEM = pl.BlockSpec(memory_space=pltpu.SMEM)
 VMEM = pl.BlockSpec(memory_space=pltpu.VMEM)
+HBM = pl.BlockSpec(memory_space=pltpu.HBM)
 
 
 def refine_call(height, raw, *rest):
@@ -238,16 +277,18 @@
         functools.partial(refine_kernel, height),
         grid=(tokens // CHUNK,),
         out_shape=jax.ShapeDtypeStruct((tokens, dim), BF16),
-        in_specs=[VMEM] * 6 + [step] + [VMEM] * (len(rest) - 6),
+        in_specs=[VMEM] * 6 + [step] + [VMEM] * (len(rest) - 7) + [HBM],
         out_specs=pl.BlockSpec((CHUNK, dim), lambda i: (i, 0)),
         scratch_shapes=[
             pltpu.VMEM((raw.shape[0] + 16, 128), F32),
             pltpu.VMEM((tokens, 9 * chans), BF16),
             pltpu.VMEM((3, tokens, 128), F32),
+            pltpu.VMEM(rest[-1].shape, BF16),
+            pltpu.SemaphoreType.DMA,
         ],
-        compiler_params=params(48),
+        compiler_params=params(32),
         name="refine",
-    )(raw, *rest)
+    )(raw, *rest[:-1], pltpu.with_memory_space_constraint(rest[-1], pltpu.HBM))
 
 
 def body(
@@ -255,7 +296,6 @@
     time_embed, gain_attn, w_qkv, w_attn_out, gain_mlp, w_up, w_down,
 ):
     n_tiles = lax.axis_size("tiles")
-    tile = lax.axis_index("tiles")
     frames, rows, width, chans = features.shape
     blocks = owners.shape[0]
     tracks = query_feats.shape[0]
@@ -267,32 +307,28 @@
     rank = jnp.sum(
         (owner[:, None] == owner[None, :]) & (number[None, :] < number[:, None]), axis=1, dtype=jnp.int32
     )
-    near = tile + jnp.arange(-1, 2, dtype=jnp.int32)
-    mine = owner[None, :] == near[:, None]
-    count = jnp.sum(mine, axis=1, dtype=jnp.int32)
-    slots = jnp.arange(CAP, dtype=jnp.int32)
-    ids = jnp.sum(
-        jnp.where(mine[:, None, :] & (rank[None, None, :] == slots[None, :, None]), number, 0),
-        axis=2,
-        dtype=jnp.int32,
-    )
-
     message = jax.ShapeDtypeStruct((CAP * frames * MSG, chans), BF16)
-    up, down = pl.pallas_call(
+    pair, cross, ids = pl.pallas_call(
         edge_kernel,
-        out_shape=(message, message),
-        in_specs=[SMEM, SMEM, SMEM, VMEM],
-        out_specs=(VMEM, VMEM),
-        scratch_shapes=[pltpu.VMEM((TILE, 48, 128), F32), pltpu.VMEM((frames * MSG + 16, 128), F32)],
+        out_shape=(message, message, jax.ShapeDtypeStruct((64,), jnp.int32)),
+        in_specs=[SMEM, SMEM, HBM],
+        out_specs=(VMEM, VMEM, SMEM),
+        scratch_shapes=[
+            pltpu.VMEM((2, CAP, frames, EDGE, 32, chans), BF16),
+            pltpu.VMEM((TILE, 48, 128), F32),
+            pltpu.VMEM((frames * MSG + 16, 128), F32),
+            pltpu.SemaphoreType.DMA((2, CAP, frames)),
+        ],
         compiler_params=params(24),
         name="edges",
-    )(ids, count, offset_cols, features)
-    low = lax.ppermute(up, "tiles", [(i, i + 1) for i in range(n_tiles - 1)])
-    high = lax.ppermute(down, "tiles", [(i + 1, i) for i in range(n_tiles - 1)])
+    )(owner, offset_cols, pltpu.with_memory_space_constraint(features, pltpu.HBM))
+    beside = [(i, ((i - 1) ^ 1) + 1) for i in range(1, n_tiles - 1)]
+    cross = lax.ppermute(cross, "tiles", beside)
+    pair = lax.ppermute(pair, "tiles", [(i, i ^ 1) for i in range(n_tiles)])
     pieces = pl.pallas_call(
         merge_kernel,
         out_shape=jax.ShapeDtypeStruct((PIECES, CAP * PROWS, chans), BF16),
-        in_specs=[SMEM, SMEM, SMEM, SMEM, SMEM, VMEM, VMEM, VMEM],
+        in_specs=[SMEM, SMEM, SMEM, VMEM, VMEM, VMEM],
         out_specs=VMEM,
         scratch_shapes=[
             pltpu.VMEM((TILE, 48, 128), F32),
@@ -302,16 +338,16 @@
         ],
         compiler_params=params(24),
         name="windows",
-    )(ids, count, tile.reshape(1), offset_cols, offset_rows, features, low, high)
+    )(ids, offset_cols, offset_rows, features, pair, cross)
     spread = lax.all_to_all(pieces, "tiles", 0, 0, tiled=True)
     routed = pl.pallas_call(
         route_kernel,
         out_shape=jax.ShapeDtypeStruct((blocks, PROWS, chans), BF16),
-        in_specs=[SMEM, SMEM, VMEM],
+        in_specs=[SMEM, VMEM],
         out_specs=VMEM,
         compiler_params=params(24),
         name="route",
-    )(owner, rank, spread)
+    )(owner * CAP + rank, spread.reshape(n_tiles * CAP, PROWS, chans))
     raw = lax.all_to_all(routed, ("frames", "tiles"), 0, 0, tiled=True)
     raw = raw.reshape(blocks * PROWS, chans)
 

time: 96.1 us -> 95 us (0.989)
  blocking collectives: 30.5 us -> 0 us
  waiting for transfers between devices: 15.3 us -> 36 us
  starting transfers between devices: 12.7 us -> 21.3 us
  Pallas kernels: 22.2 us -> 27.1 us
  local copies, waits for them, and re-layouts: 12.6 us -> 9.93 us
  other arithmetic: 1.91 us -> 0.17 us
    all_to_all x1 -> x0, blocking collectives: 30.5 us -> none  [body(): spread = lax.all_to_all(pieces, 'tiles', 0, 0, tiled=True)]
    all_to_all x0 -> x1, waiting for transfers between devices: none -> 22.5 us  [body(): spread = lax.all_to_all(pieces, 'tiles', 0, 0, tiled=True)]
    all_to_all x0 -> x1, starting transfers between devices: none -> 10.3 us  [body(): spread = lax.all_to_all(pieces, 'tiles', 0, 0, tiled=True)]
    pallas_call x1, Pallas kernels: 0.89 us -> 4.22 us  [body(): pl.pallas_call(edge_kernel, out_shape=(message, message, jax.ShapeDtypeSt...]
    unnamed x33 -> x35, local copies, waits for them, and re-layouts: 5.84 us -> 3.12 us
    ppermute x2, starting transfers between devices: 7.17 us -> 5.33 us  [the longest x1 3.7 us: body(): cross = lax.ppermute(cross, 'tiles', beside)]
    pallas_call x1, Pallas kernels: 1.16 us -> 2.95 us  [body(): pl.pallas_call(merge_kernel, out_shape=jax.ShapeDtypeStruct((PIECES, CAP...]
    ppermute x2, waiting for transfers between devices: 10.3 us -> 8.6 us  [the longest x1 8.6 us: body(): cross = lax.ppermute(cross, 'tiles', beside)]
  transfers between devices with their start and end apart: 3 -> 4, of which waited for: 3 -> 3; matrix products, arithmetic and copies ran while one was open for 9% -> 9% of each run, Pallas kernels for 0% -> 0%
where the time goes in v2:
time: 95 us; the launch traced here: 94.9 us
  waiting for transfers between devices  36 us (38%)
  Pallas kernels  27.1 us (29%)
  starting transfers between devices  21.3 us (22%)
  local copies, waits for them, and re-layouts  9.93 us (10%)
    all_to_all x1, waiting for transfers between devices, body(): spread = lax.all_to_all(pieces, 'tiles', 0, 0, tiled=True)  22.5 us
    pallas_call x1, Pallas kernels, refine_call(): pl.pallas_call(functools.partial(refine_kernel, height), grid=(tokens //...  18.4 us
    all_to_all x1, starting transfers between devices, body(): spread = lax.all_to_all(pieces, 'tiles', 0, 0, tiled=True)  10.3 us
    ppermute x1, waiting for transfers between devices, body(): cross = lax.ppermute(cross, 'tiles', beside)  8.6 us
    all_to_all x1, starting transfers between devices, body(): raw = lax.all_to_all(routed, ('frames', 'tiles'), 0, 0, tiled=True)  5.69 us
    all_to_all x1, waiting for transfers between devices, body(): raw = lax.all_to_all(routed, ('frames', 'tiles'), 0, 0, tiled=True)  4.95 us
    pallas_call x1, Pallas kernels, body(): pl.pallas_call(edge_kernel, out_shape=(message, message, jax.ShapeDtypeSt...  4.22 us
    ppermute x1, starting transfers between devices, body(): cross = lax.ppermute(cross, 'tiles', beside)  3.7 us
  transfers between devices with their start and end apart: 4, of which 3 were waited for; matrix products, arithmetic and copies ran while one was open for 9% of the time, Pallas kernels for 0%

profile of v2, /device:TPU:1, one launch (start us, length us, event | category | flops | bytes accessed | tf_op | source)
XLA Modules:
  0.0 94.9 jit_solution(9604284059479113871)
XLA Ops:
  0.0 0.7 copy-done.7
  0.7 0.7 copy-done.10
  1.3 4.2 %edges.1 = (bf16[2688,128]{1,0:T(8,128)(2,1)S(1)}, bf16[2688,128]{1,0:T(8,128)(2,1)S(1)}, s32[64]{0:T(128)S(1)}) custom-call(s32[128]{0:T(128)S(1)} %bitcast.15, s32[4,128]{1,0:T(4,128)S(1)} %copy-done.7, bf16[4,8,480,128]{3,2,1,0:T(8,128)(2,1)} %feat_ref.3), custom_call_target="tpu_custom_call" | custom-call | tf_op jit(solution)/shard_map/edges/pallas_call | solution.py:311
  5.6 1.6 %collective-permute-start = (bf16[2688,128]{1,0:T(8,128)(2,1)S(1)}, bf16[2688,128]{1,0:T(8,128)(2,1)S(1)}, u32[]{:S(2)}, u32[]{:S(2)}) collective-permute-start(bf16[2688,128]{1,0:T(8,128)(2,1)S(1)} %get-tuple-element.9), channel_id=1, source_target_pairs={{0,1},{1,0},{2,3},{3,2},{4,5},{5,4},{6,7},{7,6},{8,9},{9,8},{10,11... | collective-permute-start | bytes 2064392 | tf_op jit(solution)/shard_map/ppermute | solution.py:327
  7.2 3.7 %collective-permute-start.1 = (bf16[2688,128]{1,0:T(8,128)(2,1)S(1)}, bf16[2688,128]{1,0:T(8,128)(2,1)S(1)}, u32[]{:S(2)}, u32[]{:S(2)}) collective-permute-start(bf16[2688,128]{1,0:T(8,128)(2,1)S(1)} %get-tuple-element.10), channel_id=1, source_target_pairs={{1,2},{2,1},{3,4},{4,3},{5,6},{6,5},{7,8},{8,7},{9,10},{10,9},{11,... | collective-permute-start | bytes 2064392 | tf_op jit(solution)/shard_map/ppermute | solution.py:326
  10.9 0.0 collective-permute-done.pair_ref
  10.9 8.6 %collective-permute-done.1.cross_ref = bf16[2688,128]{1,0:T(8,128)(2,1)S(1)} collective-permute-done((bf16[2688,128]{1,0:T(8,128)(2,1)S(1)}, bf16[2688,128]{1,0:T(8,128)(2,1)S(1)}, u32[]{:S(2)}, u32[]{:S(2)}) %collective-permute-start.1) | collective-permute-done | bytes 688160 | tf_op jit(solution)/shard_map/ppermute | solution.py:326
  19.5 0.0 copy-done
  19.5 0.0 copy-done.8
  19.5 0.0 copy-done.9
  19.5 2.9 %windows.1 = bf16[32,192,128]{2,1,0:T(8,128)(2,1)} custom-call(s32[64]{0:T(128)S(1)} %get-tuple-element.8.ids_ref, s32[4,128]{1,0:T(4,128)S(1)} %copy-done.8, s32[4,128]{1,0:T(4,128)S(1)} %copy-done.9, bf16[4,8,480,128]{3,2,1,0:T(8,128)(2,1)S(1)} %copy-done, bf16[2688,128]{1,0:T(8,128)(2,1)S(1)} %collective-permute-done.pair_ref, ...), custom_call_target="tpu_custom_call" | custom-call | tf_op jit(solution)/shard_map/windows/pallas_call | solution.py:328
  22.5 10.3 %all-to-all-start = ((bf16[32,192,128]{2,1,0:T(8,128)(2,1)}), bf16[32,192,128]{2,1,0:T(8,128)(2,1)S(1)}, u32[]{:S(2)}, u32[]{:S(2)}) async-start(bf16[32,192,128]{2,1,0:T(8,128)(2,1)} %windows.1), calls=%async_computation | async-start | bytes 3145728 | tf_op jit(solution)/shard_map/all_to_all | solution.py:342
  32.8 0.0 copy-done.11
  32.8 0.2 convert_reduce_fusion
  33.0 22.5 %all-to-all-done = bf16[32,192,128]{2,1,0:T(8,128)(2,1)S(1)} async-done(((bf16[32,192,128]{2,1,0:T(8,128)(2,1)}), bf16[32,192,128]{2,1,0:T(8,128)(2,1)S(1)}, u32[]{:S(2)}, u32[]{:S(2)}) %all-to-all-start) | async-done | bytes 1572896 | tf_op jit(solution)/shard_map/all_to_all | solution.py:342
  55.5 1.5 %route.1 = bf16[128,16,128]{2,1,0:T(8,128)(2,1)} custom-call(s32[128]{0:T(128)S(1)} %multiply_add_fusion.index_ref, bf16[384,16,128]{2,1,0:T(8,128)(2,1)S(1)} %bitcast.10), custom_call_target="tpu_custom_call" | custom-call | tf_op jit(solution)/shard_map/route/pallas_call | solution.py:343
  57.0 5.7 %all-to-all-start.1 = ((bf16[128,16,128]{2,1,0:T(8,128)(2,1)}), bf16[128,16,128]{2,1,0:T(8,128)(2,1)S(1)}, u32[]{:S(2)}, u32[]{:S(2)}) async-start(bf16[128,16,128]{2,1,0:T(8,128)(2,1)} %route.1), calls=%async_computation.1 | async-start | bytes 1048576 | tf_op jit(solution)/shard_map/all_to_all | solution.py:351
  62.7 0.0 copy-done.12
  62.7 0.8 fusion.1
  63.5 0.2 copy.29
  63.7 0.0 copy-start.15
  63.8 0.0 copy-start.13
  63.8 0.0 copy-start.14
  63.8 0.0 copy-start.1
  63.8 0.0 copy-start.2
  63.8 0.0 copy-start.3
  63.8 0.0 copy-start.4
  63.8 0.0 copy-start.5
  63.8 0.0 copy-start.6
  63.9 0.2 copy.28.wk_ref
  64.1 0.2 copy.30
  64.3 1.3 %copy.31 = bf16[384,384]{0,1:T(8,128)(2,1)S(1)} copy(bf16[384,384]{1,0:T(8,128)(2,1)} %get-tuple-element.11) | data formatting | bytes 589824
  65.6 1.6 %reshape.41 = bf16[9,9,384]{2,1,0:T(8,128)(2,1)} reshape(bf16[81,384]{1,0:T(8,128)(2,1)} %param.23) | data formatting | bytes 124416 | tf_op jit(solution)/shard_map/reshape | solution.py:357
  67.1 0.9 pad.12
  68.0 0.7 reshape.42
  68.7 0.9 pad.13.wcorr_ref
  69.6 0.0 copy-done.15
  69.6 0.1 broadcast_in_dim.9
  69.7 0.7 broadcast_in_dim.10
  70.4 0.9 broadcast_in_dim.12.start_ref
  71.4 0.0 copy-done.13
  71.4 0.0 copy-done.14
  71.4 4.9 %all-to-all-done.1 = bf16[128,16,128]{2,1,0:T(8,128)(2,1)S(1)} async-done(((bf16[128,16,128]{2,1,0:T(8,128)(2,1)}), bf16[128,16,128]{2,1,0:T(8,128)(2,1)S(1)}, u32[]{:S(2)}, u32[]{:S(2)}) %all-to-all-start.1) | async-done | bytes 524320 | tf_op jit(solution)/shard_map/all_to_all | solution.py:351
  76.3 0.0 copy-done.1
  76.3 0.0 copy-done.2
  76.3 0.0 copy-done.3
  76.4 0.0 copy-done.4
  76.4 18.4 %refine.1 = bf16[2048,384]{1,0:T(8,128)(2,1)} custom-call(bf16[2048,128]{1,0:T(8,128)(2,1)S(1)} %bitcast.11, bf16[1152,128]{1,0:T(8,128)(2,1)S(1)} %bitcast.14, bf16[128,128]{1,0:T(8,128)(2,1)S(1)} %copy-done.5, bf16[128,384]{1,0:T(8,128)(2,1)S(1)} %pad.13.wcorr_ref, bf16[128,384]{1,0:T(8,128)(2,1)S(1)} %copy-done.4, f32[16,384]{1,0:T(8,128)S(1)} %copy-done.6, ...), custom_call_target="tpu_custom_call" | custom-call | tf_op jit(solution)/shard_map/refine/pallas_call | solution.py:276
  (13 shorter events, 0.1 us)
Async XLA Ops:
  0.0 0.7 copy-start.7
  0.7 0.7 copy-start.10
  1.3 18.2 %copy-start = (bf16[4,8,480,128]{3,2,1,0:T(8,128)(2,1)S(1)}, bf16[4,8,480,128]{3,2,1,0:T(8,128)(2,1)}, u32[]{:S(2)}) copy-start(bf16[4,8,480,128]{3,2,1,0:T(8,128)(2,1)} %feat_ref.3) | copy-start | bytes 11796484
  1.3 18.2 %copy-start.8 = (s32[4,128]{1,0:T(4,128)S(1)}, s32[4,128]{1,0:T(4,128)}, u32[]{:S(2)}) copy-start(s32[4,128]{1,0:T(4,128)} %cols_ref.3) | copy-start | bytes 6148
  1.3 18.2 %copy-start.9 = (s32[4,128]{1,0:T(4,128)S(1)}, s32[4,128]{1,0:T(4,128)}, u32[]{:S(2)}) copy-start(s32[4,128]{1,0:T(4,128)} %offs_ref.1) | copy-start | bytes 6148
  5.6 5.3 %collective-permute-start = (bf16[2688,128]{1,0:T(8,128)(2,1)S(1)}, bf16[2688,128]{1,0:T(8,128)(2,1)S(1)}, u32[]{:S(2)}, u32[]{:S(2)}) collective-permute-start(bf16[2688,128]{1,0:T(8,128)(2,1)S(1)} %get-tuple-element.9), channel_id=1, source_target_pairs={{0,1},{1,0},{2,3},{3,2},{4,5},{5,4},{6,7},{7,6},{8,9},{9,8},{10,11... | collective-permute-start | bytes 2064392 | tf_op jit(solution)/shard_map/ppermute | solution.py:327
  7.2 12.3 %collective-permute-start.1 = (bf16[2688,128]{1,0:T(8,128)(2,1)S(1)}, bf16[2688,128]{1,0:T(8,128)(2,1)S(1)}, u32[]{:S(2)}, u32[]{:S(2)}) collective-permute-start(bf16[2688,128]{1,0:T(8,128)(2,1)S(1)} %get-tuple-element.10), channel_id=1, source_target_pairs={{1,2},{2,1},{3,4},{4,3},{5,6},{6,5},{7,8},{8,7},{9,10},{10,9},{11,... | collective-permute-start | bytes 2064392 | tf_op jit(solution)/shard_map/ppermute | solution.py:326
  22.5 10.3 %copy-start.11 = (s32[128,1]{0,1:T(1,128)S(1)}, s32[128,1]{0,1:T(1,128)}, u32[]{:S(2)}) copy-start(s32[128,1]{0,1:T(1,128)} %param.21) | copy-start | bytes 1540
  22.5 33.0 %all-to-all-start = ((bf16[32,192,128]{2,1,0:T(8,128)(2,1)}), bf16[32,192,128]{2,1,0:T(8,128)(2,1)S(1)}, u32[]{:S(2)}, u32[]{:S(2)}) async-start(bf16[32,192,128]{2,1,0:T(8,128)(2,1)} %windows.1), calls=%async_computation | async-start | bytes 3145728 | tf_op jit(solution)/shard_map/all_to_all | solution.py:342
  55.5 7.2 %copy-start.12 = (bf16[384,1152]{1,0:T(8,128)(2,1)S(1)}, bf16[384,1152]{1,0:T(8,128)(2,1)}, u32[]{:S(2)}) copy-start(bf16[384,1152]{1,0:T(8,128)(2,1)} %param.27) | copy-start | bytes 2654212
  57.0 19.4 %all-to-all-start.1 = ((bf16[128,16,128]{2,1,0:T(8,128)(2,1)}), bf16[128,16,128]{2,1,0:T(8,128)(2,1)S(1)}, u32[]{:S(2)}, u32[]{:S(2)}) async-start(bf16[128,16,128]{2,1,0:T(8,128)(2,1)} %route.1), calls=%async_computation.1 | async-start | bytes 1048576 | tf_op jit(solution)/shard_map/all_to_all | solution.py:351
  63.7 5.9 %copy-start.15 = (s32[128]{0:T(128)S(1)}, s32[128]{0:T(128)}, u32[]{:S(2)}) copy-start(s32[128]{0:T(128)} %param.22) | copy-start | bytes 1540
  63.8 7.6 %copy-start.13 = (f32[384]{0:T(512)S(1)}, f32[384]{0:T(512)}, u32[]{:S(2)}) copy-start(f32[384]{0:T(512)} %param.26) | copy-start | bytes 4612
  63.8 7.6 %copy-start.14 = (f32[384]{0:T(512)S(1)}, f32[384]{0:T(512)}, u32[]{:S(2)}) copy-start(f32[384]{0:T(512)} %param.29) | copy-start | bytes 4612
  63.8 12.6 %copy-start.1 = (bf16[384,1536]{1,0:T(8,128)(2,1)S(1)}, bf16[384,1536]{1,0:T(8,128)(2,1)}, u32[]{:S(2)}) copy-start(bf16[384,1536]{1,0:T(8,128)(2,1)} %wup_ref.1) | copy-start | bytes 3538948
  63.8 12.6 %copy-start.2 = (bf16[3,3,128,128]{3,2,1,0:T(8,128)(2,1)S(1)}, bf16[3,3,128,128]{3,2,1,0:T(8,128)(2,1)}, u32[]{:S(2)}) copy-start(bf16[3,3,128,128]{3,2,1,0:T(8,128)(2,1)} %param.17) | copy-start | bytes 884740
  63.8 12.5 %copy-start.3 = (bf16[384,384]{1,0:T(8,128)(2,1)S(1)}, bf16[384,384]{1,0:T(8,128)(2,1)}, u32[]{:S(2)}) copy-start(bf16[384,384]{1,0:T(8,128)(2,1)} %wout_ref.1) | copy-start | bytes 884740
  63.8 12.5 %copy-start.4 = (bf16[128,384]{1,0:T(8,128)(2,1)S(1)}, bf16[128,384]{1,0:T(8,128)(2,1)}, u32[]{:S(2)}) copy-start(bf16[128,384]{1,0:T(8,128)(2,1)} %wfeat_ref.1) | copy-start | bytes 294916
  63.8 12.5 %copy-start.5 = (bf16[128,128]{1,0:T(8,128)(2,1)S(1)}, bf16[128,128]{1,0:T(8,128)(2,1)}, u32[]{:S(2)}) copy-start(bf16[128,128]{1,0:T(8,128)(2,1)} %query_ref.1) | copy-start | bytes 98308
  63.8 12.5 %copy-start.6 = (f32[16,384]{1,0:T(8,128)S(1)}, f32[16,384]{1,0:T(8,128)}, u32[]{:S(2)}) copy-start(f32[16,384]{1,0:T(8,128)} %time_ref.1) | copy-start | bytes 73732

commit v3 on v2

--- a/solution.py
+++ b/solution.py
@@ -11,15 +11,18 @@
 HEAD = 48
 WIN = 9
 RAW = WIN + 2
-CELLS = RAW * RAW
 QBLK = 128
 CAP = 12
 TILE = 8
 EDGE = 5
-MSG = 56
+CLASSES = 8
 PIECES = 32
 PROWS = 16
-SLOT = PIECES * PROWS
+OWN = 11
+SIDE = 7
+LOW = CAP * OWN
+HIGH = LOW + CAP * SIDE
+SENT = 304
 CHUNK = 1024
 BATCH = 4
 F32 = jnp.float32
@@ -36,11 +39,18 @@
         dst_ref[base + RAW * i : base + RAW * i + 16, :] = tmp_ref[i, pl.ds(8 + shift, 16), :]
 
 
-def edge_kernel(
-    owners_ref, cols_ref, feat_ref, pair_ref, cross_ref, ids_ref, buf_ref, tmp_ref, win_ref, sems
+def first_of(cell, which):
+    return (cell - which + CLASSES - 1) >> 3
+
+
+def send_kernel(
+    owners_ref, cols_ref, offs_ref, feat_ref, out_ref, here_ref, ids_ref, tmp_ref, flat_ref, piece_ref, sems
 ):
     frames, rows, wide, _ = feat_ref.shape
     tile = lax.axis_index("tiles")
+    copies = [pltpu.make_async_copy(feat_ref.at[k], here_ref.at[k], sems.at[k]) for k in range(frames)]
+    for copy in copies:
+        copy.start()
 
     def scan(b, counts):
         near = owners_ref[b] - tile + 1
@@ -50,90 +60,76 @@
 
     zero = jnp.int32(0)
     counts = lax.fori_loop(0, owners_ref.shape[0], scan, (zero, zero, zero), unroll=8)
-    for d in range(3):
-        ids_ref[48 + d] = counts[d]
-    odd = tile & 1
-    parts = []
-    for w, after in ((0, odd), (1, 1 - odd)):
-        first = jnp.where(after == 1, rows - EDGE, 0)
-        parts.append((w, 32 * after, ids_ref[48 + 2 * after], first))
-
-    def copy(w, s, k, first, block):
-        start = aligned(cols_ref[k, block] - 1, wide)
-        return pltpu.make_async_copy(
-            feat_ref.at[k, pl.ds(first, EDGE), pl.ds(start, 32), :], buf_ref.at[w, s, k], sems.at[w, s, k]
-        )
-
-    for w, at, count, first in parts:
-
-        def begin(s, carry):
-            for k in range(frames):
-                copy(w, s, k, first, ids_ref[at + s]).start()
-            return carry
-
-        lax.fori_loop(0, count, begin, 0)
     tmp_ref[...] = jnp.zeros_like(tmp_ref)
-    win_ref[...] = jnp.zeros_like(win_ref)
-    for w, at, count, first in parts:
-        out_ref = (cross_ref, pair_ref)[w]
-
-        def slot(s, carry):
-            block = ids_ref[at + s]
-            for k in range(frames):
-                copy(w, s, k, first, block).wait()
-                col = cols_ref[k, block] - 1
-                window_rows(buf_ref[w, s, k], EDGE, col - aligned(col, wide), tmp_ref, win_ref, k * MSG)
-            out_ref[pl.ds(pl.multiple_of(s * frames * MSG, 16), frames * MSG), :] = win_ref[
-                0 : frames * MSG, :
-            ].astype(BF16)
-            return carry
-
-        lax.fori_loop(0, count, slot, 0)
-
-
-def merge_kernel(
-    ids_ref, cols_ref, offs_ref, feat_ref, pair_ref, cross_ref, out_ref, tmp_ref, side_ref, win_ref, all_ref
-):
-    frames, rows, wide, _ = feat_ref.shape
-    tile = lax.axis_index("tiles")
-    odd = tile & 1
-    tmp_ref[...] = jnp.zeros_like(tmp_ref)
-    win_ref[...] = jnp.zeros_like(win_ref)
-
-    def slot(s, carry):
-        block = ids_ref[16 + s]
-        here = pl.ds(pl.multiple_of(s * frames * MSG, 16), frames * MSG)
-        side_ref[odd] = cross_ref[here, :].astype(F32)
-        side_ref[1 - odd] = pair_ref[here, :].astype(F32)
-        own = EDGE * RAW
-        for k in range(frames):
-            row, col = offs_ref[k, block], cols_ref[k, block] - 1
-            win_ref[0:MSG, :] = side_ref[0, k * MSG : (k + 1) * MSG, :]
-            start = aligned(col, wide)
-            window_rows(feat_ref[k, :, pl.ds(start, 32), :], rows, col - start, tmp_ref, win_ref, own)
-            top = own + rows * RAW
-            win_ref[top : top + MSG, :] = side_ref[1, k * MSG : (k + 1) * MSG, :]
-            all_ref[k * CELLS : k * CELLS + 128, :] = win_ref[pl.ds(row * RAW, 128), :]
-        end = frames * CELLS
-        all_ref[end:SLOT, :] = jnp.zeros((SLOT - end, 128), F32)
-        for k in range(frames):
-            first = (tile * rows + offs_ref[k, block] - WIN // 2).astype(F32)
-            all_ref[end + k : end + k + 1, :] = jnp.full((1, 128), first, F32)
-        for i in range(PIECES):
-            out_ref[i, pl.ds(pl.multiple_of(s * PROWS, 16), PROWS), :] = all_ref[
-                i * PROWS : (i + 1) * PROWS, :
-            ].astype(BF16)
+    flat_ref[...] = jnp.zeros_like(flat_ref)
+    for k in range(frames):
+        copies[k].wait()
+
+        def part(d, row0, count, place, room, k=k):
+            def slot(s, carry):
+                block = ids_ref[16 * d + s]
+                row, col = offs_ref[k, block], cols_ref[k, block] - 1
+                start = aligned(col, wide)
+                window_rows(
+                    here_ref[k, row0 : row0 + count, pl.ds(start, 32), :], count, col - start, tmp_ref, flat_ref, 16
+                )
+                at = RAW * (EDGE - row + row0 + (rows, 0, -rows)[d])
+                low = jnp.maximum(at, 0)
+                for c in range(CLASSES):
+                    source = 16 + CLASSES * first_of(low, c) + c - at
+                    target = (k * CLASSES + c) * SENT + place + s * room
+                    length = 16 if d == 1 else 8
+                    piece_ref[pl.ds(target, length), :] = flat_ref[pl.ds(source, length, stride=CLASSES), :]
+                return carry
+
+            lax.fori_loop(0, counts[d], slot, 0)
+
+        part(1, 0, rows, 0, OWN)
+        part(2, rows - EDGE, EDGE, LOW, SIDE)
+        part(0, 0, EDGE, HIGH, SIDE)
+
+    def narrow(i, carry):
+        out_ref[i] = piece_ref[pl.ds(pl.multiple_of(i * SENT, 16), SENT), :].astype(BF16)
         return carry
 
-    lax.fori_loop(0, ids_ref[49], slot, 0)
-
-
-def route_kernel(index_ref, in_ref, out_ref):
-    def step(b, carry):
-        out_ref[b] = in_ref[index_ref[b]]
+    lax.fori_loop(0, PIECES, narrow, 0)
+
+
+def route_kernel(height, owner_ref, rank_ref, offs_ref, in_ref, out_ref, wide_ref, join_ref):
+    tiles = in_ref.shape[0]
+    rows = height // tiles
+    piece = lax.axis_index("tiles")
+    frame, which = piece >> 3, piece & 7
+
+    def widen(i, carry):
+        wide_ref[pl.ds(pl.multiple_of(i * SENT, 16), SENT), :] = in_ref[i].astype(F32)
         return carry
 
-    lax.fori_loop(0, out_ref.shape[0], step, 0, unroll=16)
+    lax.fori_loop(0, tiles, widen, 0)
+    none = tiles * SENT
+    wide_ref[none:, :] = jnp.zeros_like(wide_ref[none:, :])
+    last = jnp.where(which > 0, PROWS - 1, 24)
+
+    def gather(b, carry):
+        owner, slot, row = owner_ref[b], rank_ref[b], offs_ref[frame, b]
+        before = jnp.where(owner > 0, (owner - 1) * SENT + LOW + slot * SIDE, none)
+        after = jnp.where(owner < tiles - 1, (owner + 1) * SENT + HIGH + slot * SIDE, none)
+        own = first_of(RAW * jnp.maximum(EDGE - row, 0), which)
+        over = first_of(RAW * (EDGE + rows - row), which)
+        join_ref[b, 0:8, :] = wide_ref[pl.ds(before, 8), :]
+        join_ref[b, pl.ds(own, 16), :] = wide_ref[pl.ds(owner * SENT + slot * OWN, 16), :]
+        join_ref[b, pl.ds(over, 8), :] = wide_ref[pl.ds(after, 8), :]
+        top = (owner * rows + row - WIN // 2).astype(F32)
+        join_ref[b, pl.ds(last, 1), :] = jnp.full((1, 128), top, F32)
+        return carry
+
+    lax.fori_loop(0, out_ref.shape[0], gather, 0, unroll=4)
+
+    def narrow(b, carry):
+        out_ref[b] = join_ref[b, 0:PROWS, :].astype(BF16)
+        return carry
+
+    lax.fori_loop(0, out_ref.shape[0], narrow, 0, unroll=8)
 
 
 def nt(a, b):
@@ -149,31 +145,32 @@
     wk_ref, wq_ref, wv_ref, wout_ref, gain2_ref, wup_ref, wdown_ref, out_ref,
     cells_ref, cols_ref, tok_ref, down_ref, sem,
 ):
-    groups, per = raw_ref.shape[0] // SLOT, 4
-    frames = groups * per
+    frames = raw_ref.shape[0] // 128
     step = pl.program_id(0)
 
     @pl.when(step == 0)
     def _():
         fetch = pltpu.make_async_copy(wdown_ref, down_ref, sem)
         fetch.start()
-        cells_ref[0 : groups * SLOT, :] = raw_ref[...].astype(F32)
-        cells_ref[groups * SLOT :, :] = jnp.zeros_like(cells_ref[groups * SLOT :, :])
+        for f in range(frames):
+            for c in range(CLASSES):
+                at = (f * CLASSES + c) * PROWS
+                cells_ref[pl.ds(f * 128 + c, PROWS, stride=CLASSES), :] = raw_ref[at : at + PROWS, :].astype(F32)
+        cells_ref[frames * 128 :, :] = jnp.zeros_like(cells_ref[frames * 128 :, :])
         line = lax.broadcasted_iota(jnp.int32, (128, 128), 0) // RAW
         line = line.astype(F32)
         feat = jnp.dot(query_ref[...], wfeat_ref[...], preferred_element_type=F32)
         for f in range(frames):
-            base = (f // per) * SLOT + (f % per) * CELLS
             for a in range(3):
                 for b in range(3):
-                    at = base + a * RAW + b
+                    at = f * 128 + a * RAW + b
                     cols_ref[f * 128 : (f + 1) * 128, (a * 3 + b) * 128 : (a * 3 + b + 1) * 128] = (
                         cells_ref[at : at + 128, :].astype(BF16)
                     )
         conv = jnp.dot(cols_ref[...], wconv_ref[...], preferred_element_type=F32)
         corr = []
         for f in range(frames):
-            info = (f // per) * SLOT + per * CELLS + f % per
+            info = f * 128 + 127
             row = line + cells_ref[info : info + 1, :]
             inside = (row >= 0) & (row < height)
             here = jnp.where(inside, conv[f * 128 : (f + 1) * 128], 0.0).astype(BF16)
@@ -280,7 +277,7 @@
         in_specs=[VMEM] * 6 + [step] + [VMEM] * (len(rest) - 7) + [HBM],
         out_specs=pl.BlockSpec((CHUNK, dim), lambda i: (i, 0)),
         scratch_shapes=[
-            pltpu.VMEM((raw.shape[0] + 16, 128), F32),
+            pltpu.VMEM((raw.shape[0] + 32, 128), F32),
             pltpu.VMEM((tokens, 9 * chans), BF16),
             pltpu.VMEM((3, tokens, 128), F32),
             pltpu.VMEM(rest[-1].shape, BF16),
@@ -307,47 +304,35 @@
     rank = jnp.sum(
         (owner[:, None] == owner[None, :]) & (number[None, :] < number[:, None]), axis=1, dtype=jnp.int32
     )
-    message = jax.ShapeDtypeStruct((CAP * frames * MSG, chans), BF16)
-    pair, cross, ids = pl.pallas_call(
-        edge_kernel,
-        out_shape=(message, message, jax.ShapeDtypeStruct((64,), jnp.int32)),
-        in_specs=[SMEM, SMEM, HBM],
-        out_specs=(VMEM, VMEM, SMEM),
-        scratch_shapes=[
-            pltpu.VMEM((2, CAP, frames, EDGE, 32, chans), BF16),
-            pltpu.VMEM((TILE, 48, 128), F32),
-            pltpu.VMEM((frames * MSG + 16, 128), F32),
-            pltpu.SemaphoreType.DMA((2, CAP, frames)),
-        ],
-        compiler_params=params(24),
-        name="edges",
-    )(owner, offset_cols, pltpu.with_memory_space_constraint(features, pltpu.HBM))
-    beside = [(i, ((i - 1) ^ 1) + 1) for i in range(1, n_tiles - 1)]
-    cross = lax.ppermute(cross, "tiles", beside)
-    pair = lax.ppermute(pair, "tiles", [(i, i ^ 1) for i in range(n_tiles)])
     pieces = pl.pallas_call(
-        merge_kernel,
-        out_shape=jax.ShapeDtypeStruct((PIECES, CAP * PROWS, chans), BF16),
-        in_specs=[SMEM, SMEM, SMEM, VMEM, VMEM, VMEM],
+        send_kernel,
+        out_shape=jax.ShapeDtypeStruct((PIECES, SENT, chans), BF16),
+        in_specs=[SMEM, SMEM, SMEM, HBM],
         out_specs=VMEM,
         scratch_shapes=[
+            pltpu.VMEM(features.shape, BF16),
+            pltpu.SMEM((64,), jnp.int32),
             pltpu.VMEM((TILE, 48, 128), F32),
-            pltpu.VMEM((2, frames * MSG, 128), F32),
-            pltpu.VMEM((208, 128), F32),
-            pltpu.VMEM((SLOT, 128), F32),
+            pltpu.VMEM((192, 128), F32),
+            pltpu.VMEM((PIECES * SENT, 128), F32),
+            pltpu.SemaphoreType.DMA((frames,)),
         ],
-        compiler_params=params(24),
+        compiler_params=params(32),
         name="windows",
-    )(ids, offset_cols, offset_rows, features, pair, cross)
+    )(owner, offset_cols, offset_rows, pltpu.with_memory_space_constraint(features, pltpu.HBM))
     spread = lax.all_to_all(pieces, "tiles", 0, 0, tiled=True)
     routed = pl.pallas_call(
-        route_kernel,
+        functools.partial(route_kernel, n_tiles * rows),
         out_shape=jax.ShapeDtypeStruct((blocks, PROWS, chans), BF16),
-        in_specs=[SMEM, VMEM],
+        in_specs=[SMEM, SMEM, SMEM, VMEM],
         out_specs=VMEM,
-        compiler_params=params(24),
+        scratch_shapes=[
+            pltpu.VMEM((n_tiles * SENT + 16, 128), F32),
+            pltpu.VMEM((blocks, 32, 128), F32),
+        ],
+        compiler_params=params(32),
         name="route",
-    )(owner * CAP + rank, spread.reshape(n_tiles * CAP, PROWS, chans))
+    )(owner, rank, offset_rows, spread)
     raw = lax.all_to_all(routed, ("frames", "tiles"), 0, 0, tiled=True)
     raw = raw.reshape(blocks * PROWS, chans)
 

time: 95 us -> 92.7 us (0.976)
  starting transfers between devices: 21.3 us -> 16.5 us
  local copies, waits for them, and re-layouts: 9.93 us -> 14.7 us
  waiting for transfers between devices: 36 us -> 34.6 us
  Pallas kernels: 27.1 us -> 26 us
    all_to_all x1, waiting for transfers between devices: 22.5 us -> 32.3 us  [body(): spread = lax.all_to_all(pieces, 'tiles', 0, 0, tiled=True)]
    ppermute x2 -> x0, waiting for transfers between devices: 8.6 us -> none  [the longest x1 8.6 us: body(): cross = lax.ppermute(cross, 'tiles', beside)]
    ppermute x2 -> x0, starting transfers between devices: 5.33 us -> none  [the longest x1 3.7 us: body(): cross = lax.ppermute(cross, 'tiles', beside)]
    unnamed x35 -> x33, local copies, waits for them, and re-layouts: 3.12 us -> 5.82 us
    all_to_all x1, waiting for transfers between devices: 4.95 us -> 2.31 us  [body(): raw = lax.all_to_all(routed, ('frames', 'tiles'), 0, 0, tiled=True)]
    slice x1, local copies, waits for them, and re-layouts: 0.8 us -> 1.95 us  [body(): wq, wv = (w_qkv[:, :dim].T, w_qkv[:, 2 * dim:].T)]
    pad x1, local copies, waits for them, and re-layouts: 0.04 us -> 1 us  [body(): jnp.pad(w_qkv[:, dim:2 * dim].reshape(dim, HEADS, HEAD), ((0, 0), (0, 0),...]
    pallas_call x3 -> x2, Pallas kernels: 8.68 us -> 7.77 us  [the longest x1 3.9 us: body(): pl.pallas_call(functools.partial(route_kernel, n_tiles * rows), out_shape...]
  transfers between devices with their start and end apart: 4 -> 2, of which waited for: 3 -> 2; matrix products, arithmetic and copies ran while one was open for 9% -> 12% of each run, Pallas kernels for 0% -> 0%
where the time goes in v3:
time: 92.7 us; the launch traced here: 92.3 us
  waiting for transfers between devices  34.6 us (37%)
  Pallas kernels  26 us (28%)
  starting transfers between devices  16.5 us (18%)
  local copies, waits for them, and re-layouts  14.7 us (16%)
    all_to_all x1, waiting for transfers between devices, body(): spread = lax.all_to_all(pieces, 'tiles', 0, 0, tiled=True)  32.3 us
    pallas_call x1, Pallas kernels, refine_call(): pl.pallas_call(functools.partial(refine_kernel, height), grid=(tokens //...  18.3 us
    all_to_all x1, starting transfers between devices, body(): spread = lax.all_to_all(pieces, 'tiles', 0, 0, tiled=True)  10.6 us
    all_to_all x1, starting transfers between devices, body(): raw = lax.all_to_all(routed, ('frames', 'tiles'), 0, 0, tiled=True)  5.93 us
    unnamed x33, local copies, waits for them, and re-layouts  5.82 us
    pallas_call x1, Pallas kernels, body(): pl.pallas_call(functools.partial(route_kernel, n_tiles * rows), out_shape...  3.9 us
    pallas_call x1, Pallas kernels, body(): pl.pallas_call(send_kernel, out_shape=jax.ShapeDtypeStruct((PIECES, SENT,...  3.87 us
    all_to_all x1, waiting for transfers between devices, body(): raw = lax.all_to_all(routed, ('frames', 'tiles'), 0, 0, tiled=True)  2.31 us
  transfers between devices with their start and end apart: 2, of which 2 were waited for; matrix products, arithmetic and copies ran while one was open for 12% of the time, Pallas kernels for 0%

profile of v3, /device:TPU:1, one launch (start us, length us, event | category | flops | bytes accessed | tf_op | source)
XLA Modules:
  0.0 92.3 jit_solution(15787505969266561114)
XLA Ops:
  0.0 0.0 copy-start.7
  0.0 0.7 copy-done.7
  0.7 0.0 copy-start.9
  0.7 0.7 copy-done.9
  1.4 0.7 copy-done.10
  2.0 3.9 %windows.1 = bf16[32,304,128]{2,1,0:T(8,128)(2,1)S(1)} custom-call(s32[128]{0:T(128)S(1)} %bitcast.12, s32[4,128]{1,0:T(4,128)S(1)} %copy-done.9, s32[4,128]{1,0:T(4,128)S(1)} %copy-done.7, bf16[4,8,480,128]{3,2,1,0:T(8,128)(2,1)} %feat_ref.1), custom_call_target="tpu_custom_call" | custom-call | tf_op jit(solution)/shard_map/windows/pallas_call | solution.py:307
  5.9 0.0 copy-start
  5.9 1.5 %copy-done = bf16[32,304,128]{2,1,0:T(8,128)(2,1)} copy-done((bf16[32,304,128]{2,1,0:T(8,128)(2,1)}, bf16[32,304,128]{2,1,0:T(8,128)(2,1)S(1)}, u32[]{:S(2)}) %copy-start) | copy-done | bytes 2490392
  7.4 0.0 copy-start.11
  7.4 0.0 copy-start.8
  7.4 10.6 %all-to-all-start = ((bf16[32,304,128]{2,1,0:T(8,128)(2,1)}), bf16[32,304,128]{2,1,0:T(8,128)(2,1)S(1)}, u32[]{:S(2)}, u32[]{:S(2)}) async-start(bf16[32,304,128]{2,1,0:T(8,128)(2,1)} %copy-done), calls=%async_computation | async-start | bytes 4980736 | tf_op jit(solution)/shard_map/all_to_all | solution.py:323
  18.0 0.0 copy-done.11
  18.0 0.2 convert_reduce_fusion.rank_ref
  18.1 32.3 %all-to-all-done.in_ref = bf16[32,304,128]{2,1,0:T(8,128)(2,1)S(1)} async-done(((bf16[32,304,128]{2,1,0:T(8,128)(2,1)}), bf16[32,304,128]{2,1,0:T(8,128)(2,1)S(1)}, u32[]{:S(2)}, u32[]{:S(2)}) %all-to-all-start) | async-done | bytes 2490400 | tf_op jit(solution)/shard_map/all_to_all | solution.py:323
  50.5 0.0 copy-done.8
  50.5 3.9 %route.1 = bf16[128,16,128]{2,1,0:T(8,128)(2,1)} custom-call(s32[128]{0:T(128)S(1)} %bitcast.14, s32[128]{0:T(128)S(1)} %convert_reduce_fusion.rank_ref, s32[4,128]{1,0:T(4,128)S(1)} %copy-done.8, bf16[32,304,128]{2,1,0:T(8,128)(2,1)S(1)} %all-to-all-done.in_ref), custom_call_target="tpu_custom_call" | custom-call | tf_op jit(solution)/shard_map/route/pallas_call | solution.py:324
  54.4 5.9 %all-to-all-start.1 = ((bf16[128,16,128]{2,1,0:T(8,128)(2,1)}), bf16[128,16,128]{2,1,0:T(8,128)(2,1)S(1)}, u32[]{:S(2)}, u32[]{:S(2)}) async-start(bf16[128,16,128]{2,1,0:T(8,128)(2,1)} %route.1), calls=%async_computation.1 | async-start | bytes 1048576 | tf_op jit(solution)/shard_map/all_to_all | solution.py:336
  60.3 0.0 copy-start.14
  60.3 1.9 %fusion.1 = (bf16[384,384]{1,0:T(8,128)(2,1)}, bf16[384,384]{1,0:T(8,128)(2,1)S(1)}, bf16[384,384]{1,0:T(8,128)(2,1)S(1)}) fusion(bf16[384,1152]{1,0:T(8,128)(2,1)} %param.27), kind=kLoop, calls=%fused_computation.3 | loop fusion | bytes 1769472 | tf_op jit(solution)/shard_map/slice | solution.py:341
  62.3 0.0 copy-start.12
  62.3 0.0 copy-start.13
  62.3 0.0 copy-start.3
  62.3 0.0 copy-start.4
  62.3 0.0 copy-start.5
  62.3 0.0 copy-start.6
  62.3 0.9 copy.29
  63.2 1.0 %pad.14 = bf16[384,8,64]{0,2,1:T(8,128)(2,1)S(1)} pad(bf16[384,8,48]{0,2,1:T(8,128)(2,1)} %bitcast.16, bf16[]{:T(256)} %constant.3.clone.1), padding=0_0x0_0x0_16 | pad | bytes 688130 | tf_op jit(solution)/shard_map/jit(_pad)/pad | solution.py:339
  64.2 0.2 copy.28.wk_ref
  64.4 0.2 copy.30
  64.7 1.2 %copy.31 = bf16[384,384]{0,1:T(8,128)(2,1)S(1)} copy(bf16[384,384]{1,0:T(8,128)(2,1)} %get-tuple-element.5) | data formatting | bytes 589824
  65.8 1.6 %reshape.37 = bf16[9,9,384]{2,1,0:T(8,128)(2,1)} reshape(bf16[81,384]{1,0:T(8,128)(2,1)} %param.23) | data formatting | bytes 124416 | tf_op jit(solution)/shard_map/reshape | solution.py:342
  67.4 0.9 pad.12
  68.3 0.7 reshape.38
  69.0 0.9 pad.13.wcorr_ref
  69.9 0.0 copy-done.14
  69.9 0.1 broadcast_in_dim.9
  70.0 0.7 broadcast_in_dim.10
  70.7 0.9 %broadcast_in_dim.12.start_ref = s32[2,1,1024]{2,1,0:T(1,128)S(1)} reshape(s32[2,64,16]{2,1,0:T(8,128)} %broadcast_in_dim.10) | data formatting | bytes 16384 | tf_op jit(solution)/shard_map/broadcast_in_dim | solution.py:345
  71.6 0.0 copy-done.12
  71.7 0.0 copy-done.13
  71.7 2.3 %all-to-all-done.1 = bf16[128,16,128]{2,1,0:T(8,128)(2,1)S(1)} async-done(((bf16[128,16,128]{2,1,0:T(8,128)(2,1)}), bf16[128,16,128]{2,1,0:T(8,128)(2,1)S(1)}, u32[]{:S(2)}, u32[]{:S(2)}) %all-to-all-start.1) | async-done | bytes 524320 | tf_op jit(solution)/shard_map/all_to_all | solution.py:336
  74.0 0.0 copy-done.1
  74.0 0.0 copy-done.2
  74.0 0.0 copy-done.3
  74.0 0.0 copy-done.4
  74.0 0.0 copy-done.5
  74.0 0.0 copy-done.6
  74.0 18.3 %refine.1 = bf16[2048,384]{1,0:T(8,128)(2,1)} custom-call(bf16[2048,128]{1,0:T(8,128)(2,1)S(1)} %bitcast.8, bf16[1152,128]{1,0:T(8,128)(2,1)S(1)} %bitcast.11, bf16[128,128]{1,0:T(8,128)(2,1)S(1)} %copy-done.5, bf16[128,384]{1,0:T(8,128)(2,1)S(1)} %pad.13.wcorr_ref, bf16[128,384]{1,0:T(8,128)(2,1)S(1)} %copy-done.4, f32[16,384]{1,0:T(8,128)S(1)} %copy-done.6, ...), custom_call_target="tpu_custom_call" | custom-call | tf_op jit(solution)/shard_map/refine/pallas_call | solution.py:273
  (5 shorter events, 0.0 us)
Async XLA Ops:
  0.0 0.7 copy-start.7
  0.7 0.7 copy-start.9
  1.4 0.7 copy-start.10
  5.9 1.5 %copy-start = (bf16[32,304,128]{2,1,0:T(8,128)(2,1)}, bf16[32,304,128]{2,1,0:T(8,128)(2,1)S(1)}, u32[]{:S(2)}) copy-start(bf16[32,304,128]{2,1,0:T(8,128)(2,1)S(1)} %windows.1) | copy-start | bytes 7471108
  7.4 10.6 %copy-start.11 = (s32[128,1]{0,1:T(1,128)S(1)}, s32[128,1]{0,1:T(1,128)}, u32[]{:S(2)}) copy-start(s32[128,1]{0,1:T(1,128)} %param.21) | copy-start | bytes 1540
  7.4 43.1 %copy-start.8 = (s32[4,128]{1,0:T(4,128)S(1)}, s32[4,128]{1,0:T(4,128)}, u32[]{:S(2)}) copy-start(s32[4,128]{1,0:T(4,128)} %offs_ref.3) | copy-start | bytes 6148
  7.4 43.1 %all-to-all-start = ((bf16[32,304,128]{2,1,0:T(8,128)(2,1)}), bf16[32,304,128]{2,1,0:T(8,128)(2,1)S(1)}, u32[]{:S(2)}, u32[]{:S(2)}) async-start(bf16[32,304,128]{2,1,0:T(8,128)(2,1)} %copy-done), calls=%async_computation | async-start | bytes 4980736 | tf_op jit(solution)/shard_map/all_to_all | solution.py:323
  54.4 19.6 %all-to-all-start.1 = ((bf16[128,16,128]{2,1,0:T(8,128)(2,1)}), bf16[128,16,128]{2,1,0:T(8,128)(2,1)S(1)}, u32[]{:S(2)}, u32[]{:S(2)}) async-start(bf16[128,16,128]{2,1,0:T(8,128)(2,1)} %route.1), calls=%async_computation.1 | async-start | bytes 1048576 | tf_op jit(solution)/shard_map/all_to_all | solution.py:336
  60.3 9.6 %copy-start.14 = (s32[128]{0:T(128)S(1)}, s32[128]{0:T(128)}, u32[]{:S(2)}) copy-start(s32[128]{0:T(128)} %param.22) | copy-start | bytes 1540
  62.3 9.4 %copy-start.12 = (f32[384]{0:T(512)S(1)}, f32[384]{0:T(512)}, u32[]{:S(2)}) copy-start(f32[384]{0:T(512)} %param.26) | copy-start | bytes 4612
  62.3 9.4 %copy-start.13 = (f32[384]{0:T(512)S(1)}, f32[384]{0:T(512)}, u32[]{:S(2)}) copy-start(f32[384]{0:T(512)} %param.29) | copy-start | bytes 4612
  62.3 11.7 %copy-start.1 = (bf16[384,1536]{1,0:T(8,128)(2,1)S(1)}, bf16[384,1536]{1,0:T(8,128)(2,1)}, u32[]{:S(2)}) copy-start(bf16[384,1536]{1,0:T(8,128)(2,1)} %wup_ref.1) | copy-start | bytes 3538948
  62.3 11.7 %copy-start.2 = (bf16[3,3,128,128]{3,2,1,0:T(8,128)(2,1)S(1)}, bf16[3,3,128,128]{3,2,1,0:T(8,128)(2,1)}, u32[]{:S(2)}) copy-start(bf16[3,3,128,128]{3,2,1,0:T(8,128)(2,1)} %param.17) | copy-start | bytes 884740
  62.3 11.7 %copy-start.3 = (bf16[384,384]{1,0:T(8,128)(2,1)S(1)}, bf16[384,384]{1,0:T(8,128)(2,1)}, u32[]{:S(2)}) copy-start(bf16[384,384]{1,0:T(8,128)(2,1)} %wout_ref.1) | copy-start | bytes 884740
  62.3 11.7 %copy-start.4 = (bf16[128,384]{1,0:T(8,128)(2,1)S(1)}, bf16[128,384]{1,0:T(8,128)(2,1)}, u32[]{:S(2)}) copy-start(bf16[128,384]{1,0:T(8,128)(2,1)} %wfeat_ref.1) | copy-start | bytes 294916
  62.3 11.7 %copy-start.5 = (bf16[128,128]{1,0:T(8,128)(2,1)S(1)}, bf16[128,128]{1,0:T(8,128)(2,1)}, u32[]{:S(2)}) copy-start(bf16[128,128]{1,0:T(8,128)(2,1)} %query_ref.1) | copy-start | bytes 98308
  62.3 11.7 %copy-start.6 = (f32[16,384]{1,0:T(8,128)S(1)}, f32[16,384]{1,0:T(8,128)}, u32[]{:S(2)}) copy-start(f32[16,384]{1,0:T(8,128)} %time_ref.1) | copy-start | bytes 73732

commit v4 on v3

--- a/solution.py
+++ b/solution.py
@@ -44,13 +44,27 @@
 
 
 def send_kernel(
-    owners_ref, cols_ref, offs_ref, feat_ref, out_ref, here_ref, ids_ref, tmp_ref, flat_ref, piece_ref, sems
+    owners_hbm, cols_hbm, offs_hbm, feat_ref, out_ref, owners_ref, cols_ref, offs_ref, here_ref, ids_ref, tmp_ref,
+    flat_ref, piece_ref, narrow_ref, table_sems, sems, out_sems,
 ):
     frames, rows, wide, _ = feat_ref.shape
     tile = lax.axis_index("tiles")
+    tables = [
+        pltpu.make_async_copy(source, target, table_sems.at[n])
+        for n, (source, target) in enumerate(
+            ((owners_hbm, owners_ref), (cols_hbm, cols_ref), (offs_hbm, offs_ref))
+        )
+    ]
+    for copy in tables:
+        copy.start()
     copies = [pltpu.make_async_copy(feat_ref.at[k], here_ref.at[k], sems.at[k]) for k in range(frames)]
     for copy in copies:
         copy.start()
+
+    tmp_ref[...] = jnp.zeros_like(tmp_ref)
+    flat_ref[...] = jnp.zeros_like(flat_ref)
+    for copy in tables:
+        copy.wait()
 
     def scan(b, counts):
         near = owners_ref[b] - tile + 1
@@ -60,8 +74,10 @@
 
     zero = jnp.int32(0)
     counts = lax.fori_loop(0, owners_ref.shape[0], scan, (zero, zero, zero), unroll=8)
-    tmp_ref[...] = jnp.zeros_like(tmp_ref)
-    flat_ref[...] = jnp.zeros_like(flat_ref)
+
+    def leave(i):
+        return pltpu.make_async_copy(narrow_ref.at[i], out_ref.at[i], out_sems.at[i])
+
     for k in range(frames):
         copies[k].wait()
 
@@ -88,48 +104,65 @@
         part(2, rows - EDGE, EDGE, LOW, SIDE)
         part(0, 0, EDGE, HIGH, SIDE)
 
-    def narrow(i, carry):
-        out_ref[i] = piece_ref[pl.ds(pl.multiple_of(i * SENT, 16), SENT), :].astype(BF16)
+        def narrow(i, carry):
+            narrow_ref[i] = piece_ref[pl.ds(pl.multiple_of(i * SENT, 16), SENT), :].astype(BF16)
+            leave(i).start()
+            return carry
+
+        lax.fori_loop(k * CLASSES, (k + 1) * CLASSES, narrow, 0)
+
+    def wait(i, carry):
+        leave(i).wait()
         return carry
 
-    lax.fori_loop(0, PIECES, narrow, 0)
-
-
-def route_kernel(height, owner_ref, rank_ref, offs_ref, in_ref, out_ref, wide_ref, join_ref):
-    tiles = in_ref.shape[0]
-    rows = height // tiles
-    piece = lax.axis_index("tiles")
-    frame, which = piece >> 3, piece & 7
+    lax.fori_loop(0, PIECES, wait, 0)
+
+
+def routes(owner, rank, offs, piece, tiles, rows):
+    which = piece % CLASSES
+    row = lax.dynamic_index_in_dim(offs, piece // CLASSES, 0, keepdims=False)
+    none = tiles * SENT
+    before = jnp.where(owner > 0, (owner - 1) * SENT + LOW + rank * SIDE, none)
+    after = jnp.where(owner < tiles - 1, (owner + 1) * SENT + HIGH + rank * SIDE, none)
+    own = first_of(RAW * jnp.maximum(EDGE - row, 0), which)
+    over = first_of(RAW * (EDGE + rows - row), which)
+    return jnp.stack([before, owner * SENT + rank * OWN, after, own, over, owner * rows + row - WIN // 2])
+
+
+def route_kernel(parts, index_ref, in_ref, *refs):
+    out_ref, wide_ref, join_ref, narrow_ref, sems = refs[-5:]
+    tiles, blocks = in_ref.shape[0], out_ref.shape[0]
+    which = lax.axis_index("tiles") & (CLASSES - 1)
+    wide_ref[tiles * SENT :, :] = jnp.zeros_like(wide_ref[tiles * SENT :, :])
 
     def widen(i, carry):
         wide_ref[pl.ds(pl.multiple_of(i * SENT, 16), SENT), :] = in_ref[i].astype(F32)
         return carry
 
     lax.fori_loop(0, tiles, widen, 0)
-    none = tiles * SENT
-    wide_ref[none:, :] = jnp.zeros_like(wide_ref[none:, :])
     last = jnp.where(which > 0, PROWS - 1, 24)
 
     def gather(b, carry):
-        owner, slot, row = owner_ref[b], rank_ref[b], offs_ref[frame, b]
-        before = jnp.where(owner > 0, (owner - 1) * SENT + LOW + slot * SIDE, none)
-        after = jnp.where(owner < tiles - 1, (owner + 1) * SENT + HIGH + slot * SIDE, none)
-        own = first_of(RAW * jnp.maximum(EDGE - row, 0), which)
-        over = first_of(RAW * (EDGE + rows - row), which)
-        join_ref[b, 0:8, :] = wide_ref[pl.ds(before, 8), :]
-        join_ref[b, pl.ds(own, 16), :] = wide_ref[pl.ds(owner * SENT + slot * OWN, 16), :]
-        join_ref[b, pl.ds(over, 8), :] = wide_ref[pl.ds(after, 8), :]
-        top = (owner * rows + row - WIN // 2).astype(F32)
-        join_ref[b, pl.ds(last, 1), :] = jnp.full((1, 128), top, F32)
+        join_ref[b, 0:8, :] = wide_ref[pl.ds(index_ref[0, b], 8), :]
+        join_ref[b, pl.ds(index_ref[3, b], 16), :] = wide_ref[pl.ds(index_ref[1, b], 16), :]
+        join_ref[b, pl.ds(index_ref[4, b], 8), :] = wide_ref[pl.ds(index_ref[2, b], 8), :]
+        join_ref[b, pl.ds(last, 1), :] = jnp.full((1, 128), index_ref[5, b].astype(F32), F32)
         return carry
 
-    lax.fori_loop(0, out_ref.shape[0], gather, 0, unroll=4)
-
     def narrow(b, carry):
-        out_ref[b] = join_ref[b, 0:PROWS, :].astype(BF16)
+        narrow_ref[b] = join_ref[b, 0:PROWS, :].astype(BF16)
         return carry
 
-    lax.fori_loop(0, out_ref.shape[0], narrow, 0, unroll=8)
+    each = blocks // parts
+    copies = []
+    for part in range(parts):
+        here = pl.ds(part * each, each)
+        lax.fori_loop(part * each, (part + 1) * each, gather, 0, unroll=8)
+        lax.fori_loop(part * each, (part + 1) * each, narrow, 0, unroll=8)
+        copies.append(pltpu.make_async_copy(narrow_ref.at[here], out_ref.at[here], sems.at[part]))
+        copies[-1].start()
+    for copy in copies:
+        copy.wait()
 
 
 def nt(a, b):
@@ -304,38 +337,30 @@
     rank = jnp.sum(
         (owner[:, None] == owner[None, :]) & (number[None, :] < number[:, None]), axis=1, dtype=jnp.int32
     )
+    hbm = lambda array: pltpu.with_memory_space_constraint(array, pltpu.HBM)
     pieces = pl.pallas_call(
         send_kernel,
-        out_shape=jax.ShapeDtypeStruct((PIECES, SENT, chans), BF16),
-        in_specs=[SMEM, SMEM, SMEM, HBM],
-        out_specs=VMEM,
+        out_shape=pltpu.HBM((PIECES, SENT, chans), BF16),
+        in_specs=[HBM] * 4,
+        out_specs=HBM,
         scratch_shapes=[
+            pltpu.SMEM((blocks,), jnp.int32),
+            pltpu.SMEM(offset_cols.shape, jnp.int32),
+            pltpu.SMEM(offset_rows.shape, jnp.int32),
             pltpu.VMEM(features.shape, BF16),
             pltpu.SMEM((64,), jnp.int32),
             pltpu.VMEM((TILE, 48, 128), F32),
             pltpu.VMEM((192, 128), F32),
             pltpu.VMEM((PIECES * SENT, 128), F32),
+            pltpu.VMEM((PIECES, SENT, chans), BF16),
+            pltpu.SemaphoreType.DMA((3,)),
             pltpu.SemaphoreType.DMA((frames,)),
+            pltpu.SemaphoreType.DMA((PIECES,)),
         ],
         compiler_params=params(32),
         name="windows",
-    )(owner, offset_cols, offset_rows, pltpu.with_memory_space_constraint(features, pltpu.HBM))
+    )(hbm(owner), hbm(offset_cols), hbm(offset_rows), hbm(features))
     spread = lax.all_to_all(pieces, "tiles", 0, 0, tiled=True)
-    routed = pl.pallas_call(
-        functools.partial(route_kernel, n_tiles * rows),
-        out_shape=jax.ShapeDtypeStruct((blocks, PROWS, chans), BF16),
-        in_specs=[SMEM, SMEM, SMEM, VMEM],
-        out_specs=VMEM,
-        scratch_shapes=[
-            pltpu.VMEM((n_tiles * SENT + 16, 128), F32),
-            pltpu.VMEM((blocks, 32, 128), F32),
-        ],
-        compiler_params=params(32),
-        name="route",
-    )(owner, rank, offset_rows, spread)
-    raw = lax.all_to_all(routed, ("frames", "tiles"), 0, 0, tiled=True)
-    raw = raw.reshape(blocks * PROWS, chans)
-
     wk = jnp.pad(w_qkv[:, dim : 2 * dim].reshape(dim, HEADS, HEAD), ((0, 0), (0, 0), (0, 16)))
     wk = wk.reshape(dim, HEADS * 64)
     wq, wv = w_qkv[:, :dim].T, w_qkv[:, 2 * dim :].T
@@ -343,9 +368,29 @@
     wcorr = jnp.pad(wcorr.reshape(WIN * RAW, dim), ((0, 128 - WIN * RAW), (0, 0)))
     tokens = tracks * total
     start = jnp.repeat(start_frames, total).reshape(tokens // CHUNK, 1, CHUNK)
+    gain1, gain2 = gain_attn.reshape(1, dim), gain_mlp.reshape(1, dim)
+    first = (wk, wq, wv, hbm(wcorr), start, gain1, gain2)
+    index = routes(owner, rank, offset_rows, lax.axis_index("tiles"), n_tiles, rows)
+    routed = pl.pallas_call(
+        functools.partial(route_kernel, 4),
+        out_shape=jax.ShapeDtypeStruct((blocks, PROWS, chans), BF16),
+        in_specs=[SMEM, VMEM] + [HBM] * len(first),
+        out_specs=HBM,
+        scratch_shapes=[
+            pltpu.VMEM((n_tiles * SENT + 16, 128), F32),
+            pltpu.VMEM((blocks, 32, 128), F32),
+            pltpu.VMEM((blocks, PROWS, chans), BF16),
+            pltpu.SemaphoreType.DMA((4,)),
+        ],
+        compiler_params=params(32),
+        name="route",
+    )(index, spread, *first)
+    raw = lax.all_to_all(routed, ("frames", "tiles"), 0, 0, tiled=True)
+    raw = raw.reshape(blocks * PROWS, chans)
+
     refined = refine_call(
         n_tiles * rows, raw, w_conv.reshape(9 * chans, chans), query_feats, wcorr, w_feat, time_embed,
-        start, gain_attn.reshape(1, dim), wk, wq, wv, w_attn_out, gain_mlp.reshape(1, dim), w_up, w_down,
+        start, gain1, wk, wq, wv, w_attn_out, gain2, w_up, w_down,
     )
     return refined.reshape(tracks, total, dim)
 

time: 92.7 us -> 90.5 us (0.976)
  blocking collectives: 0 us -> 19.4 us
  waiting for transfers between devices: 34.6 us -> 18.2 us
  starting transfers between devices: 16.5 us -> 12.2 us
  local copies, waits for them, and re-layouts: 14.7 us -> 12.7 us
  other arithmetic: 0.17 us -> 1.62 us
    all_to_all x0 -> x1, blocking collectives: none -> 19.4 us  [body(): raw = lax.all_to_all(routed, ('frames', 'tiles'), 0, 0, tiled=True)]
    all_to_all x1, waiting for transfers between devices: 32.3 us -> 18.2 us  [body(): spread = lax.all_to_all(pieces, 'tiles', 0, 0, tiled=True)]
    all_to_all x1 -> x0, starting transfers between devices: 5.93 us -> none  [body(): raw = lax.all_to_all(routed, ('frames', 'tiles'), 0, 0, tiled=True)]
    unnamed x33 -> x19, local copies, waits for them, and re-layouts: 5.82 us -> 3.29 us
    all_to_all x1 -> x0, waiting for transfers between devices: 2.31 us -> none  [body(): raw = lax.all_to_all(routed, ('frames', 'tiles'), 0, 0, tiled=True)]
    all_to_all x1, starting transfers between devices: 10.6 us -> 12.2 us  [body(): spread = lax.all_to_all(pieces, 'tiles', 0, 0, tiled=True)]
    reshape x2, local copies, waits for them, and re-layouts: 0.01 us -> 1.37 us  [body(): gain1, gain2 = (gain_attn.reshape(1, dim), gain_mlp.reshape(1, dim))]
  transfers between devices with their start and end apart: 2 -> 1, of which waited for: 2 -> 1; matrix products, arithmetic and copies ran while one was open for 12% -> 16% of each run, Pallas kernels for 0% -> 0%
where the time goes in v4:
time: 90.5 us; the launch traced here: 90.2 us
  Pallas kernels  25.7 us (28%)
  blocking collectives  19.4 us (21%)
  waiting for transfers between devices  18.2 us (20%)
  local copies, waits for them, and re-layouts  12.7 us (14%)
  starting transfers between devices  12.2 us (13%)
  other arithmetic  1.62 us (2%)
    all_to_all x1, blocking collectives, body(): raw = lax.all_to_all(routed, ('frames', 'tiles'), 0, 0, tiled=True)  19.4 us
    pallas_call x1, Pallas kernels, refine_call(): pl.pallas_call(functools.partial(refine_kernel, height), grid=(tokens //...  18.3 us
    all_to_all x1, waiting for transfers between devices, body(): spread = lax.all_to_all(pieces, 'tiles', 0, 0, tiled=True)  18.2 us
    all_to_all x1, starting transfers between devices, body(): spread = lax.all_to_all(pieces, 'tiles', 0, 0, tiled=True)  12.2 us
    pallas_call x1, Pallas kernels, body(): pl.pallas_call(send_kernel, out_shape=pltpu.HBM((PIECES, SENT, chans), BF...  4.23 us
    unnamed x19, local copies, waits for them, and re-layouts  3.29 us
    pallas_call x1, Pallas kernels, body(): pl.pallas_call(functools.partial(route_kernel, 4), out_shape=jax.ShapeDty...  3.21 us
    slice x1, local copies, waits for them, and re-layouts, body(): wq, wv = (w_qkv[:, :dim].T, w_qkv[:, 2 * dim:].T)  2.08 us
  transfers between devices with their start and end apart: 1, of which 1 were waited for; matrix products, arithmetic and copies ran while one was open for 16% of the time, Pallas kernels for 0%

profile of v4, /device:TPU:1, one launch (start us, length us, event | category | flops | bytes accessed | tf_op | source)
XLA Modules:
  0.0 90.2 jit_solution(6980761707479568008)
XLA Ops:
  0.0 4.2 %windows.1 = bf16[32,304,128]{2,1,0:T(8,128)(2,1)} custom-call(s32[128]{0:T(128)} %bitcast.39, s32[4,128]{1,0:T(4,128)} %cols_hbm.1, s32[4,128]{1,0:T(4,128)} %offs_hbm.1, bf16[4,8,480,128]{3,2,1,0:T(8,128)(2,1)} %feat_ref.1), custom_call_target="tpu_custom_call" | custom-call | tf_op jit(solution)/shard_map/windows/pallas_call | solution.py:341
  4.2 12.2 %all-to-all-start = ((bf16[32,304,128]{2,1,0:T(8,128)(2,1)}), bf16[32,304,128]{2,1,0:T(8,128)(2,1)S(1)}, u32[]{:S(2)}, u32[]{:S(2)}) async-start(bf16[32,304,128]{2,1,0:T(8,128)(2,1)} %windows.1), calls=%async_computation | async-start | bytes 4980736 | tf_op jit(solution)/shard_map/all_to_all | solution.py:363
  16.5 0.0 copy-start.7
  16.5 2.1 %fusion.2 = (bf16[384,384]{1,0:T(8,128)(2,1)}, bf16[384,384]{1,0:T(8,128)(2,1)}, bf16[384,384]{1,0:T(8,128)(2,1)S(1)}) fusion(bf16[384,1152]{1,0:T(8,128)(2,1)} %param.27), kind=kLoop, calls=%fused_computation.13 | loop fusion | bytes 1769472 | tf_op jit(solution)/shard_map/slice | solution.py:366
  18.6 0.9 %copy.33 = bf16[384,384]{0,1:T(8,128)(2,1)} copy(bf16[384,384]{1,0:T(8,128)(2,1)S(1)} %get-tuple-element.7) | data formatting | bytes 589824
  19.5 1.0 %pad.12 = bf16[384,8,64]{0,2,1:T(8,128)(2,1)S(1)} pad(bf16[384,8,48]{0,2,1:T(8,128)(2,1)} %bitcast.38, bf16[]{:T(256)} %constant.66.clone.1), padding=0_0x0_0x0_16 | pad | bytes 688130 | tf_op jit(solution)/shard_map/jit(_pad)/pad | solution.py:364
  20.5 0.2 copy.29.refs_0_.wk_ref
  20.7 1.2 %copy.34 = bf16[384,384]{0,1:T(8,128)(2,1)S(1)} copy(bf16[384,384]{1,0:T(8,128)(2,1)} %get-tuple-element.6) | data formatting | bytes 589824
  21.9 1.2 %copy.35 = bf16[384,384]{0,1:T(8,128)(2,1)S(1)} copy(bf16[384,384]{1,0:T(8,128)(2,1)} %get-tuple-element.5) | data formatting | bytes 589824
  23.0 0.0 copy-done.7
  23.0 0.7 reshape.164
  23.7 1.5 %pad.13 = bf16[9,11,384]{2,1,0:T(8,128)(2,1)} pad(bf16[9,9,384]{2,1,0:T(8,128)(2,1)} %reshape.164, bf16[]{:T(256)} %constant.66.clone.1), padding=0_0x0_2x0_0 | pad | bytes 138242 | tf_op jit(solution)/shard_map/jit(_pad)/pad | solution.py:367
  25.3 0.9 %reshape.165 = bf16[99,384]{1,0:T(8,128)(2,1)S(1)} reshape(bf16[9,11,384]{2,1,0:T(8,128)(2,1)} %pad.13) | data formatting | bytes 152064 | tf_op jit(solution)/shard_map/reshape | solution.py:368
  26.2 0.7 pad.14.refs_3_.wcorr_ref
  26.9 0.7 broadcast_in_dim.15
  27.6 0.1 broadcast_in_dim.16
  27.7 0.1 broadcast_in_dim.18.refs_4_.start_ref
  27.8 0.7 reshape.166.refs_5_.gain1_ref
  28.5 0.7 reshape.167.refs_6_.gain2_ref
  29.2 0.9 convert_reduce_fusion
  30.1 0.7 fusion.1
  30.8 18.2 %all-to-all-done.in_ref = bf16[32,304,128]{2,1,0:T(8,128)(2,1)S(1)} async-done(((bf16[32,304,128]{2,1,0:T(8,128)(2,1)}), bf16[32,304,128]{2,1,0:T(8,128)(2,1)S(1)}, u32[]{:S(2)}, u32[]{:S(2)}) %all-to-all-start) | async-done | bytes 2490400 | tf_op jit(solution)/shard_map/all_to_all | solution.py:363
  49.0 0.0 copy-start
  49.0 0.0 copy-start.1
  49.0 0.0 copy-start.2
  49.0 0.0 copy-start.3
  49.0 0.0 copy-start.4
  49.0 0.0 copy-start.5
  49.0 0.0 copy-start.6
  49.0 3.2 %route.1 = bf16[128,16,128]{2,1,0:T(8,128)(2,1)S(1)} custom-call(s32[6,128]{1,0:T(8,128)S(1)} %stack.2.index_ref, bf16[32,304,128]{2,1,0:T(8,128)(2,1)S(1)} %all-to-all-done.in_ref, bf16[384,512]{1,0:T(8,128)(2,1)S(1)} %copy.29.refs_0_.wk_ref, bf16[384,384]{1,0:T(8,128)(2,1)S(1)} %bitcast.31, bf16[384,384]{1,0:T(8,128)(2,1)S(1)} %bitcast.33, ...), custom_call_target="tpu_custom_call" | custom-call | tf_op jit(solution)/shard_map/route/pallas_call | solution.py:374
  52.2 19.4 %all_to_all.10 = bf16[128,16,128]{2,1,0:T(8,128)(2,1)S(1)} all-to-all(bf16[128,16,128]{2,1,0:T(8,128)(2,1)S(1)} %route.1), channel_id=1, replica_groups=mesh['frames'=4,'tiles'=32] {'frames','tiles'}, dimensions={0} | all-to-all | bytes 1048576 | tf_op jit(solution)/shard_map/all_to_all | solution.py:388
  71.7 0.0 copy-done
  71.7 0.0 copy-done.1
  71.7 0.0 copy-done.2
  71.7 0.0 copy-done.3
  71.7 0.0 copy-done.4
  71.7 0.0 copy-done.5
  71.7 0.0 copy-done.6
  71.7 18.3 %refine.1 = bf16[2048,384]{1,0:T(8,128)(2,1)} custom-call(bf16[2048,128]{1,0:T(8,128)(2,1)S(1)} %bitcast.35, bf16[1152,128]{1,0:T(8,128)(2,1)S(1)} %bitcast.36, bf16[128,128]{1,0:T(8,128)(2,1)S(1)} %copy-done.5, bf16[128,384]{1,0:T(8,128)(2,1)S(1)} %copy-done.1, bf16[128,384]{1,0:T(8,128)(2,1)S(1)} %copy-done.4, f32[16,384]{1,0:T(8,128)S(1)} %copy-done.6, ...), custom_call_target="tpu_custom_call" | custom-call | tf_op jit(solution)/shard_map/refine/pallas_call | solution.py:306
  (1 shorter events, 0.0 us)
Async XLA Ops:
  4.2 44.7 %all-to-all-start = ((bf16[32,304,128]{2,1,0:T(8,128)(2,1)}), bf16[32,304,128]{2,1,0:T(8,128)(2,1)S(1)}, u32[]{:S(2)}, u32[]{:S(2)}) async-start(bf16[32,304,128]{2,1,0:T(8,128)(2,1)} %windows.1), calls=%async_computation | async-start | bytes 4980736 | tf_op jit(solution)/shard_map/all_to_all | solution.py:363
  16.5 6.5 %copy-start.7 = (bf16[81,384]{1,0:T(8,128)(2,1)S(1)}, bf16[81,384]{1,0:T(8,128)(2,1)}, u32[]{:S(2)}) copy-start(bf16[81,384]{1,0:T(8,128)(2,1)} %param.23) | copy-start | bytes 186628
  49.0 22.7 %copy-start = (bf16[384,1536]{1,0:T(8,128)(2,1)S(1)}, bf16[384,1536]{1,0:T(8,128)(2,1)}, u32[]{:S(2)}) copy-start(bf16[384,1536]{1,0:T(8,128)(2,1)} %wup_ref.1) | copy-start | bytes 3538948
  49.0 22.7 %copy-start.1 = (bf16[128,384]{1,0:T(8,128)(2,1)S(1)}, bf16[128,384]{1,0:T(8,128)(2,1)}, u32[]{:S(2)}) copy-start(bf16[128,384]{1,0:T(8,128)(2,1)} %pad.14.refs_3_.wcorr_ref) | copy-start | bytes 294916
  49.0 22.7 %copy-start.2 = (bf16[3,3,128,128]{3,2,1,0:T(8,128)(2,1)S(1)}, bf16[3,3,128,128]{3,2,1,0:T(8,128)(2,1)}, u32[]{:S(2)}) copy-start(bf16[3,3,128,128]{3,2,1,0:T(8,128)(2,1)} %param.17) | copy-start | bytes 884740
  49.0 22.7 %copy-start.3 = (bf16[384,384]{1,0:T(8,128)(2,1)S(1)}, bf16[384,384]{1,0:T(8,128)(2,1)}, u32[]{:S(2)}) copy-start(bf16[384,384]{1,0:T(8,128)(2,1)} %wout_ref.1) | copy-start | bytes 884740
  49.0 22.7 %copy-start.4 = (bf16[128,384]{1,0:T(8,128)(2,1)S(1)}, bf16[128,384]{1,0:T(8,128)(2,1)}, u32[]{:S(2)}) copy-start(bf16[128,384]{1,0:T(8,128)(2,1)} %wfeat_ref.1) | copy-start | bytes 294916
  49.0 22.7 %copy-start.5 = (bf16[128,128]{1,0:T(8,128)(2,1)S(1)}, bf16[128,128]{1,0:T(8,128)(2,1)}, u32[]{:S(2)}) copy-start(bf16[128,128]{1,0:T(8,128)(2,1)} %query_ref.1) | copy-start | bytes 98308
  49.0 22.7 %copy-start.6 = (f32[16,384]{1,0:T(8,128)S(1)}, f32[16,384]{1,0:T(8,128)}, u32[]{:S(2)}) copy-start(f32[16,384]{1,0:T(8,128)} %time_ref.1) | copy-start | bytes 73732

commit v5 on v4

--- a/solution.py
+++ b/solution.py
@@ -24,6 +24,7 @@
 HIGH = LOW + CAP * SIDE
 SENT = 304
 CHUNK = 1024
+TOGETHER = 4
 BATCH = 4
 F32 = jnp.float32
 BF16 = jnp.bfloat16
@@ -31,12 +32,6 @@
 
 def aligned(col, wide):
     return pl.multiple_of(jnp.clip((col >> 4) << 4, 0, wide - 32), 16)
-
-
-def window_rows(source, rows, shift, tmp_ref, dst_ref, base):
-    tmp_ref[0:rows, 8:40, :] = source.astype(F32)
-    for i in range(rows):
-        dst_ref[base + RAW * i : base + RAW * i + 16, :] = tmp_ref[i, pl.ds(8 + shift, 16), :]
 
 
 def first_of(cell, which):
@@ -73,6 +68,8 @@
         return tuple(counts[d] + (near == d).astype(jnp.int32) for d in range(3))
 
     zero = jnp.int32(0)
+    for n in range(48):
+        ids_ref[n] = 0
     counts = lax.fori_loop(0, owners_ref.shape[0], scan, (zero, zero, zero), unroll=8)
 
     def leave(i):
@@ -82,23 +79,30 @@
         copies[k].wait()
 
         def part(d, row0, count, place, room, k=k):
-            def slot(s, carry):
-                block = ids_ref[16 * d + s]
-                row, col = offs_ref[k, block], cols_ref[k, block] - 1
-                start = aligned(col, wide)
-                window_rows(
-                    here_ref[k, row0 : row0 + count, pl.ds(start, 32), :], count, col - start, tmp_ref, flat_ref, 16
-                )
-                at = RAW * (EDGE - row + row0 + (rows, 0, -rows)[d])
-                low = jnp.maximum(at, 0)
-                for c in range(CLASSES):
-                    source = 16 + CLASSES * first_of(low, c) + c - at
-                    target = (k * CLASSES + c) * SENT + place + s * room
-                    length = 16 if d == 1 else 8
-                    piece_ref[pl.ds(target, length), :] = flat_ref[pl.ds(source, length, stride=CLASSES), :]
+            def slots(p, carry):
+                some = []
+                for n in range(TOGETHER):
+                    s = p * TOGETHER + n
+                    block = ids_ref[16 * d + s]
+                    col = cols_ref[k, block] - 1
+                    start = aligned(col, wide)
+                    tmp_ref[n, 0:count, 8:40, :] = here_ref[k, row0 : row0 + count, pl.ds(start, 32), :].astype(F32)
+                    some.append((s, col - start, offs_ref[k, block]))
+                for i in range(count):
+                    for n, (_, shift, _) in enumerate(some):
+                        at = 16 + RAW * i
+                        flat_ref[n, at : at + 16, :] = tmp_ref[n, i, pl.ds(8 + shift, 16), :]
+                for n, (s, _, row) in enumerate(some):
+                    at = RAW * (EDGE - row + row0 + (rows, 0, -rows)[d])
+                    low = jnp.maximum(at, 0)
+                    for c in range(CLASSES):
+                        source = 16 + CLASSES * first_of(low, c) + c - at
+                        target = (k * CLASSES + c) * SENT + place + s * room
+                        length = 16 if d == 1 else 8
+                        piece_ref[pl.ds(target, length), :] = flat_ref[n, pl.ds(source, length, stride=CLASSES), :]
                 return carry
 
-            lax.fori_loop(0, counts[d], slot, 0)
+            lax.fori_loop(0, (counts[d] + TOGETHER - 1) // TOGETHER, slots, 0)
 
         part(1, 0, rows, 0, OWN)
         part(2, rows - EDGE, EDGE, LOW, SIDE)
@@ -129,8 +133,10 @@
     return jnp.stack([before, owner * SENT + rank * OWN, after, own, over, owner * rows + row - WIN // 2])
 
 
-def route_kernel(parts, index_ref, in_ref, *refs):
-    out_ref, wide_ref, join_ref, narrow_ref, sems = refs[-5:]
+def route_kernel(index_hbm, in_ref, *refs):
+    out_ref, index_ref, wide_ref, join_ref, sem = refs[-5:]
+    table = pltpu.make_async_copy(index_hbm, index_ref, sem)
+    table.start()
     tiles, blocks = in_ref.shape[0], out_ref.shape[0]
     which = lax.axis_index("tiles") & (CLASSES - 1)
     wide_ref[tiles * SENT :, :] = jnp.zeros_like(wide_ref[tiles * SENT :, :])
@@ -140,6 +146,7 @@
         return carry
 
     lax.fori_loop(0, tiles, widen, 0)
+    table.wait()
     last = jnp.where(which > 0, PROWS - 1, 24)
 
     def gather(b, carry):
@@ -150,19 +157,11 @@
         return carry
 
     def narrow(b, carry):
-        narrow_ref[b] = join_ref[b, 0:PROWS, :].astype(BF16)
+        out_ref[b] = join_ref[b, 0:PROWS, :].astype(BF16)
         return carry
 
-    each = blocks // parts
-    copies = []
-    for part in range(parts):
-        here = pl.ds(part * each, each)
-        lax.fori_loop(part * each, (part + 1) * each, gather, 0, unroll=8)
-        lax.fori_loop(part * each, (part + 1) * each, narrow, 0, unroll=8)
-        copies.append(pltpu.make_async_copy(narrow_ref.at[here], out_ref.at[here], sems.at[part]))
-        copies[-1].start()
-    for copy in copies:
-        copy.wait()
+    lax.fori_loop(0, blocks, gather, 0, unroll=8)
+    lax.fori_loop(0, blocks, narrow, 0, unroll=8)
 
 
 def nt(a, b):
@@ -349,8 +348,8 @@
             pltpu.SMEM(offset_rows.shape, jnp.int32),
             pltpu.VMEM(features.shape, BF16),
             pltpu.SMEM((64,), jnp.int32),
-            pltpu.VMEM((TILE, 48, 128), F32),
-            pltpu.VMEM((192, 128), F32),
+            pltpu.VMEM((TOGETHER, TILE, 48, 128), F32),
+            pltpu.VMEM((TOGETHER, 192, 128), F32),
             pltpu.VMEM((PIECES * SENT, 128), F32),
             pltpu.VMEM((PIECES, SENT, chans), BF16),
             pltpu.SemaphoreType.DMA((3,)),
@@ -372,15 +371,15 @@
     first = (wk, wq, wv, hbm(wcorr), start, gain1, gain2)
     index = routes(owner, rank, offset_rows, lax.axis_index("tiles"), n_tiles, rows)
     routed = pl.pallas_call(
-        functools.partial(route_kernel, 4),
+        route_kernel,
         out_shape=jax.ShapeDtypeStruct((blocks, PROWS, chans), BF16),
-        in_specs=[SMEM, VMEM] + [HBM] * len(first),
-        out_specs=HBM,
+        in_specs=[HBM, VMEM] + [HBM] * len(first),
+        out_specs=VMEM,
         scratch_shapes=[
+            pltpu.SMEM(index.shape, jnp.int32),
             pltpu.VMEM((n_tiles * SENT + 16, 128), F32),
             pltpu.VMEM((blocks, 32, 128), F32),
-            pltpu.VMEM((blocks, PROWS, chans), BF16),
-            pltpu.SemaphoreType.DMA((4,)),
+            pltpu.SemaphoreType.DMA,
         ],
         compiler_params=params(32),
         name="route",

time: 90.5 us -> 87.9 us (0.971)
  starting transfers between devices: 12.2 us -> 9.26 us
    all_to_all x1, starting transfers between devices: 12.2 us -> 9.26 us  [body(): spread = lax.all_to_all(pieces, 'tiles', 0, 0, tiled=True)]
    pallas_call x1, Pallas kernels: 4.23 us -> 5.76 us  [body(): pl.pallas_call(send_kernel, out_shape=pltpu.HBM((PIECES, SENT, chans), BF...]
    pallas_call x1, Pallas kernels: 3.21 us -> 1.95 us  [body(): pl.pallas_call(route_kernel, out_shape=jax.ShapeDtypeStruct((blocks, PROW...]
where the time goes in v5:
time: 87.9 us; the launch traced here: 87.5 us
  Pallas kernels  26 us (30%)
  blocking collectives  19.4 us (22%)
  waiting for transfers between devices  18.2 us (21%)
  local copies, waits for them, and re-layouts  12.7 us (14%)
  starting transfers between devices  9.26 us (11%)
  other arithmetic  1.62 us (2%)
    all_to_all x1, blocking collectives, body(): raw = lax.all_to_all(routed, ('frames', 'tiles'), 0, 0, tiled=True)  19.4 us
    pallas_call x1, Pallas kernels, refine_call(): pl.pallas_call(functools.partial(refine_kernel, height), grid=(tokens //...  18.3 us
    all_to_all x1, waiting for transfers between devices, body(): spread = lax.all_to_all(pieces, 'tiles', 0, 0, tiled=True)  18.2 us
    all_to_all x1, starting transfers between devices, body(): spread = lax.all_to_all(pieces, 'tiles', 0, 0, tiled=True)  9.26 us
    pallas_call x1, Pallas kernels, body(): pl.pallas_call(send_kernel, out_shape=pltpu.HBM((PIECES, SENT, chans), BF...  5.76 us
    unnamed x19, local copies, waits for them, and re-layouts  3.29 us
    slice x1, local copies, waits for them, and re-layouts, body(): wq, wv = (w_qkv[:, :dim].T, w_qkv[:, 2 * dim:].T)  2.08 us
    pallas_call x1, Pallas kernels, body(): pl.pallas_call(route_kernel, out_shape=jax.ShapeDtypeStruct((blocks, PROW...  1.95 us
  transfers between devices with their start and end apart: 1, of which 1 were waited for; matrix products, arithmetic and copies ran while one was open for 16% of the time, Pallas kernels for 0%

profile of v5, /device:TPU:1, one launch (start us, length us, event | category | flops | bytes accessed | tf_op | source)
XLA Modules:
  0.0 87.5 jit_solution(14713298077247499862)
XLA Ops:
  0.0 5.8 %windows.1 = bf16[32,304,128]{2,1,0:T(8,128)(2,1)} custom-call(s32[128]{0:T(128)} %bitcast.39, s32[4,128]{1,0:T(4,128)} %cols_hbm.1, s32[4,128]{1,0:T(4,128)} %offs_hbm.1, bf16[4,8,480,128]{3,2,1,0:T(8,128)(2,1)} %feat_ref.1), custom_call_target="tpu_custom_call" | custom-call | tf_op jit(solution)/shard_map/windows/pallas_call | solution.py:340
  5.8 9.3 %all-to-all-start = ((bf16[32,304,128]{2,1,0:T(8,128)(2,1)}), bf16[32,304,128]{2,1,0:T(8,128)(2,1)S(1)}, u32[]{:S(2)}, u32[]{:S(2)}) async-start(bf16[32,304,128]{2,1,0:T(8,128)(2,1)} %windows.1), calls=%async_computation | async-start | bytes 4980736 | tf_op jit(solution)/shard_map/all_to_all | solution.py:362
  15.1 0.0 copy-start.7
  15.1 2.1 %fusion.2 = (bf16[384,384]{1,0:T(8,128)(2,1)}, bf16[384,384]{1,0:T(8,128)(2,1)}, bf16[384,384]{1,0:T(8,128)(2,1)S(1)}) fusion(bf16[384,1152]{1,0:T(8,128)(2,1)} %param.27), kind=kLoop, calls=%fused_computation.13 | loop fusion | bytes 1769472 | tf_op jit(solution)/shard_map/slice | solution.py:365
  17.1 0.9 %copy.33 = bf16[384,384]{0,1:T(8,128)(2,1)} copy(bf16[384,384]{1,0:T(8,128)(2,1)S(1)} %get-tuple-element.7) | data formatting | bytes 589824
  18.1 1.0 %pad.12 = bf16[384,8,64]{0,2,1:T(8,128)(2,1)S(1)} pad(bf16[384,8,48]{0,2,1:T(8,128)(2,1)} %bitcast.38, bf16[]{:T(256)} %constant.66.clone.1), padding=0_0x0_0x0_16 | pad | bytes 688130 | tf_op jit(solution)/shard_map/jit(_pad)/pad | solution.py:363
  19.1 0.2 copy.29.refs_0_.wk_ref
  19.3 1.2 %copy.34 = bf16[384,384]{0,1:T(8,128)(2,1)S(1)} copy(bf16[384,384]{1,0:T(8,128)(2,1)} %get-tuple-element.6) | data formatting | bytes 589824
  20.4 1.2 %copy.35 = bf16[384,384]{0,1:T(8,128)(2,1)S(1)} copy(bf16[384,384]{1,0:T(8,128)(2,1)} %get-tuple-element.5) | data formatting | bytes 589824
  21.6 0.0 copy-done.7
  21.6 0.7 reshape.164
  22.3 1.5 %pad.13 = bf16[9,11,384]{2,1,0:T(8,128)(2,1)} pad(bf16[9,9,384]{2,1,0:T(8,128)(2,1)} %reshape.164, bf16[]{:T(256)} %constant.66.clone.1), padding=0_0x0_2x0_0 | pad | bytes 138242 | tf_op jit(solution)/shard_map/jit(_pad)/pad | solution.py:366
  23.8 0.9 %reshape.165 = bf16[99,384]{1,0:T(8,128)(2,1)S(1)} reshape(bf16[9,11,384]{2,1,0:T(8,128)(2,1)} %pad.13) | data formatting | bytes 152064 | tf_op jit(solution)/shard_map/reshape | solution.py:367
  24.8 0.7 pad.14.refs_3_.wcorr_ref
  25.4 0.7 broadcast_in_dim.15
  26.2 0.1 broadcast_in_dim.16
  26.2 0.1 broadcast_in_dim.18.refs_4_.start_ref
  26.4 0.7 reshape.166.refs_5_.gain1_ref
  27.0 0.7 reshape.167.refs_6_.gain2_ref
  27.7 0.9 %convert_reduce_fusion = s32[128]{0:T(128)S(1)} fusion(s32[128]{0:T(128)} %bitcast.40), kind=kLoop, calls=%fused_computation | loop fusion | flops 81792 | bytes 1024 | tf_op jit(solution)/shard_map/reduce_sum | solution.py:336
  28.6 0.7 fusion.1
  29.4 18.2 %all-to-all-done.in_ref = bf16[32,304,128]{2,1,0:T(8,128)(2,1)S(1)} async-done(((bf16[32,304,128]{2,1,0:T(8,128)(2,1)}), bf16[32,304,128]{2,1,0:T(8,128)(2,1)S(1)}, u32[]{:S(2)}, u32[]{:S(2)}) %all-to-all-start) | async-done | bytes 2490400 | tf_op jit(solution)/shard_map/all_to_all | solution.py:362
  47.6 0.0 copy-start
  47.6 0.0 copy-start.1
  47.6 0.0 copy-start.2
  47.6 0.0 copy-start.3
  47.6 0.0 copy-start.4
  47.6 0.0 copy-start.5
  47.6 0.0 copy-start.6
  47.6 1.9 %route.1 = bf16[128,16,128]{2,1,0:T(8,128)(2,1)S(1)} custom-call(s32[6,128]{1,0:T(8,128)S(1)} %stack.2.index_hbm, bf16[32,304,128]{2,1,0:T(8,128)(2,1)S(1)} %all-to-all-done.in_ref, bf16[384,512]{1,0:T(8,128)(2,1)S(1)} %copy.29.refs_0_.wk_ref, bf16[384,384]{1,0:T(8,128)(2,1)S(1)} %bitcast.31, bf16[384,384]{1,0:T(8,128)(2,1)S(1)} %bitcast.33, ...), custom_call_target="tpu_custom_call" | custom-call | tf_op jit(solution)/shard_map/route/pallas_call | solution.py:373
  49.6 19.4 %all_to_all.10 = bf16[128,16,128]{2,1,0:T(8,128)(2,1)S(1)} all-to-all(bf16[128,16,128]{2,1,0:T(8,128)(2,1)S(1)} %route.1), channel_id=1, replica_groups=mesh['frames'=4,'tiles'=32] {'frames','tiles'}, dimensions={0} | all-to-all | bytes 1048576 | tf_op jit(solution)/shard_map/all_to_all | solution.py:387
  69.0 0.0 copy-done
  69.0 0.0 copy-done.1
  69.0 0.0 copy-done.2
  69.0 0.0 copy-done.3
  69.0 0.0 copy-done.4
  69.0 0.0 copy-done.5
  69.0 0.0 copy-done.6
  69.0 18.3 %refine.1 = bf16[2048,384]{1,0:T(8,128)(2,1)} custom-call(bf16[2048,128]{1,0:T(8,128)(2,1)S(1)} %bitcast.35, bf16[1152,128]{1,0:T(8,128)(2,1)S(1)} %bitcast.36, bf16[128,128]{1,0:T(8,128)(2,1)S(1)} %copy-done.5, bf16[128,384]{1,0:T(8,128)(2,1)S(1)} %copy-done.1, bf16[128,384]{1,0:T(8,128)(2,1)S(1)} %copy-done.4, f32[16,384]{1,0:T(8,128)S(1)} %copy-done.6, ...), custom_call_target="tpu_custom_call" | custom-call | tf_op jit(solution)/shard_map/refine/pallas_call | solution.py:305
  (1 shorter events, 0.0 us)
Async XLA Ops:
  5.8 41.8 %all-to-all-start = ((bf16[32,304,128]{2,1,0:T(8,128)(2,1)}), bf16[32,304,128]{2,1,0:T(8,128)(2,1)S(1)}, u32[]{:S(2)}, u32[]{:S(2)}) async-start(bf16[32,304,128]{2,1,0:T(8,128)(2,1)} %windows.1), calls=%async_computation | async-start | bytes 4980736 | tf_op jit(solution)/shard_map/all_to_all | solution.py:362
  15.1 6.5 %copy-start.7 = (bf16[81,384]{1,0:T(8,128)(2,1)S(1)}, bf16[81,384]{1,0:T(8,128)(2,1)}, u32[]{:S(2)}) copy-start(bf16[81,384]{1,0:T(8,128)(2,1)} %param.23) | copy-start | bytes 186628
  47.6 21.4 %copy-start = (bf16[384,1536]{1,0:T(8,128)(2,1)S(1)}, bf16[384,1536]{1,0:T(8,128)(2,1)}, u32[]{:S(2)}) copy-start(bf16[384,1536]{1,0:T(8,128)(2,1)} %wup_ref.1) | copy-start | bytes 3538948
  47.6 21.4 %copy-start.1 = (bf16[128,384]{1,0:T(8,128)(2,1)S(1)}, bf16[128,384]{1,0:T(8,128)(2,1)}, u32[]{:S(2)}) copy-start(bf16[128,384]{1,0:T(8,128)(2,1)} %pad.14.refs_3_.wcorr_ref) | copy-start | bytes 294916
  47.6 21.4 %copy-start.2 = (bf16[3,3,128,128]{3,2,1,0:T(8,128)(2,1)S(1)}, bf16[3,3,128,128]{3,2,1,0:T(8,128)(2,1)}, u32[]{:S(2)}) copy-start(bf16[3,3,128,128]{3,2,1,0:T(8,128)(2,1)} %param.17) | copy-start | bytes 884740
  47.6 21.4 %copy-start.3 = (bf16[384,384]{1,0:T(8,128)(2,1)S(1)}, bf16[384,384]{1,0:T(8,128)(2,1)}, u32[]{:S(2)}) copy-start(bf16[384,384]{1,0:T(8,128)(2,1)} %wout_ref.1) | copy-start | bytes 884740
  47.6 21.4 %copy-start.4 = (bf16[128,384]{1,0:T(8,128)(2,1)S(1)}, bf16[128,384]{1,0:T(8,128)(2,1)}, u32[]{:S(2)}) copy-start(bf16[128,384]{1,0:T(8,128)(2,1)} %wfeat_ref.1) | copy-start | bytes 294916
  47.6 21.4 %copy-start.5 = (bf16[128,128]{1,0:T(8,128)(2,1)S(1)}, bf16[128,128]{1,0:T(8,128)(2,1)}, u32[]{:S(2)}) copy-start(bf16[128,128]{1,0:T(8,128)(2,1)} %query_ref.1) | copy-start | bytes 98308
  47.6 21.4 %copy-start.6 = (f32[16,384]{1,0:T(8,128)S(1)}, f32[16,384]{1,0:T(8,128)}, u32[]{:S(2)}) copy-start(f32[16,384]{1,0:T(8,128)} %time_ref.1) | copy-start | bytes 73732

commit v6 on v5

--- a/solution.py
+++ b/solution.py
@@ -113,7 +113,7 @@
             leave(i).start()
             return carry
 
-        lax.fori_loop(k * CLASSES, (k + 1) * CLASSES, narrow, 0)
+        lax.fori_loop(k * CLASSES, (k + 1) * CLASSES, narrow, 0, unroll=4)
 
     def wait(i, carry):
         leave(i).wait()
@@ -174,7 +174,7 @@
 
 def refine_kernel(
     height, raw_ref, wconv_ref, query_ref, wcorr_ref, wfeat_ref, time_ref, start_ref, gain1_ref,
-    wk_ref, wq_ref, wv_ref, wout_ref, gain2_ref, wup_ref, wdown_ref, out_ref,
+    wk_ref, wqv_ref, wout_ref, gain2_ref, wup_ref, wdown_ref, out_ref,
     cells_ref, cols_ref, tok_ref, down_ref, sem,
 ):
     frames = raw_ref.shape[0] // 128
@@ -189,15 +189,15 @@
                 at = (f * CLASSES + c) * PROWS
                 cells_ref[pl.ds(f * 128 + c, PROWS, stride=CLASSES), :] = raw_ref[at : at + PROWS, :].astype(F32)
         cells_ref[frames * 128 :, :] = jnp.zeros_like(cells_ref[frames * 128 :, :])
-        line = lax.broadcasted_iota(jnp.int32, (128, 128), 0) // RAW
+        line = lax.broadcasted_iota(jnp.int32, (112, 128), 0) // RAW
         line = line.astype(F32)
         feat = jnp.dot(query_ref[...], wfeat_ref[...], preferred_element_type=F32)
         for f in range(frames):
             for a in range(3):
                 for b in range(3):
                     at = f * 128 + a * RAW + b
-                    cols_ref[f * 128 : (f + 1) * 128, (a * 3 + b) * 128 : (a * 3 + b + 1) * 128] = (
-                        cells_ref[at : at + 128, :].astype(BF16)
+                    cols_ref[f * 112 : (f + 1) * 112, (a * 3 + b) * 128 : (a * 3 + b + 1) * 128] = (
+                        cells_ref[at : at + 112, :].astype(BF16)
                     )
         conv = jnp.dot(cols_ref[...], wconv_ref[...], preferred_element_type=F32)
         corr = []
@@ -205,7 +205,7 @@
             info = f * 128 + 127
             row = line + cells_ref[info : info + 1, :]
             inside = (row >= 0) & (row < height)
-            here = jnp.where(inside, conv[f * 128 : (f + 1) * 128], 0.0).astype(BF16)
+            here = jnp.where(inside, conv[f * 112 : (f + 1) * 112], 0.0).astype(BF16)
             corr.append((nt(query_ref[...], here) * (128 ** -0.5)).astype(BF16))
         tokens = jnp.dot(
             jnp.concatenate(corr, axis=0), wcorr_ref[...], preferred_element_type=F32
@@ -222,8 +222,8 @@
     tokens = jnp.concatenate([tok_ref[part, here, :] for part in range(3)], axis=1)
     normed = rms_scale(tokens, gain1_ref[...]).astype(BF16)
     keys = jnp.dot(normed, wk_ref[...], preferred_element_type=F32).astype(BF16)
-    query = nt(wq_ref[...], normed).astype(BF16)
-    values = nt(wv_ref[...], normed).astype(BF16)
+    both = nt(wqv_ref[...], normed).astype(BF16)
+    query, values = both[: HEADS * HEAD], both[HEADS * HEAD :]
     track = lax.broadcasted_iota(jnp.int32, (16, 128), 1) // frames
     frame = lax.broadcasted_iota(jnp.int32, (16, 128), 0)
     key_track = lax.broadcasted_iota(jnp.int32, (128, 128), 0) // frames
@@ -310,7 +310,7 @@
         out_specs=pl.BlockSpec((CHUNK, dim), lambda i: (i, 0)),
         scratch_shapes=[
             pltpu.VMEM((raw.shape[0] + 32, 128), F32),
-            pltpu.VMEM((tokens, 9 * chans), BF16),
+            pltpu.VMEM((tokens // 128 * 112, 9 * chans), BF16),
             pltpu.VMEM((3, tokens, 128), F32),
             pltpu.VMEM(rest[-1].shape, BF16),
             pltpu.SemaphoreType.DMA,
@@ -362,13 +362,13 @@
     spread = lax.all_to_all(pieces, "tiles", 0, 0, tiled=True)
     wk = jnp.pad(w_qkv[:, dim : 2 * dim].reshape(dim, HEADS, HEAD), ((0, 0), (0, 0), (0, 16)))
     wk = wk.reshape(dim, HEADS * 64)
-    wq, wv = w_qkv[:, :dim].T, w_qkv[:, 2 * dim :].T
+    wqv = jnp.concatenate([w_qkv[:, :dim], w_qkv[:, 2 * dim :]], axis=1).T
     wcorr = jnp.pad(w_corr.reshape(WIN, WIN, dim), ((0, 0), (0, RAW - WIN), (0, 0)))
-    wcorr = jnp.pad(wcorr.reshape(WIN * RAW, dim), ((0, 128 - WIN * RAW), (0, 0)))
+    wcorr = jnp.pad(wcorr.reshape(WIN * RAW, dim), ((0, 112 - WIN * RAW), (0, 0)))
     tokens = tracks * total
     start = jnp.repeat(start_frames, total).reshape(tokens // CHUNK, 1, CHUNK)
     gain1, gain2 = gain_attn.reshape(1, dim), gain_mlp.reshape(1, dim)
-    first = (wk, wq, wv, hbm(wcorr), start, gain1, gain2)
+    first = (wk, wqv, hbm(wcorr), start, gain1, gain2)
     index = routes(owner, rank, offset_rows, lax.axis_index("tiles"), n_tiles, rows)
     routed = pl.pallas_call(
         route_kernel,
@@ -389,7 +389,7 @@
 
     refined = refine_call(
         n_tiles * rows, raw, w_conv.reshape(9 * chans, chans), query_feats, wcorr, w_feat, time_embed,
-        start, gain1, wk, wq, wv, w_attn_out, gain2, w_up, w_down,
+        start, gain1, wk, wqv, w_attn_out, gain2, w_up, w_down,
     )
     return refined.reshape(tracks, total, dim)
 

time: 87.9 us -> 87.3 us (level)
  local copies, waits for them, and re-layouts: 12.7 us -> 9 us
  waiting for transfers between devices: 18.2 us -> 21.4 us
  Pallas kernels: 26 us -> 24.5 us
    all_to_all x1, waiting for transfers between devices: 18.2 us -> 21.4 us  [body(): spread = lax.all_to_all(pieces, 'tiles', 0, 0, tiled=True)]
    pad x1, local copies, waits for them, and re-layouts: 1.55 us -> 0.01 us  [body(): jnp.pad(w_corr.reshape(WIN, WIN, dim), ((0, 0), (0, RAW - WIN), (0, 0)))]
    unnamed x19 -> x27, local copies, waits for them, and re-layouts: 3.29 us -> 4.7 us
    reshape x2, local copies, waits for them, and re-layouts: 1.37 us -> 0.01 us  [body(): gain1, gain2 = (gain_attn.reshape(1, dim), gain_mlp.reshape(1, dim))]
    pallas_call x1, Pallas kernels: 5.76 us -> 4.55 us  [body(): pl.pallas_call(send_kernel, out_shape=pltpu.HBM((PIECES, SENT, chans), BF...]
    transpose x0 -> x1, other arithmetic: none -> 1.11 us  [body(): wqv = jnp.concatenate([w_qkv[:, :dim], w_qkv[:, 2 * dim:]], axis=1).T]
    reshape x1, local copies, waits for them, and re-layouts: 0.94 us -> 0.04 us  [body(): wcorr.reshape(WIN * RAW, dim)]
  transfers between devices with their start and end apart: 1 -> 1, of which waited for: 1 -> 1; matrix products, arithmetic and copies ran while one was open for 16% -> 13% of each run, Pallas kernels for 0% -> 0%
where the time goes in v6:
time: 87.3 us; the launch traced here: 86.7 us
  Pallas kernels  24.5 us (28%)
  waiting for transfers between devices  21.4 us (25%)
  blocking collectives  19.4 us (22%)
  starting transfers between devices  10 us (11%)
  local copies, waits for them, and re-layouts  9 us (10%)
  other arithmetic  1.98 us (2%)
    all_to_all x1, waiting for transfers between devices, body(): spread = lax.all_to_all(pieces, 'tiles', 0, 0, tiled=True)  21.4 us
    all_to_all x1, blocking collectives, body(): raw = lax.all_to_all(routed, ('frames', 'tiles'), 0, 0, tiled=True)  19.4 us
    pallas_call x1, Pallas kernels, refine_call(): pl.pallas_call(functools.partial(refine_kernel, height), grid=(tokens //...  18 us
    all_to_all x1, starting transfers between devices, body(): spread = lax.all_to_all(pieces, 'tiles', 0, 0, tiled=True)  10 us
    unnamed x27, local copies, waits for them, and re-layouts  4.7 us
    pallas_call x1, Pallas kernels, body(): pl.pallas_call(send_kernel, out_shape=pltpu.HBM((PIECES, SENT, chans), BF...  4.55 us
    slice x1, local copies, waits for them, and re-layouts, body(): wqv = jnp.concatenate([w_qkv[:, :dim], w_qkv[:, 2 * dim:]], axis=1).T  2.05 us
    pallas_call x1, Pallas kernels, body(): pl.pallas_call(route_kernel, out_shape=jax.ShapeDtypeStruct((blocks, PROW...  1.94 us
  transfers between devices with their start and end apart: 1, of which 1 were waited for; matrix products, arithmetic and copies ran while one was open for 13% of the time, Pallas kernels for 0%

profile of v6, /device:TPU:1, one launch (start us, length us, event | category | flops | bytes accessed | tf_op | source)
XLA Modules:
  0.0 86.7 jit_solution(13968830170846666111)
XLA Ops:
  0.0 4.5 %windows.1 = bf16[32,304,128]{2,1,0:T(8,128)(2,1)} custom-call(s32[128]{0:T(128)} %bitcast.35, s32[4,128]{1,0:T(4,128)} %cols_hbm.1, s32[4,128]{1,0:T(4,128)} %offs_hbm.1, bf16[4,8,480,128]{3,2,1,0:T(8,128)(2,1)} %feat_ref.1), custom_call_target="tpu_custom_call" | custom-call | tf_op jit(solution)/shard_map/windows/pallas_call | solution.py:340
  4.6 10.0 %all-to-all-start = ((bf16[32,304,128]{2,1,0:T(8,128)(2,1)}), bf16[32,304,128]{2,1,0:T(8,128)(2,1)S(1)}, u32[]{:S(2)}, u32[]{:S(2)}) async-start(bf16[32,304,128]{2,1,0:T(8,128)(2,1)} %windows.1), calls=%async_computation | async-start | bytes 4980736 | tf_op jit(solution)/shard_map/all_to_all | solution.py:362
  14.6 2.0 %fusion.2 = (bf16[384,384]{1,0:T(8,128)(2,1)}, bf16[384,384]{1,0:T(8,128)(2,1)S(1)}, bf16[384,384]{1,0:T(8,128)(2,1)}) fusion(bf16[384,1152]{1,0:T(8,128)(2,1)} %param.27), kind=kLoop, calls=%fused_computation.14 | loop fusion | bytes 1769472 | tf_op jit(solution)/shard_map/slice | solution.py:365
  16.7 0.9 %copy.33 = bf16[384,384]{0,1:T(8,128)(2,1)} copy(bf16[384,384]{1,0:T(8,128)(2,1)S(1)} %get-tuple-element.6) | data formatting | bytes 589824
  17.6 0.0 copy-start.7
  17.6 1.0 %pad.12 = bf16[384,8,64]{0,2,1:T(8,128)(2,1)S(1)} pad(bf16[384,8,48]{0,2,1:T(8,128)(2,1)} %bitcast.34, bf16[]{:T(256)} %constant.66.clone.1), padding=0_0x0_0x0_16 | pad | bytes 688130 | tf_op jit(solution)/shard_map/jit(_pad)/pad | solution.py:363
  18.6 0.0 copy-start.11
  18.6 0.2 copy.29.refs_0_.wk_ref
  18.8 0.0 copy-start.9
  18.8 0.0 copy-start.10
  18.8 0.0 copy-start.8
  18.8 1.9 %copy.35 = bf16[384,384]{0,1:T(8,128)(2,1)} copy(bf16[384,384]{1,0:T(8,128)(2,1)} %get-tuple-element.7) | data formatting | bytes 589824
  20.7 1.8 %copy.34 = bf16[384,384]{0,1:T(8,128)(2,1)} copy(bf16[384,384]{1,0:T(8,128)(2,1)} %get-tuple-element.5) | data formatting | bytes 589824
  22.6 0.0 copy-done.7
  22.7 0.7 pad.14.refs_2_.wcorr_ref
  23.3 0.0 copy-done.11
  23.3 0.1 broadcast_in_dim.15
  23.4 0.1 broadcast_in_dim.16
  23.5 0.1 broadcast_in_dim.18.refs_3_.start_ref
  23.6 0.0 copy-done.9
  23.6 0.0 copy-done.10
  23.7 0.0 copy-done.8
  23.7 0.2 convert_reduce_fusion
  23.8 0.7 fusion.1
  24.6 1.1 %maximum_bitcast_fusion.refs_1_.wqv_ref = bf16[768,384]{1,0:T(8,128)(2,1)S(1)} fusion(bf16[384,384]{0,1:T(8,128)(2,1)} %copy.35, bf16[384,384]{0,1:T(8,128)(2,1)} %copy.34), kind=kLoop, calls=%fused_computation | loop fusion | flops 1179648 | bytes 1179648 | tf_op jit(solution)/shard_map/transpose | solution.py:365
  25.7 0.0 copy-start.5
  25.7 0.0 copy-start.6
  25.7 21.4 %all-to-all-done.in_ref = bf16[32,304,128]{2,1,0:T(8,128)(2,1)S(1)} async-done(((bf16[32,304,128]{2,1,0:T(8,128)(2,1)}), bf16[32,304,128]{2,1,0:T(8,128)(2,1)S(1)}, u32[]{:S(2)}, u32[]{:S(2)}) %all-to-all-start) | async-done | bytes 2490400 | tf_op jit(solution)/shard_map/all_to_all | solution.py:362
  47.1 0.0 copy-start
  47.1 0.0 copy-start.1
  47.1 0.0 copy-start.4
  47.1 1.9 %route.1 = bf16[128,16,128]{2,1,0:T(8,128)(2,1)S(1)} custom-call(s32[6,128]{1,0:T(8,128)S(1)} %stack.2.index_hbm, bf16[32,304,128]{2,1,0:T(8,128)(2,1)S(1)} %all-to-all-done.in_ref, bf16[384,512]{1,0:T(8,128)(2,1)S(1)} %copy.29.refs_0_.wk_ref, bf16[768,384]{1,0:T(8,128)(2,1)S(1)} %maximum_bitcast_fusion.refs_1_.wqv_ref, ...), custom_call_target="tpu_custom_call" | custom-call | tf_op jit(solution)/shard_map/route/pallas_call | solution.py:373
  49.1 0.0 copy-start.2
  49.1 0.0 copy-start.3
  49.1 19.4 %all_to_all.10 = bf16[128,16,128]{2,1,0:T(8,128)(2,1)S(1)} all-to-all(bf16[128,16,128]{2,1,0:T(8,128)(2,1)S(1)} %route.1), channel_id=1, replica_groups=mesh['frames'=4,'tiles'=32] {'frames','tiles'}, dimensions={0} | all-to-all | bytes 1048576 | tf_op jit(solution)/shard_map/all_to_all | solution.py:387
  68.5 0.0 copy-done.5
  68.5 0.0 copy-done.6
  68.5 0.0 copy-done
  68.5 0.0 copy-done.1
  68.5 0.0 copy-done.4
  68.5 0.0 copy-done.2
  68.5 0.0 copy-done.3
  68.5 18.0 %refine.1 = bf16[2048,384]{1,0:T(8,128)(2,1)} custom-call(bf16[2048,128]{1,0:T(8,128)(2,1)S(1)} %bitcast.31, bf16[1152,128]{1,0:T(8,128)(2,1)S(1)} %bitcast.32, bf16[128,128]{1,0:T(8,128)(2,1)S(1)} %copy-done.5, bf16[112,384]{1,0:T(8,128)(2,1)S(1)} %copy-done.1, bf16[128,384]{1,0:T(8,128)(2,1)S(1)} %copy-done.4, f32[16,384]{1,0:T(8,128)S(1)} %copy-done.6, ...), custom_call_target="tpu_custom_call" | custom-call | tf_op jit(solution)/shard_map/refine/pallas_call | solution.py:305
  (6 shorter events, 0.1 us)
Async XLA Ops:
  4.6 42.5 %all-to-all-start = ((bf16[32,304,128]{2,1,0:T(8,128)(2,1)}), bf16[32,304,128]{2,1,0:T(8,128)(2,1)S(1)}, u32[]{:S(2)}, u32[]{:S(2)}) async-start(bf16[32,304,128]{2,1,0:T(8,128)(2,1)} %windows.1), calls=%async_computation | async-start | bytes 4980736 | tf_op jit(solution)/shard_map/all_to_all | solution.py:362
  17.6 5.0 %copy-start.7 = (bf16[81,384]{1,0:T(8,128)(2,1)S(1)}, bf16[81,384]{1,0:T(8,128)(2,1)}, u32[]{:S(2)}) copy-start(bf16[81,384]{1,0:T(8,128)(2,1)} %param.23) | copy-start | bytes 186628
  18.6 4.7 %copy-start.11 = (s32[128]{0:T(128)S(1)}, s32[128]{0:T(128)}, u32[]{:S(2)}) copy-start(s32[128]{0:T(128)} %param.22) | copy-start | bytes 1540
  18.8 4.8 %copy-start.9 = (f32[384]{0:T(512)S(1)}, f32[384]{0:T(512)}, u32[]{:S(2)}) copy-start(f32[384]{0:T(512)} %param.26) | copy-start | bytes 4612
  18.8 4.8 %copy-start.10 = (f32[384]{0:T(512)S(1)}, f32[384]{0:T(512)}, u32[]{:S(2)}) copy-start(f32[384]{0:T(512)} %param.29) | copy-start | bytes 4612
  18.8 4.8 %copy-start.8 = (s32[128,1]{0,1:T(1,128)S(1)}, s32[128,1]{0,1:T(1,128)}, u32[]{:S(2)}) copy-start(s32[128,1]{0,1:T(1,128)} %param.21) | copy-start | bytes 1540
  25.7 42.8 %copy-start.5 = (bf16[128,128]{1,0:T(8,128)(2,1)S(1)}, bf16[128,128]{1,0:T(8,128)(2,1)}, u32[]{:S(2)}) copy-start(bf16[128,128]{1,0:T(8,128)(2,1)} %query_ref.1) | copy-start | bytes 98308
  25.7 42.8 %copy-start.6 = (f32[16,384]{1,0:T(8,128)S(1)}, f32[16,384]{1,0:T(8,128)}, u32[]{:S(2)}) copy-start(f32[16,384]{1,0:T(8,128)} %time_ref.1) | copy-start | bytes 73732
  47.1 21.4 %copy-start = (bf16[384,1536]{1,0:T(8,128)(2,1)S(1)}, bf16[384,1536]{1,0:T(8,128)(2,1)}, u32[]{:S(2)}) copy-start(bf16[384,1536]{1,0:T(8,128)(2,1)} %wup_ref.1) | copy-start | bytes 3538948
  47.1 21.4 %copy-start.1 = (bf16[112,384]{1,0:T(8,128)(2,1)S(1)}, bf16[112,384]{1,0:T(8,128)(2,1)}, u32[]{:S(2)}) copy-start(bf16[112,384]{1,0:T(8,128)(2,1)} %pad.14.refs_2_.wcorr_ref) | copy-start | bytes 258052
  47.1 21.4 %copy-start.4 = (bf16[128,384]{1,0:T(8,128)(2,1)S(1)}, bf16[128,384]{1,0:T(8,128)(2,1)}, u32[]{:S(2)}) copy-start(bf16[128,384]{1,0:T(8,128)(2,1)} %wfeat_ref.1) | copy-start | bytes 294916
  49.1 19.5 %copy-start.2 = (bf16[3,3,128,128]{3,2,1,0:T(8,128)(2,1)S(1)}, bf16[3,3,128,128]{3,2,1,0:T(8,128)(2,1)}, u32[]{:S(2)}) copy-start(bf16[3,3,128,128]{3,2,1,0:T(8,128)(2,1)} %param.17) | copy-start | bytes 884740
  49.1 19.5 %copy-start.3 = (bf16[384,384]{1,0:T(8,128)(2,1)S(1)}, bf16[384,384]{1,0:T(8,128)(2,1)}, u32[]{:S(2)}) copy-start(bf16[384,384]{1,0:T(8,128)(2,1)} %wout_ref.1) | copy-start | bytes 884740

commit v7 on v6

--- a/solution.py
+++ b/solution.py
@@ -126,11 +126,12 @@
     which = piece % CLASSES
     row = lax.dynamic_index_in_dim(offs, piece // CLASSES, 0, keepdims=False)
     none = tiles * SENT
-    before = jnp.where(owner > 0, (owner - 1) * SENT + LOW + rank * SIDE, none)
-    after = jnp.where(owner < tiles - 1, (owner + 1) * SENT + HIGH + rank * SIDE, none)
+    turned = tiles - 1 - owner
+    before = jnp.where(owner > 0, (turned + 1) * SENT + LOW + rank * SIDE, none)
+    after = jnp.where(owner < tiles - 1, (turned - 1) * SENT + HIGH + rank * SIDE, none)
     own = first_of(RAW * jnp.maximum(EDGE - row, 0), which)
     over = first_of(RAW * (EDGE + rows - row), which)
-    return jnp.stack([before, owner * SENT + rank * OWN, after, own, over, owner * rows + row - WIN // 2])
+    return jnp.stack([before, turned * SENT + rank * OWN, after, own, over, owner * rows + row - WIN // 2])
 
 
 def route_kernel(index_hbm, in_ref, *refs):
@@ -138,7 +139,7 @@
     table = pltpu.make_async_copy(index_hbm, index_ref, sem)
     table.start()
     tiles, blocks = in_ref.shape[0], out_ref.shape[0]
-    which = lax.axis_index("tiles") & (CLASSES - 1)
+    which = (tiles - 1 - lax.axis_index("tiles")) & (CLASSES - 1)
     wide_ref[tiles * SENT :, :] = jnp.zeros_like(wide_ref[tiles * SENT :, :])
 
     def widen(i, carry):
@@ -186,7 +187,8 @@
         fetch.start()
         for f in range(frames):
             for c in range(CLASSES):
-                at = (f * CLASSES + c) * PROWS
+                group, k = divmod(f, PIECES // CLASSES)
+                at = (group * PIECES + PIECES - 1 - k * CLASSES - c) * PROWS
                 cells_ref[pl.ds(f * 128 + c, PROWS, stride=CLASSES), :] = raw_ref[at : at + PROWS, :].astype(F32)
         cells_ref[frames * 128 :, :] = jnp.zeros_like(cells_ref[frames * 128 :, :])
         line = lax.broadcasted_iota(jnp.int32, (112, 128), 0) // RAW
@@ -359,7 +361,9 @@
         compiler_params=params(32),
         name="windows",
     )(hbm(owner), hbm(offset_cols), hbm(offset_rows), hbm(features))
-    spread = lax.all_to_all(pieces, "tiles", 0, 0, tiled=True)
+    spread = lax.all_to_all(
+        pieces, "tiles", 0, 0, tiled=True, axis_index_groups=[list(range(n_tiles))[::-1]]
+    )
     wk = jnp.pad(w_qkv[:, dim : 2 * dim].reshape(dim, HEADS, HEAD), ((0, 0), (0, 0), (0, 16)))
     wk = wk.reshape(dim, HEADS * 64)
     wqv = jnp.concatenate([w_qkv[:, :dim], w_qkv[:, 2 * dim :]], axis=1).T
@@ -369,7 +373,7 @@
     start = jnp.repeat(start_frames, total).reshape(tokens // CHUNK, 1, CHUNK)
     gain1, gain2 = gain_attn.reshape(1, dim), gain_mlp.reshape(1, dim)
     first = (wk, wqv, hbm(wcorr), start, gain1, gain2)
-    index = routes(owner, rank, offset_rows, lax.axis_index("tiles"), n_tiles, rows)
+    index = routes(owner, rank, offset_rows, n_tiles - 1 - lax.axis_index("tiles"), n_tiles, rows)
     routed = pl.pallas_call(
         route_kernel,
         out_shape=jax.ShapeDtypeStruct((blocks, PROWS, chans), BF16),

time: 87.3 us -> 86.8 us (level)
  waiting for transfers between devices: 21.4 us -> 18.8 us
  Pallas kernels: 24.5 us -> 25.9 us
  blocking collectives: 19.4 us -> 20.5 us
    all_to_all x1, waiting for transfers between devices: 21.4 us -> 18.8 us  [body(): lax.all_to_all(pieces, 'tiles', 0, 0, tiled=True, axis_index_groups=[list...]
    pallas_call x1, Pallas kernels: 4.55 us -> 5.91 us  [body(): pl.pallas_call(send_kernel, out_shape=pltpu.HBM((PIECES, SENT, chans), BF...]
    all_to_all x1, blocking collectives: 19.4 us -> 20.5 us  [body(): raw = lax.all_to_all(routed, ('frames', 'tiles'), 0, 0, tiled=True)]
where the time goes in v7:
time: 86.8 us; the launch traced here: 86.6 us
  Pallas kernels  25.9 us (30%)
  blocking collectives  20.5 us (24%)
  waiting for transfers between devices  18.8 us (22%)
  starting transfers between devices  10 us (12%)
  local copies, waits for them, and re-layouts  9 us (10%)
  other arithmetic  1.98 us (2%)
    all_to_all x1, blocking collectives, body(): raw = lax.all_to_all(routed, ('frames', 'tiles'), 0, 0, tiled=True)  20.5 us
    all_to_all x1, waiting for transfers between devices, body(): lax.all_to_all(pieces, 'tiles', 0, 0, tiled=True, axis_index_groups=[list...  18.8 us
    pallas_call x1, Pallas kernels, refine_call(): pl.pallas_call(functools.partial(refine_kernel, height), grid=(tokens //...  18 us
    all_to_all x1, starting transfers between devices, body(): lax.all_to_all(pieces, 'tiles', 0, 0, tiled=True, axis_index_groups=[list...  10 us
    pallas_call x1, Pallas kernels, body(): pl.pallas_call(send_kernel, out_shape=pltpu.HBM((PIECES, SENT, chans), BF...  5.91 us
    unnamed x27, local copies, waits for them, and re-layouts  4.7 us
    slice x1, local copies, waits for them, and re-layouts, body(): wqv = jnp.concatenate([w_qkv[:, :dim], w_qkv[:, 2 * dim:]], axis=1).T  2.05 us
    pallas_call x1, Pallas kernels, body(): pl.pallas_call(route_kernel, out_shape=jax.ShapeDtypeStruct((blocks, PROW...  1.95 us
  transfers between devices with their start and end apart: 1, of which 1 were waited for; matrix products, arithmetic and copies ran while one was open for 13% of the time, Pallas kernels for 0%

profile of v7, /device:TPU:1, one launch (start us, length us, event | category | flops | bytes accessed | tf_op | source)
XLA Modules:
  0.0 86.6 jit_solution(17373116386223423336)
XLA Ops:
  0.0 5.9 %windows.1 = bf16[32,304,128]{2,1,0:T(8,128)(2,1)} custom-call(s32[128]{0:T(128)} %bitcast.35, s32[4,128]{1,0:T(4,128)} %cols_hbm.1, s32[4,128]{1,0:T(4,128)} %offs_hbm.1, bf16[4,8,480,128]{3,2,1,0:T(8,128)(2,1)} %feat_ref.1), custom_call_target="tpu_custom_call" | custom-call | tf_op jit(solution)/shard_map/windows/pallas_call | solution.py:342
  5.9 10.0 %all-to-all-start = ((bf16[32,304,128]{2,1,0:T(8,128)(2,1)}), bf16[32,304,128]{2,1,0:T(8,128)(2,1)S(1)}, u32[]{:S(2)}, u32[]{:S(2)}) async-start(bf16[32,304,128]{2,1,0:T(8,128)(2,1)} %windows.1), calls=%async_computation | async-start | bytes 4980736 | tf_op jit(solution)/shard_map/all_to_all | solution.py:364
  16.0 2.0 %fusion.2 = (bf16[384,384]{1,0:T(8,128)(2,1)}, bf16[384,384]{1,0:T(8,128)(2,1)S(1)}, bf16[384,384]{1,0:T(8,128)(2,1)}) fusion(bf16[384,1152]{1,0:T(8,128)(2,1)} %param.27), kind=kLoop, calls=%fused_computation.14 | loop fusion | bytes 1769472 | tf_op jit(solution)/shard_map/slice | solution.py:369
  18.0 0.9 %copy.33 = bf16[384,384]{0,1:T(8,128)(2,1)} copy(bf16[384,384]{1,0:T(8,128)(2,1)S(1)} %get-tuple-element.6) | data formatting | bytes 589824
  18.9 0.0 copy-start.7
  18.9 1.0 %pad.12 = bf16[384,8,64]{0,2,1:T(8,128)(2,1)S(1)} pad(bf16[384,8,48]{0,2,1:T(8,128)(2,1)} %bitcast.34, bf16[]{:T(256)} %constant.71.clone.1), padding=0_0x0_0x0_16 | pad | bytes 688130 | tf_op jit(solution)/shard_map/jit(_pad)/pad | solution.py:367
  19.9 0.0 copy-start.11
  20.0 0.2 copy.29.refs_0_.wk_ref
  20.2 0.0 copy-start.9
  20.2 0.0 copy-start.10
  20.2 0.0 copy-start.8
  20.2 1.9 %copy.35 = bf16[384,384]{0,1:T(8,128)(2,1)} copy(bf16[384,384]{1,0:T(8,128)(2,1)} %get-tuple-element.7) | data formatting | bytes 589824
  22.1 1.8 %copy.34 = bf16[384,384]{0,1:T(8,128)(2,1)} copy(bf16[384,384]{1,0:T(8,128)(2,1)} %get-tuple-element.5) | data formatting | bytes 589824
  23.9 0.0 copy-done.7
  24.0 0.7 pad.14.refs_2_.wcorr_ref
  24.7 0.0 copy-done.11
  24.7 0.1 broadcast_in_dim.15
  24.8 0.1 broadcast_in_dim.16
  24.8 0.1 broadcast_in_dim.18.refs_3_.start_ref
  24.9 0.0 copy-done.9
  25.0 0.0 copy-done.10
  25.0 0.0 copy-done.8
  25.0 0.2 convert_reduce_fusion
  25.2 0.7 fusion.1
  25.9 1.1 %maximum_bitcast_fusion.refs_1_.wqv_ref = bf16[768,384]{1,0:T(8,128)(2,1)S(1)} fusion(bf16[384,384]{0,1:T(8,128)(2,1)} %copy.35, bf16[384,384]{0,1:T(8,128)(2,1)} %copy.34), kind=kLoop, calls=%fused_computation | loop fusion | flops 1179648 | bytes 1179648 | tf_op jit(solution)/shard_map/transpose | solution.py:369
  27.0 0.0 copy-start.5
  27.0 0.0 copy-start.6
  27.1 18.8 %all-to-all-done.in_ref = bf16[32,304,128]{2,1,0:T(8,128)(2,1)S(1)} async-done(((bf16[32,304,128]{2,1,0:T(8,128)(2,1)}), bf16[32,304,128]{2,1,0:T(8,128)(2,1)S(1)}, u32[]{:S(2)}, u32[]{:S(2)}) %all-to-all-start) | async-done | bytes 2490400 | tf_op jit(solution)/shard_map/all_to_all | solution.py:364
  45.8 0.0 copy-start
  45.8 0.0 copy-start.1
  45.8 0.0 copy-start.4
  45.8 2.0 %route.1 = bf16[128,16,128]{2,1,0:T(8,128)(2,1)S(1)} custom-call(s32[6,128]{1,0:T(8,128)S(1)} %stack.2.index_hbm, bf16[32,304,128]{2,1,0:T(8,128)(2,1)S(1)} %all-to-all-done.in_ref, bf16[384,512]{1,0:T(8,128)(2,1)S(1)} %copy.29.refs_0_.wk_ref, bf16[768,384]{1,0:T(8,128)(2,1)S(1)} %maximum_bitcast_fusion.refs_1_.wqv_ref, ...), custom_call_target="tpu_custom_call" | custom-call | tf_op jit(solution)/shard_map/route/pallas_call | solution.py:377
  47.8 0.0 copy-start.2
  47.8 0.0 copy-start.3
  47.8 20.5 %all_to_all.10 = bf16[128,16,128]{2,1,0:T(8,128)(2,1)S(1)} all-to-all(bf16[128,16,128]{2,1,0:T(8,128)(2,1)S(1)} %route.1), channel_id=1, replica_groups=mesh['frames'=4,'tiles'=32] {'frames','tiles'}, dimensions={0} | all-to-all | bytes 1048576 | tf_op jit(solution)/shard_map/all_to_all | solution.py:391
  68.3 0.0 copy-done.5
  68.3 0.0 copy-done.6
  68.4 0.0 copy-done
  68.4 0.0 copy-done.1
  68.4 0.0 copy-done.4
  68.4 0.0 copy-done.2
  68.4 0.0 copy-done.3
  68.4 18.0 %refine.1 = bf16[2048,384]{1,0:T(8,128)(2,1)} custom-call(bf16[2048,128]{1,0:T(8,128)(2,1)S(1)} %bitcast.31, bf16[1152,128]{1,0:T(8,128)(2,1)S(1)} %bitcast.32, bf16[128,128]{1,0:T(8,128)(2,1)S(1)} %copy-done.5, bf16[112,384]{1,0:T(8,128)(2,1)S(1)} %copy-done.1, bf16[128,384]{1,0:T(8,128)(2,1)S(1)} %copy-done.4, f32[16,384]{1,0:T(8,128)S(1)} %copy-done.6, ...), custom_call_target="tpu_custom_call" | custom-call | tf_op jit(solution)/shard_map/refine/pallas_call | solution.py:307
  (6 shorter events, 0.1 us)
Async XLA Ops:
  5.9 39.9 %all-to-all-start = ((bf16[32,304,128]{2,1,0:T(8,128)(2,1)}), bf16[32,304,128]{2,1,0:T(8,128)(2,1)S(1)}, u32[]{:S(2)}, u32[]{:S(2)}) async-start(bf16[32,304,128]{2,1,0:T(8,128)(2,1)} %windows.1), calls=%async_computation | async-start | bytes 4980736 | tf_op jit(solution)/shard_map/all_to_all | solution.py:364
  18.9 5.0 %copy-start.7 = (bf16[81,384]{1,0:T(8,128)(2,1)S(1)}, bf16[81,384]{1,0:T(8,128)(2,1)}, u32[]{:S(2)}) copy-start(bf16[81,384]{1,0:T(8,128)(2,1)} %param.23) | copy-start | bytes 186628
  19.9 4.7 %copy-start.11 = (s32[128]{0:T(128)S(1)}, s32[128]{0:T(128)}, u32[]{:S(2)}) copy-start(s32[128]{0:T(128)} %param.22) | copy-start | bytes 1540
  20.2 4.8 %copy-start.9 = (f32[384]{0:T(512)S(1)}, f32[384]{0:T(512)}, u32[]{:S(2)}) copy-start(f32[384]{0:T(512)} %param.26) | copy-start | bytes 4612
  20.2 4.8 %copy-start.10 = (f32[384]{0:T(512)S(1)}, f32[384]{0:T(512)}, u32[]{:S(2)}) copy-start(f32[384]{0:T(512)} %param.29) | copy-start | bytes 4612
  20.2 4.8 %copy-start.8 = (s32[128,1]{0,1:T(1,128)S(1)}, s32[128,1]{0,1:T(1,128)}, u32[]{:S(2)}) copy-start(s32[128,1]{0,1:T(1,128)} %param.21) | copy-start | bytes 1540
  27.0 41.3 %copy-start.5 = (bf16[128,128]{1,0:T(8,128)(2,1)S(1)}, bf16[128,128]{1,0:T(8,128)(2,1)}, u32[]{:S(2)}) copy-start(bf16[128,128]{1,0:T(8,128)(2,1)} %query_ref.1) | copy-start | bytes 98308
  27.0 41.3 %copy-start.6 = (f32[16,384]{1,0:T(8,128)S(1)}, f32[16,384]{1,0:T(8,128)}, u32[]{:S(2)}) copy-start(f32[16,384]{1,0:T(8,128)} %time_ref.1) | copy-start | bytes 73732
  45.8 22.5 %copy-start = (bf16[384,1536]{1,0:T(8,128)(2,1)S(1)}, bf16[384,1536]{1,0:T(8,128)(2,1)}, u32[]{:S(2)}) copy-start(bf16[384,1536]{1,0:T(8,128)(2,1)} %wup_ref.1) | copy-start | bytes 3538948
  45.8 22.5 %copy-start.1 = (bf16[112,384]{1,0:T(8,128)(2,1)S(1)}, bf16[112,384]{1,0:T(8,128)(2,1)}, u32[]{:S(2)}) copy-start(bf16[112,384]{1,0:T(8,128)(2,1)} %pad.14.refs_2_.wcorr_ref) | copy-start | bytes 258052
  45.8 22.5 %copy-start.4 = (bf16[128,384]{1,0:T(8,128)(2,1)S(1)}, bf16[128,384]{1,0:T(8,128)(2,1)}, u32[]{:S(2)}) copy-start(bf16[128,384]{1,0:T(8,128)(2,1)} %wfeat_ref.1) | copy-start | bytes 294916
  47.8 20.6 %copy-start.2 = (bf16[3,3,128,128]{3,2,1,0:T(8,128)(2,1)S(1)}, bf16[3,3,128,128]{3,2,1,0:T(8,128)(2,1)}, u32[]{:S(2)}) copy-start(bf16[3,3,128,128]{3,2,1,0:T(8,128)(2,1)} %param.17) | copy-start | bytes 884740
  47.8 20.6 %copy-start.3 = (bf16[384,384]{1,0:T(8,128)(2,1)S(1)}, bf16[384,384]{1,0:T(8,128)(2,1)}, u32[]{:S(2)}) copy-start(bf16[384,384]{1,0:T(8,128)(2,1)} %wout_ref.1) | copy-start | bytes 884740
